TPU v7x, 256 devices: a whole 4x4x8 slice. The times are simulated.
256 devices in a mesh: clip: 4 (over y), blk: 16 (over z_lo, x, core), head: 4 (over z_hi).
Axes of the slice: x: 4, y: 4, z: 8 (z_hi: 4, z_lo: 2; z = z_hi * 2 + z_lo), core: 2. Of those that a mesh axis runs over, the one named last changes fastest.
Arguments:
- query_rows: bfloat16 [16384, 2560], P(('clip', 'blk', 'head')), parts along dimension 0, may hold values from -32 to 32
- key_rows: bfloat16 [16384, 2560], P(('clip', 'blk', 'head')), parts along dimension 0, may hold values from -12 to 12
- value_rows: bfloat16 [16384, 2560], P(('clip', 'blk', 'head')), parts along dimension 0, may hold values from -12 to 12
- query_tan: bfloat16 [16384, 2560], P(('clip', 'blk', 'head')), parts along dimension 0, may hold values from -6 to 6
- key_tan: bfloat16 [16384, 2560], P(('clip', 'blk', 'head')), parts along dimension 0, may hold values from -6 to 6
- value_tan: bfloat16 [16384, 2560], P(('clip', 'blk', 'head')), parts along dimension 0, may hold values from -6 to 6
Outputs:
- attended: bfloat16 [16384, 2560], P(('clip', 'blk', 'head')), parts along dimension 0
- attended_tan: bfloat16 [16384, 2560], P(('clip', 'blk', 'head')), parts along dimension 0
There are 4 independent parts, one for each index of `clip`. A program takes and returns all parts, laid end to end along the dimension named above; each array names one. Nothing has to cross between parts.
All inputs are finite; a program needn't handle non-finite values.
Results may differ from a plain program's by a relative error of at most 0.0066.
Values may be sent and summed in bfloat16 or wider, within the bound.
No kernel may reach another device: no remote copies, remote signals or barrier semaphores. Data moves between devices by JAX's collectives and lax.ppermute only.
A program may use at most 128 MiB of HBM per device.

v0:
```python
import jax
import jax.numpy as jnp
from jax import lax
from jax.sharding import PartitionSpec as P

HEAD_DIM = 128


LOW_START = -1e30


def split_heads(array):
    return array.reshape(array.shape[0], array.shape[1] // HEAD_DIM, HEAD_DIM)


def split_blocks(pieces):
    length = pieces[0].shape[0]
    block_count = -(-length // 2048)
    while length % block_count:
        block_count += 1
    blocks = tuple(
        (
            split_heads(piece).reshape(
                block_count, length // block_count, piece.shape[1] // HEAD_DIM, HEAD_DIM
            )
            for piece in pieces
        )
    )
    return (block_count, blocks)


def over_blocks(step, carried_state, pieces):
    block_count, blocks = split_blocks(pieces)

    def scan_step(state_now, key_block):
        return (step(state_now, key_block), None)

    result, unused = lax.scan(scan_step, carried_state, blocks)
    return result


def plain_scores(query_heads, key_heads):
    score_scale = HEAD_DIM ** (-0.5)
    return (
        jnp.einsum("qhd,khd->qhk", query_heads, key_heads, preferred_element_type=jnp.float32)
        * score_scale
    )


def tangent_scores(paired, key_heads, keytan_heads):
    score_scale = HEAD_DIM ** (-0.5)
    joined = jnp.concatenate([keytan_heads, key_heads], axis=-1)
    return (
        jnp.einsum("qhd,khd->qhk", paired, joined, preferred_element_type=jnp.float32) * score_scale
    )


def tangent_terms(weights, score_tan, value_heads, valuetan_heads):
    tilted = weights * score_tan
    weights_low = weights.astype(jnp.bfloat16)
    tilted_low = tilted.astype(jnp.bfloat16)
    stacked_weights = jnp.concatenate([tilted_low, weights_low], axis=-1)
    stacked_values = jnp.concatenate([value_heads, valuetan_heads], axis=0)
    carried_part = jnp.einsum(
        "qhk,khd->qhd", stacked_weights, stacked_values, preferred_element_type=jnp.float32
    )
    return (jnp.sum(tilted, axis=-1), carried_part, weights_low)


def per_device(query_rows, key_rows, value_rows, query_tan, key_tan, value_tan):
    spread = (
        lax.all_to_all(query_rows, "head", split_axis=1, concat_axis=0, tiled=True),
        lax.all_to_all(key_rows, "head", split_axis=1, concat_axis=0, tiled=True),
        lax.all_to_all(value_rows, "head", split_axis=1, concat_axis=0, tiled=True),
        lax.all_to_all(query_tan, "head", split_axis=1, concat_axis=0, tiled=True),
        lax.all_to_all(key_tan, "head", split_axis=1, concat_axis=0, tiled=True),
        lax.all_to_all(value_tan, "head", split_axis=1, concat_axis=0, tiled=True),
    )
    query_heads = split_heads(spread[0])
    paired = jnp.concatenate([query_heads, split_heads(spread[3])], axis=-1)
    row_count, head_count = (query_heads.shape[0], query_heads.shape[1])
    floor_row = jnp.full((row_count, head_count), LOW_START, jnp.float32)
    zero_row = jnp.zeros((row_count, head_count), jnp.float32)
    zero_full = jnp.zeros((row_count, head_count, HEAD_DIM), jnp.float32)

    def primal_step(carried_state, key_block):
        row_peak, row_total, mixed_sum = carried_state
        key_heads, value_heads = key_block
        scores = plain_scores(query_heads, key_heads)
        new_peak = jnp.maximum(row_peak, jnp.max(scores, axis=-1))
        rescale = jnp.exp(row_peak - new_peak)
        weights = jnp.exp(scores - new_peak[..., None])
        row_total = rescale * row_total + jnp.sum(weights, axis=-1)
        mixed_sum = rescale[..., None] * mixed_sum + jnp.einsum(
            "qhk,khd->qhd",
            weights.astype(jnp.bfloat16),
            value_heads,
            preferred_element_type=jnp.float32,
        )
        return (new_peak, row_total, mixed_sum)

    row_peak, row_total, mixed_sum = over_blocks(
        primal_step,
        (floor_row, zero_row, zero_full),
        (
            lax.all_gather(spread[1], "blk", axis=0, tiled=True),
            lax.all_gather(spread[2], "blk", axis=0, tiled=True),
        ),
    )

    def tangent_step(carried_state, key_block):
        row_slope, carried = carried_state
        key_heads, value_heads, keytan_heads, valuetan_heads = key_block
        scores = plain_scores(query_heads, key_heads)
        score_tan = tangent_scores(paired, key_heads, keytan_heads)
        weights = jnp.exp(scores - row_peak[..., None])
        slope_part, carried_part, weights_low = tangent_terms(
            weights, score_tan, value_heads, valuetan_heads
        )
        return (row_slope + slope_part, carried + carried_part)

    row_slope, carried = over_blocks(
        tangent_step,
        (zero_row, zero_full),
        (
            lax.all_gather(spread[1], "blk", axis=0, tiled=True),
            lax.all_gather(spread[2], "blk", axis=0, tiled=True),
            lax.all_gather(spread[4], "blk", axis=0, tiled=True),
            lax.all_gather(spread[5], "blk", axis=0, tiled=True),
        ),
    )
    attended = (
        (mixed_sum / row_total[..., None])
        .astype(jnp.bfloat16)
        .reshape(row_count, head_count * HEAD_DIM)
    )
    attended_tan = (
        ((carried - mixed_sum * (row_slope / row_total)[..., None]) / row_total[..., None])
        .astype(jnp.bfloat16)
        .reshape(row_count, head_count * HEAD_DIM)
    )
    returned = (
        lax.all_to_all(attended, "head", split_axis=0, concat_axis=1, tiled=True),
        lax.all_to_all(attended_tan, "head", split_axis=0, concat_axis=1, tiled=True),
    )
    return (returned[0], returned[1])


def solution(mesh):
    return jax.shard_map(
        per_device,
        mesh=mesh,
        in_specs=(
            P(("clip", "blk", "head"), None),
            P(("clip", "blk", "head"), None),
            P(("clip", "blk", "head"), None),
            P(("clip", "blk", "head"), None),
            P(("clip", "blk", "head"), None),
            P(("clip", "blk", "head"), None),
        ),
        out_specs=(P(("clip", "blk", "head"), None), P(("clip", "blk", "head"), None)),
        check_vma=False,
    )
```

profile of v0, /device:TPU:40, one launch (start us, length us, event | category | flops | bytes accessed | tf_op | source)
XLA Modules:
  0.0 345.0 jit_solution(2415751659717892681)
XLA Ops:
  7.2 1.1 copy.110
  8.3 20.1 %all_to_all.146 = bf16[64,4,640]{2,0,1:T(8,128)(2,1)} all-to-all(bf16[64,4,640]{2,0,1:T(8,128)(2,1)S(1)} %bitcast.138), channel_id=1, replica_groups=mesh['clip'=4,'blk'=16,'head'=4] {'head'}, dimensions={1} | all-to-all | bytes 655360 | tf_op jit(solution)/shard_map/all_to_all | solution.py:73
  28.4 1.0 copy.108
  29.4 13.5 %all_to_all.147 = bf16[64,4,640]{2,0,1:T(8,128)(2,1)} all-to-all(bf16[64,4,640]{2,0,1:T(8,128)(2,1)S(1)} %bitcast.139), channel_id=1, replica_groups=mesh['clip'=4,'blk'=16,'head'=4] {'head'}, dimensions={1} | all-to-all | bytes 655360 | tf_op jit(solution)/shard_map/all_to_all | solution.py:74
  43.0 1.0 copy.107
  44.0 19.0 %all_to_all.148 = bf16[64,4,640]{2,0,1:T(8,128)(2,1)} all-to-all(bf16[64,4,640]{2,0,1:T(8,128)(2,1)S(1)} %bitcast.140), channel_id=1, replica_groups=mesh['clip'=4,'blk'=16,'head'=4] {'head'}, dimensions={1} | all-to-all | bytes 655360 | tf_op jit(solution)/shard_map/all_to_all | solution.py:76
  63.1 1.0 copy.105
  64.1 18.0 %all_to_all.149 = bf16[64,4,640]{2,0,1:T(8,128)(2,1)} all-to-all(bf16[64,4,640]{2,0,1:T(8,128)(2,1)S(1)} %bitcast.141), channel_id=1, replica_groups=mesh['clip'=4,'blk'=16,'head'=4] {'head'}, dimensions={1} | all-to-all | bytes 655360 | tf_op jit(solution)/shard_map/all_to_all | solution.py:77
  82.8 3.5 %all-to-all-start.1 = ((bf16[64,4,640]{2,0,1:T(8,128)(2,1)}), bf16[64,4,640]{2,0,1:T(8,128)(2,1)S(1)}, u32[]{:S(2)}, u32[]{:S(2)}) async-start(bf16[64,4,640]{2,0,1:T(8,128)(2,1)} %bitcast.98), calls=%async_computation.1 | async-start | bytes 655360 | tf_op jit(solution)/shard_map/all_to_all | solution.py:72
  87.1 9.3 %all-to-all-done.1 = bf16[64,4,640]{2,0,1:T(8,128)(2,1)S(1)} async-done(((bf16[64,4,640]{2,0,1:T(8,128)(2,1)}), bf16[64,4,640]{2,0,1:T(8,128)(2,1)S(1)}, u32[]{:S(2)}, u32[]{:S(2)}) %all-to-all-start.1) | async-done | bytes 327712 | tf_op jit(solution)/shard_map/all_to_all | solution.py:72
  96.4 3.5 %all-to-all-start.5 = ((bf16[64,4,640]{2,0,1:T(8,128)(2,1)}), bf16[64,4,640]{2,0,1:T(8,128)(2,1)S(1)}, u32[]{:S(2)}, u32[]{:S(2)}) async-start(bf16[64,4,640]{2,0,1:T(8,128)(2,1)} %bitcast.95), calls=%async_computation.5 | async-start | bytes 655360 | tf_op jit(solution)/shard_map/all_to_all | solution.py:75
  100.3 14.4 %all-to-all-done.5 = bf16[64,4,640]{2,0,1:T(8,128)(2,1)S(1)} async-done(((bf16[64,4,640]{2,0,1:T(8,128)(2,1)}), bf16[64,4,640]{2,0,1:T(8,128)(2,1)S(1)}, u32[]{:S(2)}, u32[]{:S(2)}) %all-to-all-start.5) | async-done | bytes 327712 | tf_op jit(solution)/shard_map/all_to_all | solution.py:75
  116.4 12.7 %reshape.49 = bf16[2,2048,5,128]{3,2,1,0:T(8,128)(2,1)} reshape(bf16[4096,640]{1,0:T(8,128)(2,1)} %all-gather.5.cloned.1.call-done) | data formatting | bytes 10485760 | tf_op jit(solution)/shard_map/reshape;reshape | solution.py:23
  129.1 6.5 %copy.63 = bf16[2,2048,5,128]{3,1,2,0:T(8,128)(2,1)} copy(bf16[2,2048,5,128]{3,2,1,0:T(8,128)(2,1)} %reshape.49) | data formatting | bytes 10485760
  135.7 12.7 %reshape.50 = bf16[2,2048,5,128]{3,2,1,0:T(8,128)(2,1)} reshape(bf16[4096,640]{1,0:T(8,128)(2,1)} %all-gather.7.cloned.1.call-done) | data formatting | bytes 10485760 | tf_op jit(solution)/shard_map/reshape;reshape | solution.py:23
  148.3 11.3 %copy.65 = bf16[2,2048,5,128]{1,3,2,0:T(8,128)(2,1)} copy(bf16[2,2048,5,128]{3,2,1,0:T(8,128)(2,1)} %reshape.50) | data formatting | bytes 10485760
  159.6 14.7 %all-gather.9.cloned.1.call-done = bf16[4096,640]{1,0:T(8,128)(2,1)} async-done(((bf16[256,640]{1,0:T(8,128)(2,1)}), bf16[4096,640]{1,0:T(8,128)(2,1)}) %all-gather.9.cloned.1.call-update) | async-done | bytes 5242896 | tf_op jit(solution)/shard_map/all_gather | solution.py:128
  174.3 12.7 %reshape.47 = bf16[2,2048,5,128]{3,2,1,0:T(8,128)(2,1)} reshape(bf16[4096,640]{1,0:T(8,128)(2,1)} %all-gather.9.cloned.1.call-done) | data formatting | bytes 10485760 | tf_op jit(solution)/shard_map/reshape;reshape | solution.py:23
  186.9 6.8 %copy.75 = bf16[2,2048,5,128]{3,1,2,0:T(8,128)(2,1)} copy(bf16[2,2048,5,128]{3,2,1,0:T(8,128)(2,1)} %reshape.47) | data formatting | bytes 10485760
  193.7 36.6 %while.28 = (s32[]{:T(128)}, f32[256,5]{0,1:T(8,128)S(1)}, f32[256,5]{0,1:T(8,128)S(1)}, f32[256,5,128]{0,2,1:T(8,128)S(1)}, bf16[2,2048,5,128]{3,1,2,0:T(8,128)...) while((s32[]{:T(128)}, f32[256,5]{0,1:T(8,128)S(1)}, ...), condition=%wide.region_3.4_spmd.clone, body=%wide.region_0.3_spmd.clone.sunk | while | flops 1363646720 | bytes 80364680 | solution.py:38
  193.7 7.3 %bitcast_reduce_fusion.2 = (f32[256,5]{0,1:T(8,128)S(1)}, f32[5,2048,256]{2,1,0:T(8,128)}) fusion(bf16[256,5,128]{2,0,1:T(8,128)(2,1)S(1)} %get-tuple-element.407, bf16[2,2048,5,128]{3,1,2,0:T(8,128)(2,1)} %get-tuple-element.406, s32[]{:T(128)} %get-tuple-element.393), kind=kOutput, calls=%fused_computation.1.clone.1 | convolution fusion | flops 676330240 | bytes 13440512 | tf_op jit(solution)/shard_map/while/body/eval_jaxpr/qhd,khd->qhk/dot_general | solution.py:45
  201.1 6.1 %fusion.75 = f32[256,5]{0,1:T(8,128)S(1)} fusion(f32[5,2048,256]{2,1,0:T(8,128)} %get-tuple-element.363, f32[256,5]{0,1:T(8,128)S(1)} %select_maximum_fusion.2), kind=kLoop, calls=%fused_computation.4.clone.1 | loop fusion | flops 7863040 | bytes 10496000 | tf_op jit(solution)/shard_map/while/body/eval_jaxpr/reduce_sum | solution.py:93
  207.1 1.3 copy-done
  208.4 3.8 %fusion.77 = f32[256,5,128]{0,2,1:T(8,128)S(1)} fusion(f32[5,2048,256]{2,1,0:T(8,128)S(1)} %copy-done, f32[256,5]{0,1:T(8,128)S(1)} %select_maximum_fusion.2, bf16[2,2048,5,128]{1,3,2,0:T(8,128)(2,1)} %get-tuple-element.408, s32[]{:T(128)} %get-tuple-element.393, f32[256,5,128]{0,2,1:T(8,128)S(1)} %get-tuple-element.396, ...), kind=kOutput, calls=%fused_computation.14.clone.1 | convolution fusion | flops 679444480 | bytes 14428673 | tf_op jit(solution)/shard_map/while/body/eval_jaxpr/qhk,khd->qhd/dot_general | solution.py:94
  212.2 7.3 %bitcast_reduce_fusion.2 = (f32[256,5]{0,1:T(8,128)S(1)}, f32[5,2048,256]{2,1,0:T(8,128)}) fusion(bf16[256,5,128]{2,0,1:T(8,128)(2,1)S(1)} %get-tuple-element.407, bf16[2,2048,5,128]{3,1,2,0:T(8,128)(2,1)} %get-tuple-element.406, s32[]{:T(128)} %get-tuple-element.393), kind=kOutput, calls=%fused_computation.1.clone.1 | convolution fusion | flops 676330240 | bytes 13440512 | tf_op jit(solution)/shard_map/while/body/eval_jaxpr/qhd,khd->qhk/dot_general | solution.py:45
  219.6 5.8 %fusion.75 = f32[256,5]{0,1:T(8,128)S(1)} fusion(f32[5,2048,256]{2,1,0:T(8,128)} %get-tuple-element.363, f32[256,5]{0,1:T(8,128)S(1)} %select_maximum_fusion.2), kind=kLoop, calls=%fused_computation.4.clone.1 | loop fusion | flops 7863040 | bytes 10496000 | tf_op jit(solution)/shard_map/while/body/eval_jaxpr/reduce_sum | solution.py:93
  225.4 1.1 copy-done
  226.5 3.7 %fusion.77 = f32[256,5,128]{0,2,1:T(8,128)S(1)} fusion(f32[5,2048,256]{2,1,0:T(8,128)S(1)} %copy-done, f32[256,5]{0,1:T(8,128)S(1)} %select_maximum_fusion.2, bf16[2,2048,5,128]{1,3,2,0:T(8,128)(2,1)} %get-tuple-element.408, s32[]{:T(128)} %get-tuple-element.393, f32[256,5,128]{0,2,1:T(8,128)S(1)} %get-tuple-element.396, ...), kind=kOutput, calls=%fused_computation.14.clone.1 | convolution fusion | flops 679444480 | bytes 14428673 | tf_op jit(solution)/shard_map/while/body/eval_jaxpr/qhk,khd->qhd/dot_general | solution.py:94
  230.3 12.9 %reshape.48 = bf16[2,2048,5,128]{3,2,1,0:T(8,128)(2,1)} reshape(bf16[4096,640]{1,0:T(8,128)(2,1)} %all-gather.11.cloned.1.call-done) | data formatting | bytes 10485760 | tf_op jit(solution)/shard_map/reshape;reshape | solution.py:23
  243.2 11.2 %copy.78 = bf16[2,2048,5,128]{1,3,2,0:T(8,128)(2,1)} copy(bf16[2,2048,5,128]{3,2,1,0:T(8,128)(2,1)} %reshape.48) | data formatting | bytes 10485760
  254.4 46.3 %while.29 = (s32[]{:T(128)}, f32[256,5]{0,1:T(8,128)S(1)}, f32[256,5,128]{0,2,1:T(8,128)}, bf16[2,2048,5,128]{3,1,2,0:T(8,128)(2,1)}, bf16[256,5,128]{2,0,1:T(8,...) while((s32[]{:T(128)}, f32[256,5]{0,1:T(8,128)S(1)}, ...), condition=%wide.region_6.7_spmd.clone, body=%wide.region_4.6_spmd.clone.sunk | while | flops 3421308160 | bytes 94075064 | solution.py:38
  254.4 2.9 dynamic-slice_bitcast_fusion.6
  257.4 3.6 %fusion.83 = (bf16[256,5,2048]{0,2,1:T(8,128)(2,1)}, f32[5,2048,256]{2,1,0:T(8,128)S(1)}) fusion(f32[256,5]{0,1:T(8,128)S(1)} %get-tuple-element.440, bf16[2048,5,128]{2,0,1:T(8,128)(2,1)S(1)} %get-tuple-element.376, bf16[256,5,128]{2,0,1:T(8,128)(2,1)S(1)} %get-tuple-element.439), kind=kOutput, calls=%fused_computation.30.clone.1 | convolution fusion | flops 678952960 | bytes 18682880 | tf_op jit(solution)/shard_map/while/body/eval_jaxpr/qhd,khd->qhk/dot_general | solution.py:45
  260.9 5.8 %fusion.84 = (bf16[256,5,2048]{0,2,1:T(8,128)(2,1)}, f32[256,5]{0,1:T(8,128)S(1)}) fusion(bf16[256,5,256]{2,0,1:T(8,128)(2,1)} %get-tuple-element.442, bf16[2048,5,128]{2,0,1:T(8,128)(2,1)S(1)} %get-tuple-element.376, bf16[2048,5,128]{2,0,1:T(8,128)(2,1)S(1)} %get-tuple-element.377, f32[256,5]{0,1:T(8,128)S(1)} %get-tuple-element.440, ...), kind=kOutput, calls=%fused_computation.56.clone.1 | convolution fusion | flops 1368390400 | bytes 21637120 | tf_op jit(solution)/shard_map/while/body/eval_jaxpr/qhd,khd->qhk/dot_general | solution.py:54
  266.7 3.7 %dynamic-slice_bitcast_fusion.7 = (bf16[2048,5,128]{0,2,1:T(8,128)(2,1)S(1)}, bf16[2048,5,128]{0,2,1:T(8,128)(2,1)}) fusion(bf16[2,2048,5,128]{1,3,2,0:T(8,128)(2,1)} %get-tuple-element.444, s32[]{:T(128)} %get-tuple-element.423, bf16[2,2048,5,128]{1,3,2,0:T(8,128)(2,1)S(1)} %bitcast.129), kind=kLoop, calls=%fused_computation.38.clone.1 | loop fusion | bytes 10485764 | tf_op jit(solution)/shard_map/while/body/jit(dynamic_index_in_dim)/squeeze | solution.py:38
  270.3 7.2 %fusion.85 = f32[256,5,128]{0,2,1:T(8,128)} fusion(bf16[256,5,2048]{0,2,1:T(8,128)(2,1)} %get-tuple-element.380, bf16[256,5,2048]{0,2,1:T(8,128)(2,1)} %get-tuple-element.381, bf16[2048,5,128]{0,2,1:T(8,128)(2,1)S(1)} %get-tuple-element.382, bf16[2048,5,128]{0,2,1:T(8,128)(2,1)} %get-tuple-element.383, f32[256,5,128]{0,2,1:T(8,128)} %get-tuple-element.425, ...), kind=kOutput, calls=%fused_computation.43.clone.1 | convolution fusion | flops 1373962240 | bytes 17039360 | tf_op jit(solution)/shard_map/while/body/eval_jaxpr/qhk,khd->qhd/dot_general | solution.py:64
  277.5 2.9 dynamic-slice_bitcast_fusion.6
  280.5 3.6 %fusion.83 = (bf16[256,5,2048]{0,2,1:T(8,128)(2,1)}, f32[5,2048,256]{2,1,0:T(8,128)S(1)}) fusion(f32[256,5]{0,1:T(8,128)S(1)} %get-tuple-element.440, bf16[2048,5,128]{2,0,1:T(8,128)(2,1)S(1)} %get-tuple-element.376, bf16[256,5,128]{2,0,1:T(8,128)(2,1)S(1)} %get-tuple-element.439), kind=kOutput, calls=%fused_computation.30.clone.1 | convolution fusion | flops 678952960 | bytes 18682880 | tf_op jit(solution)/shard_map/while/body/eval_jaxpr/qhd,khd->qhk/dot_general | solution.py:45
  284.0 5.8 %fusion.84 = (bf16[256,5,2048]{0,2,1:T(8,128)(2,1)}, f32[256,5]{0,1:T(8,128)S(1)}) fusion(bf16[256,5,256]{2,0,1:T(8,128)(2,1)} %get-tuple-element.442, bf16[2048,5,128]{2,0,1:T(8,128)(2,1)S(1)} %get-tuple-element.376, bf16[2048,5,128]{2,0,1:T(8,128)(2,1)S(1)} %get-tuple-element.377, f32[256,5]{0,1:T(8,128)S(1)} %get-tuple-element.440, ...), kind=kOutput, calls=%fused_computation.56.clone.1 | convolution fusion | flops 1368390400 | bytes 21637120 | tf_op jit(solution)/shard_map/while/body/eval_jaxpr/qhd,khd->qhk/dot_general | solution.py:54
  289.8 3.7 %dynamic-slice_bitcast_fusion.7 = (bf16[2048,5,128]{0,2,1:T(8,128)(2,1)S(1)}, bf16[2048,5,128]{0,2,1:T(8,128)(2,1)}) fusion(bf16[2,2048,5,128]{1,3,2,0:T(8,128)(2,1)} %get-tuple-element.444, s32[]{:T(128)} %get-tuple-element.423, bf16[2,2048,5,128]{1,3,2,0:T(8,128)(2,1)S(1)} %bitcast.129), kind=kLoop, calls=%fused_computation.38.clone.1 | loop fusion | bytes 10485764 | tf_op jit(solution)/shard_map/while/body/jit(dynamic_index_in_dim)/squeeze | solution.py:38
  293.4 7.3 %fusion.85 = f32[256,5,128]{0,2,1:T(8,128)} fusion(bf16[256,5,2048]{0,2,1:T(8,128)(2,1)} %get-tuple-element.380, bf16[256,5,2048]{0,2,1:T(8,128)(2,1)} %get-tuple-element.381, bf16[2048,5,128]{0,2,1:T(8,128)(2,1)S(1)} %get-tuple-element.382, bf16[2048,5,128]{0,2,1:T(8,128)(2,1)} %get-tuple-element.383, f32[256,5,128]{0,2,1:T(8,128)} %get-tuple-element.425, ...), kind=kOutput, calls=%fused_computation.43.clone.1 | convolution fusion | flops 1373962240 | bytes 17039360 | tf_op jit(solution)/shard_map/while/body/eval_jaxpr/qhk,khd->qhd/dot_general | solution.py:64
  300.7 1.4 divide_convert_fusion
  302.5 1.1 all_to_all.119
  303.6 6.5 %all-to-all-start.3 = ((bf16[4,64,640]{2,1,0:T(8,128)(2,1)}), bf16[4,64,640]{2,1,0:T(8,128)(2,1)S(1)}, u32[]{:S(2)}, u32[]{:S(2)}) async-start(bf16[4,64,640]{2,1,0:T(8,128)(2,1)} %all_to_all.119), calls=%async_computation.3 | async-start | bytes 655360 | tf_op jit(solution)/shard_map/all_to_all | solution.py:143
  310.4 1.1 all_to_all.134
  311.5 11.6 %all-to-all-done.3 = bf16[4,64,640]{2,1,0:T(8,128)(2,1)S(1)} async-done(((bf16[4,64,640]{2,1,0:T(8,128)(2,1)}), bf16[4,64,640]{2,1,0:T(8,128)(2,1)S(1)}, u32[]{:S(2)}, u32[]{:S(2)}) %all-to-all-start.3) | async-done | bytes 327712 | tf_op jit(solution)/shard_map/all_to_all | solution.py:143
  323.2 3.5 %all-to-all-start.7 = ((bf16[4,64,640]{2,1,0:T(8,128)(2,1)}), bf16[4,64,640]{2,1,0:T(8,128)(2,1)S(1)}, u32[]{:S(2)}, u32[]{:S(2)}) async-start(bf16[4,64,640]{2,1,0:T(8,128)(2,1)} %all_to_all.134), calls=%async_computation.7 | async-start | bytes 655360 | tf_op jit(solution)/shard_map/all_to_all | solution.py:144
  327.4 10.3 %all-to-all-done.7 = bf16[4,64,640]{2,1,0:T(8,128)(2,1)S(1)} async-done(((bf16[4,64,640]{2,1,0:T(8,128)(2,1)}), bf16[4,64,640]{2,1,0:T(8,128)(2,1)S(1)}, u32[]{:S(2)}, u32[]{:S(2)}) %all-to-all-start.7) | async-done | bytes 327712 | tf_op jit(solution)/shard_map/all_to_all | solution.py:144
  (58 shorter events, 6.0 us)
Async XLA Ops:
  7.2 74.9 %copy-start.4 = (bf16[64,2560]{1,0:T(8,128)(2,1)S(1)}, bf16[64,2560]{1,0:T(8,128)(2,1)}, u32[]{:S(2)}) copy-start(bf16[64,2560]{1,0:T(8,128)(2,1)} %param.10) | copy-start | bytes 983044
  7.2 79.1 %copy-start.5 = (bf16[64,2560]{1,0:T(8,128)(2,1)S(1)}, bf16[64,2560]{1,0:T(8,128)(2,1)}, u32[]{:S(2)}) copy-start(bf16[64,2560]{1,0:T(8,128)(2,1)} %param.13) | copy-start | bytes 983044
  7.2 109.2 %all-gather.5.cloned.1.call-start = ((), (), s32[]{:S(2)}) async-start(), calls=%async_computation.8 | async-start | bytes 5570560 | tf_op jit(solution)/shard_map/all_gather | solution.py:106
  28.4 107.3 %all-gather.7.cloned.1.call-start = ((), (), s32[]{:S(2)}) async-start(), calls=%async_computation.9 | async-start | bytes 5570560 | tf_op jit(solution)/shard_map/all_gather | solution.py:107
  42.9 131.4 %all-gather.9.cloned.1.call-start = ((), (), s32[]{:S(2)}) async-start(), calls=%async_computation.10 | async-start | bytes 5570560 | tf_op jit(solution)/shard_map/all_gather | solution.py:128
  63.0 167.3 %all-gather.11.cloned.1.call-start = ((), (), s32[]{:S(2)}) async-start(), calls=%async_computation.11 | async-start | bytes 5570560 | tf_op jit(solution)/shard_map/all_gather | solution.py:129
  82.8 13.5 %all-to-all-start.1 = ((bf16[64,4,640]{2,0,1:T(8,128)(2,1)}), bf16[64,4,640]{2,0,1:T(8,128)(2,1)S(1)}, u32[]{:S(2)}, u32[]{:S(2)}) async-start(bf16[64,4,640]{2,0,1:T(8,128)(2,1)} %bitcast.98), calls=%async_computation.1 | async-start | bytes 655360 | tf_op jit(solution)/shard_map/all_to_all | solution.py:72
  96.4 18.4 %all-to-all-start.5 = ((bf16[64,4,640]{2,0,1:T(8,128)(2,1)}), bf16[64,4,640]{2,0,1:T(8,128)(2,1)S(1)}, u32[]{:S(2)}, u32[]{:S(2)}) async-start(bf16[64,4,640]{2,0,1:T(8,128)(2,1)} %bitcast.95), calls=%async_computation.5 | async-start | bytes 655360 | tf_op jit(solution)/shard_map/all_to_all | solution.py:75
  201.1 7.4 %copy-start = (f32[5,2048,256]{2,1,0:T(8,128)S(1)}, f32[5,2048,256]{2,1,0:T(8,128)}, u32[]{:S(2)}) copy-start(f32[5,2048,256]{2,1,0:T(8,128)} %get-tuple-element.363) | copy-start | bytes 31457284 | tf_op jit(solution)/shard_map/while
  219.6 7.0 %copy-start = (f32[5,2048,256]{2,1,0:T(8,128)S(1)}, f32[5,2048,256]{2,1,0:T(8,128)}, u32[]{:S(2)}) copy-start(f32[5,2048,256]{2,1,0:T(8,128)} %get-tuple-element.363) | copy-start | bytes 31457284 | tf_op jit(solution)/shard_map/while
  230.3 12.9 %copy-start.1 = (f32[256,5,128]{0,2,1:T(8,128)}, f32[256,5,128]{0,2,1:T(8,128)S(1)}, u32[]{:S(2)}) copy-start(f32[256,5,128]{0,2,1:T(8,128)S(1)} %get-tuple-element.94) | copy-start | bytes 1966084
  230.3 12.9 %copy-start.2 = (f32[256,5]{0,1:T(8,128)}, f32[256,5]{0,1:T(8,128)S(1)}, u32[]{:S(2)}) copy-start(f32[256,5]{0,1:T(8,128)S(1)} %get-tuple-element.95) | copy-start | bytes 15364
  254.4 46.3 %copy-start.3 = (f32[256,5]{0,1:T(8,128)S(1)}, f32[256,5]{0,1:T(8,128)}, u32[]{:S(2)}) copy-start(f32[256,5]{0,1:T(8,128)} %copy-done.2) | copy-start | bytes 15364
  257.3 9.3 %slice-start = ((s8[5242880]{0:T(1024)(128)(4,1)}), s8[4194304]{0:T(1024)(128)(4,1)S(1)}, s32[]{:S(2)}) async-start(s8[5242880]{0:T(1024)(128)(4,1)} %bitcast.128), calls=%async_computation.12 | async-start | bytes 8388608 | tf_op jit(solution)/shard_map/while
  260.9 5.8 %slice-start.1 = ((s8[5242880]{0:T(1024)(128)(4,1)}), s8[1048576]{0:T(1024)(128)(4,1)S(1)}, s32[]{:S(2)}) async-start(s8[5242880]{0:T(1024)(128)(4,1)} %bitcast.128), calls=%async_computation.13 | async-start | bytes 2097152 | tf_op jit(solution)/shard_map/while
  280.5 9.3 %slice-start = ((s8[5242880]{0:T(1024)(128)(4,1)}), s8[4194304]{0:T(1024)(128)(4,1)S(1)}, s32[]{:S(2)}) async-start(s8[5242880]{0:T(1024)(128)(4,1)} %bitcast.128), calls=%async_computation.12 | async-start | bytes 8388608 | tf_op jit(solution)/shard_map/while
  284.0 5.8 %slice-start.1 = ((s8[5242880]{0:T(1024)(128)(4,1)}), s8[1048576]{0:T(1024)(128)(4,1)S(1)}, s32[]{:S(2)}) async-start(s8[5242880]{0:T(1024)(128)(4,1)} %bitcast.128), calls=%async_computation.13 | async-start | bytes 2097152 | tf_op jit(solution)/shard_map/while
  303.6 19.6 %all-to-all-start.3 = ((bf16[4,64,640]{2,1,0:T(8,128)(2,1)}), bf16[4,64,640]{2,1,0:T(8,128)(2,1)S(1)}, u32[]{:S(2)}, u32[]{:S(2)}) async-start(bf16[4,64,640]{2,1,0:T(8,128)(2,1)} %all_to_all.119), calls=%async_computation.3 | async-start | bytes 655360 | tf_op jit(solution)/shard_map/all_to_all | solution.py:143
  323.2 14.5 %all-to-all-start.7 = ((bf16[4,64,640]{2,1,0:T(8,128)(2,1)}), bf16[4,64,640]{2,1,0:T(8,128)(2,1)S(1)}, u32[]{:S(2)}, u32[]{:S(2)}) async-start(bf16[4,64,640]{2,1,0:T(8,128)(2,1)} %all_to_all.134), calls=%async_computation.7 | async-start | bytes 655360 | tf_op jit(solution)/shard_map/all_to_all | solution.py:144
Sparse Core Ops, SparseCore 0:
  28.5 51.5 all-gather.4
  82.0 48.3 all-gather.6
  132.2 42.0 all-gather.8
  176.0 41.9 all-gather.10
where the time goes:
time: 348 us; the launch traced here: 345 us
  local copies, waits for them, and re-layouts  114 us (33%)
  blocking collectives  70.5 us (20%)
  waiting for transfers between devices  60.4 us (17%)
  matrix products  55.2 us (16%)
  starting transfers between devices  17 us (5%)
  between operations  14 us (4%)
  other arithmetic  13.6 us (4%)
    another operation x4, local copies, waits for them, and re-layouts, split_blocks(): split_heads(piece)  50.9 us
    unnamed x16, local copies, waits for them, and re-layouts  36.9 us
    dot_general x4, matrix products, plain_scores(): jnp.einsum('qhd,khd->qhk', query_heads, key_heads, preferred_element_type...  21.8 us
    all_to_all x1, blocking collectives, per_device(): lax.all_to_all(key_rows, 'head', split_axis=1, concat_axis=0, tiled=True)  20.1 us
    all_to_all x1, blocking collectives, per_device(): lax.all_to_all(key_tan, 'head', split_axis=1, concat_axis=0, tiled=True)  19 us
    all_to_all x1, blocking collectives, per_device(): lax.all_to_all(value_tan, 'head', split_axis=1, concat_axis=0, tiled=True)  18 us
    all_gather x1, waiting for transfers between devices, per_device(): lax.all_gather(spread[4], 'blk', axis=0, tiled=True)  14.7 us
    dot_general x2, matrix products, tangent_terms(): jnp.einsum('qhk,khd->qhd', stacked_weights, stacked_values, preferred_ele...  14.4 us
  transfers between devices with their start and end apart: 8, of which 5 were waited for; matrix products, arithmetic and copies ran while one was open for 30% of the time, Pallas kernels for 0%

commit v1 on v0

v1 whole, which is shorter than its diff:
```python
import functools

import jax
import jax.numpy as jnp
from jax import lax
from jax.experimental import pallas as pl
from jax.experimental.pallas import tpu as pltpu
from jax.sharding import Mesh
from jax.sharding import PartitionSpec as P

HEAD_DIM = 128
HEADS_HERE = 5
GROUPS = 4
ROWS = 64
AXES = ("clip", "zlo", "x", "core", "zhi")
Z = ("zlo", "zhi")
SCALE = HEAD_DIM**-0.5
LOG2E = 1.4426950408889634
CHUNKS = ((0, 2), (2, 5))
VMEM = 40 * 1024 * 1024


def z_index(z):
    return (z % 2) * 4 + z // 2


def z_perm(even, odd):
    return [(z_index(z), z_index((z + (odd if z % 2 else even)) % 8)) for z in range(8)]


TO = (z_perm(-1, 1), z_perm(2, -2), z_perm(-3, 3))
BACK = (z_perm(-1, 1), z_perm(-2, 2), z_perm(-3, 3))
PAIR = z_perm(1, -1)
SWAP = [(0, 1), (1, 0)]
RIGHT = [(i, (i + 1) % 4) for i in range(4)]
LEFT = [(i, (i + 3) % 4) for i in range(4)]


def spec(shape, index_map=None):
    return pl.BlockSpec(shape, index_map) if index_map else pl.BlockSpec(memory_space=pltpu.VMEM)


def pack_body(offs, q, k, v, dq, dk, dv, *outs):
    at = 0
    for source, group in (((k, v, dk, dv), CHUNKS), ((q, dq), CHUNKS)):
        for low, high in group:
            for slot in range(4):
                out = outs[at]
                at += 1
                for a, ref in enumerate(source):
                    for h in range(low, high):
                        col = pl.multiple_of(offs[slot] + h * HEAD_DIM, HEAD_DIM)
                        out[h - low, a] = ref[:, pl.ds(col, HEAD_DIM)]


def pack(offs, arrays):
    shapes = [
        jax.ShapeDtypeStruct((high - low, count, ROWS, HEAD_DIM), jnp.bfloat16)
        for count in (4, 2)
        for low, high in CHUNKS
        for _ in range(4)
    ]
    n = len(CHUNKS)
    outs = pl.pallas_call(
        pack_body,
        out_shape=shapes,
        in_specs=[pl.BlockSpec(memory_space=pltpu.SMEM)] + [spec(None)] * 6,
        out_specs=[spec(None)] * len(shapes),
        compiler_params=pltpu.CompilerParams(vmem_limit_bytes=VMEM),
        name="pack",
    )(offs, *arrays)
    groups = [outs[4 * i : 4 * i + 4] for i in range(2 * n)]
    return groups[:n], groups[n:]


def unpack_body(offs, *refs):
    out, out_tan = refs[-2:]
    at = 0
    for low, high in CHUNKS:
        for slot in range(4):
            ref = refs[at]
            at += 1
            for h in range(low, high):
                col = pl.multiple_of(offs[slot] + h * HEAD_DIM, HEAD_DIM)
                out[:, pl.ds(col, HEAD_DIM)] = ref[h - low, 0]
                out_tan[:, pl.ds(col, HEAD_DIM)] = ref[h - low, 1]


def unpack(offs, pieces):
    shape = jax.ShapeDtypeStruct((ROWS, GROUPS * HEADS_HERE * HEAD_DIM), jnp.bfloat16)
    return pl.pallas_call(
        unpack_body,
        out_shape=[shape, shape],
        in_specs=[pl.BlockSpec(memory_space=pltpu.SMEM)] + [spec(None)] * len(pieces),
        out_specs=[spec(None)] * 2,
        compiler_params=pltpu.CompilerParams(vmem_limit_bytes=VMEM),
        name="unpack",
    )(offs, *pieces)


def fold(block):
    return block.reshape(block.shape[0] * block.shape[1], block.shape[2])


def core_part(q_ref, kv_refs, kk, vv):
    row = 0
    for ref in kv_refs:
        rows = pl.ds(row, ref.shape[0] * ROWS)
        row += ref.shape[0] * ROWS
        kk[rows, :HEAD_DIM] = fold(ref[:, 0, 0])
        kk[rows, HEAD_DIM:] = fold(ref[:, 0, 2])
        vv[rows, :HEAD_DIM] = fold(ref[:, 0, 1])
        vv[rows, HEAD_DIM:] = fold(ref[:, 0, 3])
    q, dq = fold(q_ref[:, 0, 0]), fold(q_ref[:, 0, 1])
    nt = (((1,), (1,)), ((), ()))
    dot = functools.partial(lax.dot_general, preferred_element_type=jnp.float32)
    s = dot(q, kk[:, :HEAD_DIM], nt)
    st = dot(jnp.concatenate([dq, q], axis=1), kk[...], nt)
    m = jnp.max(s, axis=1, keepdims=True)
    p = jnp.exp2((s - m) * (SCALE * LOG2E))
    t = p * st
    total = jnp.sum(p, axis=1, keepdims=True)
    slope = jnp.sum(t, axis=1, keepdims=True)
    nn = (((1,), (0,)), ((), ()))
    pv = dot(p.astype(jnp.bfloat16), vv[...], nn)
    tv = dot(t.astype(jnp.bfloat16), vv[:, :HEAD_DIM], nn)
    inverse = 1.0 / total
    att = pv[:, :HEAD_DIM] * inverse
    slope = slope * (inverse * SCALE)
    tan = (pv[:, HEAD_DIM:] + tv * SCALE) * inverse - att * slope
    return att, tan, m * SCALE + jnp.log(total), slope


def three(value):
    high = value.astype(jnp.bfloat16).astype(jnp.float32)
    rest = value - high
    middle = rest.astype(jnp.bfloat16).astype(jnp.float32)
    return high, middle, rest - middle


def far_body(count, *refs):
    q_ref, kv_refs, out, kk, vv = refs[0], refs[1 : 1 + count], *refs[1 + count :]
    att, tan, lse, slope = core_part(q_ref, kv_refs, kk, vv)
    n = att.shape[0]
    out[0, :n] = att.astype(jnp.bfloat16)
    out[0, n : 2 * n] = tan.astype(jnp.bfloat16)
    lane = lax.broadcasted_iota(jnp.int32, (n, HEAD_DIM), 1)
    stats = jnp.zeros((n, HEAD_DIM), jnp.float32)
    for i, column in enumerate(three(lse) + three(slope)):
        stats = jnp.where(lane == i, column, stats)
    flat = jnp.transpose(stats)[:16].astype(jnp.bfloat16)
    out[0, 2 * n : 2 * n + 16] = flat[:, :HEAD_DIM]
    out[0, 2 * n + 16 :] = flat[:, HEAD_DIM:]


def near_body(count, *refs):
    q_ref, kv_refs, got = refs[0], refs[1 : 1 + count], refs[1 + count]
    outs, (kk, vv) = refs[2 + count : 6 + count], refs[6 + count :]
    att, tan, lse, slope = core_part(q_ref, kv_refs, kk, vv)
    n = att.shape[0]
    att2 = got[0, :n].astype(jnp.float32)
    tan2 = got[0, n : 2 * n].astype(jnp.float32)
    flat = jnp.concatenate([got[0, 2 * n : 2 * n + 16], got[0, 2 * n + 16 :]], axis=1)
    flat = flat.astype(jnp.float32)

    def column(i):
        line = flat[i : i + 1] + flat[i + 1 : i + 2] + flat[i + 2 : i + 3]
        return jnp.transpose(jnp.broadcast_to(line, (HEAD_DIM, n)))

    lse2, slope2 = column(0), column(3)
    w1 = 1.0 / (1.0 + jnp.exp(lse2 - lse))
    w2 = 1.0 / (1.0 + jnp.exp(lse - lse2))
    tan = w1 * tan + w2 * tan2 + (w1 * w2) * (slope - slope2) * (att - att2)
    att = w1 * att + w2 * att2
    for slot in range(4):
        rows = slice(slot * ROWS, (slot + 1) * ROWS)
        outs[slot][0, 0] = att[rows].astype(jnp.bfloat16)
        outs[slot][0, 1] = tan[rows].astype(jnp.bfloat16)


def attend(q, pieces, low, high, got=None):
    heads = high - low
    keys = sum(array.shape[0] for array, _ in pieces) * ROWS
    rows = 4 * ROWS
    in_specs = [pl.BlockSpec((4, 1, 2, ROWS, HEAD_DIM), lambda h: (0, h, 0, 0, 0))]
    for array, first in pieces:
        in_specs.append(
            pl.BlockSpec(
                (array.shape[0], 1, 4, ROWS, HEAD_DIM),
                lambda h, shift=low - first: (0, h + shift, 0, 0, 0),
            )
        )
    args = [q] + [array for array, _ in pieces]
    wide = 2 * rows + 32
    if got is None:
        body = functools.partial(far_body, len(pieces))
        out_shape = jax.ShapeDtypeStruct((heads, wide, HEAD_DIM), jnp.bfloat16)
        out_specs = pl.BlockSpec((1, wide, HEAD_DIM), lambda h: (h, 0, 0))
    else:
        body = functools.partial(near_body, len(pieces))
        args.append(got)
        in_specs.append(pl.BlockSpec((1, wide, HEAD_DIM), lambda h: (h, 0, 0)))
        out_shape = [jax.ShapeDtypeStruct((heads, 2, ROWS, HEAD_DIM), jnp.bfloat16)] * 4
        out_specs = [pl.BlockSpec((1, 2, ROWS, HEAD_DIM), lambda h: (h, 0, 0, 0))] * 4
    return pl.pallas_call(
        body,
        grid=(heads,),
        out_shape=out_shape,
        in_specs=in_specs,
        out_specs=out_specs,
        scratch_shapes=[pltpu.VMEM((keys, 2 * HEAD_DIM), jnp.bfloat16)] * 2,
        compiler_params=pltpu.CompilerParams(vmem_limit_bytes=VMEM),
        cost_estimate=pl.CostEstimate(
            flops=16 * heads * rows * keys * HEAD_DIM,
            bytes_accessed=heads * keys * 4 * HEAD_DIM * 2,
            transcendentals=heads * rows * keys,
        ),
        name="far_rows" if got is None else "near_rows",
    )(*args)


def over_x(array):
    half = array.shape[0] // 2
    right = lax.ppermute(array, "x", RIGHT)
    left = lax.ppermute(array, "x", LEFT)
    if half == 0:
        return [array, right, left, lax.ppermute(right, "x", RIGHT)]
    return [
        array,
        right,
        left,
        lax.ppermute(right[:half], "x", RIGHT),
        lax.ppermute(left[half:], "x", LEFT),
    ]


def both_cores(arrays):
    return list(arrays) + [lax.ppermute(array, "core", SWAP) for array in arrays]


def per_device(query_rows, key_rows, value_rows, query_tan, key_tan, value_tan):
    group, parity = lax.axis_index("zhi"), lax.axis_index("zlo")
    step = 2 * parity - 1
    slots = jnp.stack([group, group + step, group - step, group + 2]) % GROUPS
    offs = (slots * (HEADS_HERE * HEAD_DIM)).astype(jnp.int32)
    kv, qs = pack(offs, (query_rows, key_rows, value_rows, query_tan, key_tan, value_tan))

    def spread(blocks):
        return [blocks[0]] + [lax.ppermute(b, Z, perm) for b, perm in zip(blocks[1:], TO)]

    kv = [spread(blocks) for blocks in kv]
    pieces = [
        [(array, low) for array in both_cores(over_x(jnp.stack(kv[c])))]
        for c, (low, high) in enumerate(CHUNKS)
    ]
    qs = [jnp.stack(spread(blocks)) for blocks in qs]
    far_qs = [lax.ppermute(q, Z, PAIR) for q in qs]
    back = []
    for c, (low, high) in enumerate(CHUNKS):
        sent = attend(far_qs[c], pieces[c], low, high)
        got = lax.ppermute(sent, Z, PAIR)
        outs = attend(qs[c], pieces[c], low, high, got)
        back += [outs[0]] + [lax.ppermute(o, Z, perm) for o, perm in zip(outs[1:], BACK)]
    return tuple(unpack(offs, back))


def solution(mesh):
    fine = Mesh(mesh.devices.reshape(4, 2, 4, 2, 4), AXES)
    rows = P(AXES, None)
    return jax.shard_map(
        per_device,
        mesh=fine,
        in_specs=(rows,) * 6,
        out_specs=(rows, rows),
        check_vma=False,
    )
```

time: 348 us -> 146 us (0.42)
  local copies, waits for them, and re-layouts: 114 us -> 5.92 us
  blocking collectives: 70.5 us -> 0 us
  matrix products: 55.2 us -> 0 us
  starting transfers between devices: 17 us -> 61.8 us
  Pallas kernels: 0 us -> 21.8 us
  other arithmetic: 13.6 us -> 0.34 us
  between operations: 14 us -> 0.82 us
  waiting for transfers between devices: 60.4 us -> 53.1 us
    all_to_all x4 -> x0, blocking collectives: 70.5 us -> none  [the longest x1 20.1 us: per_device(): lax.all_to_all(key_rows, 'head', split_axis=1, concat_axis=0, tiled=True)]
    ppermute x0 -> x40, starting transfers between devices: none -> 61.8 us  [the longest x12 32.1 us: spread(): lax.ppermute(b, Z, perm)]
    dot_general x10 -> x0, matrix products: 55.2 us -> none  [the longest x4 21.8 us: plain_scores(): jnp.einsum('qhd,khd->qhk', query_heads, key_heads, preferred_element_type...]
    ppermute x0 -> x40, waiting for transfers between devices: none -> 53.1 us  [the longest x2 15.1 us: over_x(): lax.ppermute(left[half:], 'x', LEFT)]
    another operation x4 -> x0, local copies, waits for them, and re-layouts: 50.9 us -> none  [split_blocks(): split_heads(piece)]
    all_to_all x4 -> x0, waiting for transfers between devices: 45.7 us -> none  [the longest x1 14.4 us: per_device(): lax.all_to_all(query_tan, 'head', split_axis=1, concat_axis=0, tiled=True)]
    unnamed x16 -> x12, local copies, waits for them, and re-layouts: 36.9 us -> 5.83 us
    pallas_call x0 -> x6, Pallas kernels: none -> 21.8 us  [the longest x4 19.4 us: attend(): pl.pallas_call(body, grid=(heads,), out_shape=out_shape, in_specs=in_spec...]
  transfers between devices with their start and end apart: 8 -> 40, of which waited for: 5 -> 13; matrix products, arithmetic and copies ran while one was open for 30% -> 0% of each run, Pallas kernels for 0% -> 13%
where the time goes in v1:
time: 146 us; the launch traced here: 144 us
  starting transfers between devices  61.8 us (42%)
  waiting for transfers between devices  53.1 us (36%)
  Pallas kernels  21.8 us (15%)
  local copies, waits for them, and re-layouts  5.92 us (4%)
    ppermute x12, starting transfers between devices, spread(): lax.ppermute(b, Z, perm)  32.1 us
    pallas_call x4, Pallas kernels, attend(): pl.pallas_call(body, grid=(heads,), out_shape=out_shape, in_specs=in_spec...  19.4 us
    ppermute x2, waiting for transfers between devices, over_x(): lax.ppermute(left[half:], 'x', LEFT)  15.1 us
    ppermute x12, waiting for transfers between devices, spread(): lax.ppermute(b, Z, perm)  14.5 us
    ppermute x6, starting transfers between devices, per_device(): lax.ppermute(o, Z, perm)  11.4 us
    ppermute x2, waiting for transfers between devices, per_device(): got = lax.ppermute(sent, Z, PAIR)  6.81 us
    ppermute x6, waiting for transfers between devices, per_device(): lax.ppermute(o, Z, perm)  6.55 us
    ppermute x2, waiting for transfers between devices, over_x(): lax.ppermute(right[:half], 'x', RIGHT)  6.2 us
  transfers between devices with their start and end apart: 40, of which 13 were waited for; matrix products, arithmetic and copies ran while one was open for 0% of the time, Pallas kernels for 13%

profile of v1, /device:TPU:40, one launch (start us, length us, event | category | flops | bytes accessed | tf_op | source)
XLA Modules:
  0.0 143.8 jit_solution(5801649946756469142)
XLA Ops:
  0.7 1.0 copy-done
  1.7 1.0 copy-done.1
  2.7 1.0 copy-done.2
  3.6 1.0 copy-done.3
  4.6 1.0 copy-done.4
  5.6 1.0 copy-done.5
  6.6 0.9 pack.1
  7.5 2.0 %collective-permute-start.3 = (bf16[2,4,64,128]{3,2,1,0:T(8,128)(2,1)S(1)}, bf16[2,4,64,128]{3,2,1,0:T(8,128)(2,1)S(1)}, u32[]{:S(2)}, u32[]{:S(2)}) collective-permute-start(bf16[2,4,64,128]{3,2,1,0:T(8,128)(2,1)S(1)} %get-tuple-element.31), channel_id=1, source_target_pairs={{0,35},{32,1},{1,32},{33,2},{2,33},{34,3},{3,34},{35,0},{4,39},{36... | collective-permute-start | bytes 393224 | tf_op jit(solution)/shard_map/ppermute | solution.py:249
  9.5 3.6 %collective-permute-start.4 = (bf16[2,4,64,128]{3,2,1,0:T(8,128)(2,1)S(1)}, bf16[2,4,64,128]{3,2,1,0:T(8,128)(2,1)S(1)}, u32[]{:S(2)}, u32[]{:S(2)}) collective-permute-start(bf16[2,4,64,128]{3,2,1,0:T(8,128)(2,1)S(1)} %get-tuple-element.32), channel_id=1, source_target_pairs={{0,1},{32,35},{1,2},{33,32},{2,3},{34,33},{3,0},{35,34},{4,5},{36,... | collective-permute-start | bytes 393224 | tf_op jit(solution)/shard_map/ppermute | solution.py:249
  13.1 2.8 %collective-permute-start.5 = (bf16[2,4,64,128]{3,2,1,0:T(8,128)(2,1)S(1)}, bf16[2,4,64,128]{3,2,1,0:T(8,128)(2,1)S(1)}, u32[]{:S(2)}, u32[]{:S(2)}) collective-permute-start(bf16[2,4,64,128]{3,2,1,0:T(8,128)(2,1)S(1)} %get-tuple-element.33), channel_id=1, source_target_pairs={{0,34},{32,2},{1,35},{33,3},{2,32},{34,0},{3,33},{35,1},{4,38},{36... | collective-permute-start | bytes 393224 | tf_op jit(solution)/shard_map/ppermute | solution.py:249
  15.9 1.0 collective-permute-start
  16.9 3.9 %collective-permute-start.1 = (bf16[2,2,64,128]{3,2,1,0:T(8,128)(2,1)S(1)}, bf16[2,2,64,128]{3,2,1,0:T(8,128)(2,1)S(1)}, u32[]{:S(2)}, u32[]{:S(2)}) collective-permute-start(bf16[2,2,64,128]{3,2,1,0:T(8,128)(2,1)S(1)} %get-tuple-element.28), channel_id=1, source_target_pairs={{0,1},{32,35},{1,2},{33,32},{2,3},{34,33},{3,0},{35,34},{4,5},{36,... | collective-permute-start | bytes 196616 | tf_op jit(solution)/shard_map/ppermute | solution.py:249
  20.8 7.2 %collective-permute-start.2 = (bf16[2,2,64,128]{3,2,1,0:T(8,128)(2,1)S(1)}, bf16[2,2,64,128]{3,2,1,0:T(8,128)(2,1)S(1)}, u32[]{:S(2)}, u32[]{:S(2)}) collective-permute-start(bf16[2,2,64,128]{3,2,1,0:T(8,128)(2,1)S(1)} %get-tuple-element.29), channel_id=1, source_target_pairs={{0,34},{32,2},{1,35},{33,3},{2,32},{34,0},{3,33},{35,1},{4,38},{36... | collective-permute-start | bytes 196616 | tf_op jit(solution)/shard_map/ppermute | solution.py:249
  28.4 2.8 %collective-permute-start.7 = (bf16[4,2,4,64,128]{4,3,2,1,0:T(8,128)(2,1)S(1)}, bf16[4,2,4,64,128]{4,3,2,1,0:T(8,128)(2,1)S(1)}, u32[]{:S(2)}, u32[]{:S(2)}) collective-permute-start(bf16[4,2,4,64,128]{4,3,2,1,0:T(8,128)(2,1)S(1)} %pad_maximum_fusion.1.refs_1_), channel_id=1, source_target_pairs={{0,24},{8,0},{16,8},{24,16},{1,25},{9,1},{17,9},{25,17},{2,26},{10... | collective-permute-start | bytes 1572872 | tf_op jit(solution)/shard_map/ppermute | solution.py:225
  31.2 1.0 collective-permute-start.20
  32.2 1.0 collective-permute-start.23
  33.7 5.1 %collective-permute-start.25 = (bf16[3,4,64,128]{3,2,1,0:T(8,128)(2,1)S(1)}, bf16[3,4,64,128]{3,2,1,0:T(8,128)(2,1)S(1)}, u32[]{:S(2)}, u32[]{:S(2)}) collective-permute-start(bf16[3,4,64,128]{3,2,1,0:T(8,128)(2,1)S(1)} %get-tuple-element.45), channel_id=1, source_target_pairs={{0,34},{32,2},{1,35},{33,3},{2,32},{34,0},{3,33},{35,1},{4,38},{36... | collective-permute-start | bytes 589832 | tf_op jit(solution)/shard_map/ppermute | solution.py:249
  38.8 3.1 %collective-permute-done.20 = bf16[3,2,64,128]{3,2,1,0:T(8,128)(2,1)S(1)} collective-permute-done((bf16[3,2,64,128]{3,2,1,0:T(8,128)(2,1)S(1)}, bf16[3,2,64,128]{3,2,1,0:T(8,128)(2,1)S(1)}, u32[]{:S(2)}, u32[]{:S(2)}) %collective-permute-start.20) | collective-permute-done | bytes 98336 | tf_op jit(solution)/shard_map/ppermute | solution.py:249
  42.0 9.7 %collective-permute-done.23 = bf16[3,4,64,128]{3,2,1,0:T(8,128)(2,1)S(1)} collective-permute-done((bf16[3,4,64,128]{3,2,1,0:T(8,128)(2,1)S(1)}, bf16[3,4,64,128]{3,2,1,0:T(8,128)(2,1)S(1)}, u32[]{:S(2)}, u32[]{:S(2)}) %collective-permute-start.23) | collective-permute-done | bytes 196640 | tf_op jit(solution)/shard_map/ppermute | solution.py:249
  51.7 4.0 %collective-permute-start.22 = (bf16[3,2,64,128]{3,2,1,0:T(8,128)(2,1)S(1)}, bf16[3,2,64,128]{3,2,1,0:T(8,128)(2,1)S(1)}, u32[]{:S(2)}, u32[]{:S(2)}) collective-permute-start(bf16[3,2,64,128]{3,2,1,0:T(8,128)(2,1)S(1)} %get-tuple-element.41), channel_id=1, source_target_pairs={{0,34},{32,2},{1,35},{33,3},{2,32},{34,0},{3,33},{35,1},{4,38},{36... | collective-permute-start | bytes 294920 | tf_op jit(solution)/shard_map/ppermute | solution.py:249
  55.7 1.3 collective-permute-start.15
  57.1 1.3 collective-permute-done.21
  58.4 1.7 %collective-permute-start.27 = (bf16[4,3,4,64,128]{4,3,2,1,0:T(8,128)(2,1)S(1)}, bf16[4,3,4,64,128]{4,3,2,1,0:T(8,128)(2,1)S(1)}, u32[]{:S(2)}, u32[]{:S(2)}) collective-permute-start(bf16[4,3,4,64,128]{4,3,2,1,0:T(8,128)(2,1)S(1)} %pad_maximum_fusion.refs_1_), channel_id=1, source_target_pairs={{0,24},{8,0},{16,8},{24,16},{1,25},{9,1},{17,9},{25,17},{2,26},{10... | collective-permute-start | bytes 2359304 | tf_op jit(solution)/shard_map/ppermute | solution.py:225
  60.5 2.7 %collective-permute-start.35 = (bf16[4,3,2,64,128]{4,3,2,1,0:T(8,128)(2,1)S(1)}, bf16[4,3,2,64,128]{4,3,2,1,0:T(8,128)(2,1)S(1)}, u32[]{:S(2)}, u32[]{:S(2)}) collective-permute-start(bf16[4,3,2,64,128]{4,3,2,1,0:T(8,128)(2,1)S(1)} %pad_maximum_fusion.2.refs_0_), channel_id=1, source_target_pairs={{0,32},{32,0},{1,33},{33,1},{2,34},{34,2},{3,35},{35,3},{4,36},{36... | collective-permute-start | bytes 1179656 | tf_op jit(solution)/shard_map/ppermute | solution.py:257
  63.2 3.3 %collective-permute-start.9 = (bf16[2,2,4,64,128]{4,3,2,1,0:T(8,128)(2,1)S(1)}, bf16[2,2,4,64,128]{4,3,2,1,0:T(8,128)(2,1)S(1)}, u32[]{:S(2)}, u32[]{:S(2)}) collective-permute-start(bf16[2,2,4,64,128]{4,3,2,1,0:T(8,128)(2,1)S(1)} %slice.17), channel_id=1, source_target_pairs={{0,24},{8,0},{16,8},{24,16},{1,25},{9,1},{17,9},{25,17},{2,26},{10... | collective-permute-start | bytes 786440 | tf_op jit(solution)/shard_map/ppermute | solution.py:233
  66.6 3.9 %collective-permute-done.35.refs_0_ = bf16[4,3,2,64,128]{4,3,2,1,0:T(8,128)(2,1)S(1)} collective-permute-done((bf16[4,3,2,64,128]{4,3,2,1,0:T(8,128)(2,1)S(1)}, bf16[4,3,2,64,128]{4,3,2,1,0:T(8,128)(2,1)S(1)}, u32[]{:S(2)}, u32[]{:S(2)}) %collective-permute-start.35) | collective-permute-done | bytes 393248 | tf_op jit(solution)/shard_map/ppermute | solution.py:257
  70.6 6.5 %collective-permute-done.9.refs_5_ = bf16[2,2,4,64,128]{4,3,2,1,0:T(8,128)(2,1)S(1)} collective-permute-done((bf16[2,2,4,64,128]{4,3,2,1,0:T(8,128)(2,1)S(1)}, bf16[2,2,4,64,128]{4,3,2,1,0:T(8,128)(2,1)S(1)}, u32[]{:S(2)}, u32[]{:S(2)}) %collective-permute-start.9) | collective-permute-done | bytes 262176 | tf_op jit(solution)/shard_map/ppermute | solution.py:233
  77.1 3.5 %collective-permute-done.8.refs_4_ = bf16[2,2,4,64,128]{4,3,2,1,0:T(8,128)(2,1)S(1)} collective-permute-done((bf16[2,2,4,64,128]{4,3,2,1,0:T(8,128)(2,1)S(1)}, bf16[2,2,4,64,128]{4,3,2,1,0:T(8,128)(2,1)S(1)}, u32[]{:S(2)}, u32[]{:S(2)}) %collective-permute-start.8) | collective-permute-done | bytes 262176 | tf_op jit(solution)/shard_map/ppermute | solution.py:232
  80.6 0.5 collective-permute-start.14
  81.8 1.7 %collective-permute-start.29 = (bf16[2,3,4,64,128]{4,3,2,1,0:T(8,128)(2,1)S(1)}, bf16[2,3,4,64,128]{4,3,2,1,0:T(8,128)(2,1)S(1)}, u32[]{:S(2)}, u32[]{:S(2)}) collective-permute-start(bf16[2,3,4,64,128]{4,3,2,1,0:T(8,128)(2,1)S(1)} %slice.19), channel_id=1, source_target_pairs={{0,24},{8,0},{16,8},{24,16},{1,25},{9,1},{17,9},{25,17},{2,26},{10... | collective-permute-start | bytes 1179656 | tf_op jit(solution)/shard_map/ppermute | solution.py:233
  84.4 8.6 %collective-permute-done.29.refs_5_ = bf16[2,3,4,64,128]{4,3,2,1,0:T(8,128)(2,1)S(1)} collective-permute-done((bf16[2,3,4,64,128]{4,3,2,1,0:T(8,128)(2,1)S(1)}, bf16[2,3,4,64,128]{4,3,2,1,0:T(8,128)(2,1)S(1)}, u32[]{:S(2)}, u32[]{:S(2)}) %collective-permute-start.29) | collective-permute-done | bytes 393248 | tf_op jit(solution)/shard_map/ppermute | solution.py:233
  92.9 2.7 %collective-permute-done.28.refs_4_ = bf16[2,3,4,64,128]{4,3,2,1,0:T(8,128)(2,1)S(1)} collective-permute-done((bf16[2,3,4,64,128]{4,3,2,1,0:T(8,128)(2,1)S(1)}, bf16[2,3,4,64,128]{4,3,2,1,0:T(8,128)(2,1)S(1)}, u32[]{:S(2)}, u32[]{:S(2)}) %collective-permute-start.28) | collective-permute-done | bytes 393248 | tf_op jit(solution)/shard_map/ppermute | solution.py:232
  95.6 4.0 %far_rows.2 = bf16[2,544,128]{2,1,0:T(8,128)(2,1)S(1)} custom-call(bf16[4,2,2,64,128]{4,3,2,1,0:T(8,128)(2,1)S(1)} %collective-permute-done.15.refs_0_, bf16[4,2,4,64,128]{4,3,2,1,0:T(8,128)(2,1)S(1)} %pad_maximum_fusion.1.refs_1_, bf16[4,2,4,64,128]{4,3,2,1,0:T(8,128)(2,1)S(1)} %collective-permute-done.6.refs_2_, ...), custom_call_target="tpu_custom_call" | custom-call | flops 2147483648 | bytes 4194304 | tf_op jit(solution)/shard_map/far_rows/pallas_call | solution.py:205
  99.6 2.3 %collective-permute-start.16 = (bf16[2,544,128]{2,1,0:T(8,128)(2,1)S(1)}, bf16[2,544,128]{2,1,0:T(8,128)(2,1)S(1)}, u32[]{:S(2)}, u32[]{:S(2)}) collective-permute-start(bf16[2,544,128]{2,1,0:T(8,128)(2,1)S(1)} %far_rows.2), channel_id=1, source_target_pairs={{0,32},{32,0},{1,33},{33,1},{2,34},{34,2},{3,35},{35,3},{4,36},{36... | collective-permute-start | bytes 835592 | tf_op jit(solution)/shard_map/ppermute | solution.py:261
  101.9 5.9 %far_rows.3 = bf16[3,544,128]{2,1,0:T(8,128)(2,1)S(1)} custom-call(bf16[4,3,2,64,128]{4,3,2,1,0:T(8,128)(2,1)S(1)} %collective-permute-done.35.refs_0_, bf16[4,3,4,64,128]{4,3,2,1,0:T(8,128)(2,1)S(1)} %pad_maximum_fusion.refs_1_, bf16[4,3,4,64,128]{4,3,2,1,0:T(8,128)(2,1)S(1)} %collective-permute-done.26.refs_2_, ...), custom_call_target="tpu_custom_call" | custom-call | flops 3221225472 | bytes 6291456 | tf_op jit(solution)/shard_map/far_rows/pallas_call | solution.py:205
  108.0 1.2 collective-permute-done.16.refs_11_
  109.2 3.8 %near_rows.2 = (bf16[2,2,64,128]{3,2,1,0:T(8,128)(2,1)S(1)}, bf16[2,2,64,128]{3,2,1,0:T(8,128)(2,1)S(1)}, bf16[2,2,64,128]{3,2,1,0:T(8,128)(2,1)S(1)}, bf16[2,2,64,128]{3,2,1,0:T(8,128)(2,1)S(1)}) custom-call(bf16[4,2,2,64,128]{4,3,2,1,0:T(8,128)(2,1)S(1)} %pad_maximum_fusion.3.refs_0_, bf16[4,2,4,64,128]{4,3,2,1,0:T(8,128)(2,1)S(1)} %pad_maximum_fusion.1.refs_1_, ...), custom_call_target="tpu_custom_call" | custom-call | flops 2147483648 | bytes 4194304 | tf_op jit(solution)/shard_map/near_rows/pallas_call | solution.py:205
  113.0 1.1 collective-permute-start.17
  114.1 5.6 %collective-permute-done.36.refs_11_ = bf16[3,544,128]{2,1,0:T(8,128)(2,1)S(1)} collective-permute-done((bf16[3,544,128]{2,1,0:T(8,128)(2,1)S(1)}, bf16[3,544,128]{2,1,0:T(8,128)(2,1)S(1)}, u32[]{:S(2)}, u32[]{:S(2)}) %collective-permute-start.36) | collective-permute-done | bytes 417824 | tf_op jit(solution)/shard_map/ppermute | solution.py:261
  119.7 5.7 %near_rows.3 = (bf16[3,2,64,128]{3,2,1,0:T(8,128)(2,1)S(1)}, bf16[3,2,64,128]{3,2,1,0:T(8,128)(2,1)S(1)}, bf16[3,2,64,128]{3,2,1,0:T(8,128)(2,1)S(1)}, bf16[3,2,64,128]{3,2,1,0:T(8,128)(2,1)S(1)}) custom-call(bf16[4,3,2,64,128]{4,3,2,1,0:T(8,128)(2,1)S(1)} %pad_maximum_fusion.2.refs_0_, bf16[4,3,4,64,128]{4,3,2,1,0:T(8,128)(2,1)S(1)} %pad_maximum_fusion.refs_1_, ...), custom_call_target="tpu_custom_call" | custom-call | flops 3221225472 | bytes 6291456 | tf_op jit(solution)/shard_map/near_rows/pallas_call | solution.py:205
  125.4 1.1 collective-permute-start.37
  126.5 3.3 %collective-permute-start.38 = (bf16[3,2,64,128]{3,2,1,0:T(8,128)(2,1)S(1)}, bf16[3,2,64,128]{3,2,1,0:T(8,128)(2,1)S(1)}, u32[]{:S(2)}, u32[]{:S(2)}) collective-permute-start(bf16[3,2,64,128]{3,2,1,0:T(8,128)(2,1)S(1)} %get-tuple-element.48), channel_id=1, source_target_pairs={{0,3},{32,33},{1,0},{33,34},{2,1},{34,35},{3,2},{35,32},{4,7},{36,... | collective-permute-start | bytes 294920 | tf_op jit(solution)/shard_map/ppermute | solution.py:263
  129.8 1.3 collective-permute-start.39
  131.1 1.3 collective-permute-start.18
  132.4 3.3 %collective-permute-start.19 = (bf16[2,2,64,128]{3,2,1,0:T(8,128)(2,1)S(1)}, bf16[2,2,64,128]{3,2,1,0:T(8,128)(2,1)S(1)}, u32[]{:S(2)}, u32[]{:S(2)}) collective-permute-start(bf16[2,2,64,128]{3,2,1,0:T(8,128)(2,1)S(1)} %get-tuple-element.37), channel_id=1, source_target_pairs={{0,34},{32,2},{1,35},{33,3},{2,32},{34,0},{3,33},{35,1},{4,38},{36... | collective-permute-start | bytes 196616 | tf_op jit(solution)/shard_map/ppermute | solution.py:263
  135.7 5.1 %collective-permute-done.18.refs_2_ = bf16[2,2,64,128]{3,2,1,0:T(8,128)(2,1)S(1)} collective-permute-done((bf16[2,2,64,128]{3,2,1,0:T(8,128)(2,1)S(1)}, bf16[2,2,64,128]{3,2,1,0:T(8,128)(2,1)S(1)}, u32[]{:S(2)}, u32[]{:S(2)}) %collective-permute-start.18) | collective-permute-done | bytes 65568 | tf_op jit(solution)/shard_map/ppermute | solution.py:263
  140.8 1.5 %collective-permute-done.19.refs_3_ = bf16[2,2,64,128]{3,2,1,0:T(8,128)(2,1)S(1)} collective-permute-done((bf16[2,2,64,128]{3,2,1,0:T(8,128)(2,1)S(1)}, bf16[2,2,64,128]{3,2,1,0:T(8,128)(2,1)S(1)}, u32[]{:S(2)}, u32[]{:S(2)}) %collective-permute-start.19) | collective-permute-done | bytes 65568 | tf_op jit(solution)/shard_map/ppermute | solution.py:263
  142.3 1.5 %unpack.1 = (bf16[64,2560]{1,0:T(8,128)(2,1)}, bf16[64,2560]{1,0:T(8,128)(2,1)}) custom-call(s32[4]{0:T(128)S(1)} %fusion.offs, bf16[2,2,64,128]{3,2,1,0:T(8,128)(2,1)S(1)} %get-tuple-element.34.refs_0_, bf16[2,2,64,128]{3,2,1,0:T(8,128)(2,1)S(1)} %collective-permute-done.17.refs_1_, bf16[2,2,64,128]{3,2,1,0:T(8,128)(2,1)S(1)} %collective-permute-done.18.refs_2_, ...), custom_call_target="tpu_custom_call" | custom-call | tf_op jit(solution)/shard_map/unpack/pallas_call | solution.py:91
  (59 shorter events, 3.2 us)
Async XLA Ops:
  0.7 1.0 copy-start
  1.7 1.0 copy-start.1
  2.7 1.0 copy-start.2
  3.6 1.0 copy-start.3
  4.6 1.0 copy-start.4
  5.6 1.0 copy-start.5
  7.5 13.3 %collective-permute-start.3 = (bf16[2,4,64,128]{3,2,1,0:T(8,128)(2,1)S(1)}, bf16[2,4,64,128]{3,2,1,0:T(8,128)(2,1)S(1)}, u32[]{:S(2)}, u32[]{:S(2)}) collective-permute-start(bf16[2,4,64,128]{3,2,1,0:T(8,128)(2,1)S(1)} %get-tuple-element.31), channel_id=1, source_target_pairs={{0,35},{32,1},{1,32},{33,2},{2,33},{34,3},{3,34},{35,0},{4,39},{36... | collective-permute-start | bytes 393224 | tf_op jit(solution)/shard_map/ppermute | solution.py:249
  9.5 18.5 %collective-permute-start.4 = (bf16[2,4,64,128]{3,2,1,0:T(8,128)(2,1)S(1)}, bf16[2,4,64,128]{3,2,1,0:T(8,128)(2,1)S(1)}, u32[]{:S(2)}, u32[]{:S(2)}) collective-permute-start(bf16[2,4,64,128]{3,2,1,0:T(8,128)(2,1)S(1)} %get-tuple-element.32), channel_id=1, source_target_pairs={{0,1},{32,35},{1,2},{33,32},{2,3},{34,33},{3,0},{35,34},{4,5},{36,... | collective-permute-start | bytes 393224 | tf_op jit(solution)/shard_map/ppermute | solution.py:249
  13.1 15.2 %collective-permute-start.5 = (bf16[2,4,64,128]{3,2,1,0:T(8,128)(2,1)S(1)}, bf16[2,4,64,128]{3,2,1,0:T(8,128)(2,1)S(1)}, u32[]{:S(2)}, u32[]{:S(2)}) collective-permute-start(bf16[2,4,64,128]{3,2,1,0:T(8,128)(2,1)S(1)} %get-tuple-element.33), channel_id=1, source_target_pairs={{0,34},{32,2},{1,35},{33,3},{2,32},{34,0},{3,33},{35,1},{4,38},{36... | collective-permute-start | bytes 393224 | tf_op jit(solution)/shard_map/ppermute | solution.py:249
  15.9 16.3 %collective-permute-start = (bf16[2,2,64,128]{3,2,1,0:T(8,128)(2,1)S(1)}, bf16[2,2,64,128]{3,2,1,0:T(8,128)(2,1)S(1)}, u32[]{:S(2)}, u32[]{:S(2)}) collective-permute-start(bf16[2,2,64,128]{3,2,1,0:T(8,128)(2,1)S(1)} %get-tuple-element.27), channel_id=1, source_target_pairs={{0,35},{32,1},{1,32},{33,2},{2,33},{34,3},{3,34},{35,0},{4,39},{36... | collective-permute-start | bytes 196616 | tf_op jit(solution)/shard_map/ppermute | solution.py:249
  16.9 16.3 %collective-permute-start.1 = (bf16[2,2,64,128]{3,2,1,0:T(8,128)(2,1)S(1)}, bf16[2,2,64,128]{3,2,1,0:T(8,128)(2,1)S(1)}, u32[]{:S(2)}, u32[]{:S(2)}) collective-permute-start(bf16[2,2,64,128]{3,2,1,0:T(8,128)(2,1)S(1)} %get-tuple-element.28), channel_id=1, source_target_pairs={{0,1},{32,35},{1,2},{33,32},{2,3},{34,33},{3,0},{35,34},{4,5},{36,... | collective-permute-start | bytes 196616 | tf_op jit(solution)/shard_map/ppermute | solution.py:249
  20.8 12.9 %collective-permute-start.2 = (bf16[2,2,64,128]{3,2,1,0:T(8,128)(2,1)S(1)}, bf16[2,2,64,128]{3,2,1,0:T(8,128)(2,1)S(1)}, u32[]{:S(2)}, u32[]{:S(2)}) collective-permute-start(bf16[2,2,64,128]{3,2,1,0:T(8,128)(2,1)S(1)} %get-tuple-element.29), channel_id=1, source_target_pairs={{0,34},{32,2},{1,35},{33,3},{2,32},{34,0},{3,33},{35,1},{4,38},{36... | collective-permute-start | bytes 196616 | tf_op jit(solution)/shard_map/ppermute | solution.py:249
  28.4 32.1 %collective-permute-start.7 = (bf16[4,2,4,64,128]{4,3,2,1,0:T(8,128)(2,1)S(1)}, bf16[4,2,4,64,128]{4,3,2,1,0:T(8,128)(2,1)S(1)}, u32[]{:S(2)}, u32[]{:S(2)}) collective-permute-start(bf16[4,2,4,64,128]{4,3,2,1,0:T(8,128)(2,1)S(1)} %pad_maximum_fusion.1.refs_1_), channel_id=1, source_target_pairs={{0,24},{8,0},{16,8},{24,16},{1,25},{9,1},{17,9},{25,17},{2,26},{10... | collective-permute-start | bytes 1572872 | tf_op jit(solution)/shard_map/ppermute | solution.py:225
  31.2 10.7 %collective-permute-start.20 = (bf16[3,2,64,128]{3,2,1,0:T(8,128)(2,1)S(1)}, bf16[3,2,64,128]{3,2,1,0:T(8,128)(2,1)S(1)}, u32[]{:S(2)}, u32[]{:S(2)}) collective-permute-start(bf16[3,2,64,128]{3,2,1,0:T(8,128)(2,1)S(1)} %get-tuple-element.39), channel_id=1, source_target_pairs={{0,35},{32,1},{1,32},{33,2},{2,33},{34,3},{3,34},{35,0},{4,39},{36... | collective-permute-start | bytes 294920 | tf_op jit(solution)/shard_map/ppermute | solution.py:249
  32.2 19.4 %collective-permute-start.23 = (bf16[3,4,64,128]{3,2,1,0:T(8,128)(2,1)S(1)}, bf16[3,4,64,128]{3,2,1,0:T(8,128)(2,1)S(1)}, u32[]{:S(2)}, u32[]{:S(2)}) collective-permute-start(bf16[3,4,64,128]{3,2,1,0:T(8,128)(2,1)S(1)} %get-tuple-element.43), channel_id=1, source_target_pairs={{0,35},{32,1},{1,32},{33,2},{2,33},{34,3},{3,34},{35,0},{4,39},{36... | collective-permute-start | bytes 589832 | tf_op jit(solution)/shard_map/ppermute | solution.py:249
  33.2 18.4 %collective-permute-start.24 = (bf16[3,4,64,128]{3,2,1,0:T(8,128)(2,1)S(1)}, bf16[3,4,64,128]{3,2,1,0:T(8,128)(2,1)S(1)}, u32[]{:S(2)}, u32[]{:S(2)}) collective-permute-start(bf16[3,4,64,128]{3,2,1,0:T(8,128)(2,1)S(1)} %get-tuple-element.44), channel_id=1, source_target_pairs={{0,1},{32,35},{1,2},{33,32},{2,3},{34,33},{3,0},{35,34},{4,5},{36,... | collective-permute-start | bytes 589832 | tf_op jit(solution)/shard_map/ppermute | solution.py:249
  33.7 22.0 %collective-permute-start.25 = (bf16[3,4,64,128]{3,2,1,0:T(8,128)(2,1)S(1)}, bf16[3,4,64,128]{3,2,1,0:T(8,128)(2,1)S(1)}, u32[]{:S(2)}, u32[]{:S(2)}) collective-permute-start(bf16[3,4,64,128]{3,2,1,0:T(8,128)(2,1)S(1)} %get-tuple-element.45), channel_id=1, source_target_pairs={{0,34},{32,2},{1,35},{33,3},{2,32},{34,0},{3,33},{35,1},{4,38},{36... | collective-permute-start | bytes 589832 | tf_op jit(solution)/shard_map/ppermute | solution.py:249
  41.9 21.3 %collective-permute-start.6 = (bf16[4,2,4,64,128]{4,3,2,1,0:T(8,128)(2,1)S(1)}, bf16[4,2,4,64,128]{4,3,2,1,0:T(8,128)(2,1)S(1)}, u32[]{:S(2)}, u32[]{:S(2)}) collective-permute-start(bf16[4,2,4,64,128]{4,3,2,1,0:T(8,128)(2,1)S(1)} %pad_maximum_fusion.1.refs_1_), channel_id=1, source_target_pairs={{0,8},{8,16},{16,24},{24,0},{1,9},{9,17},{17,25},{25,1},{2,10},{10... | collective-permute-start | bytes 1572872 | tf_op jit(solution)/shard_map/ppermute | solution.py:224
  51.7 6.7 %collective-permute-start.21 = (bf16[3,2,64,128]{3,2,1,0:T(8,128)(2,1)S(1)}, bf16[3,2,64,128]{3,2,1,0:T(8,128)(2,1)S(1)}, u32[]{:S(2)}, u32[]{:S(2)}) collective-permute-start(bf16[3,2,64,128]{3,2,1,0:T(8,128)(2,1)S(1)} %get-tuple-element.40), channel_id=1, source_target_pairs={{0,1},{32,35},{1,2},{33,32},{2,3},{34,33},{3,0},{35,34},{4,5},{36,... | collective-permute-start | bytes 294920 | tf_op jit(solution)/shard_map/ppermute | solution.py:249
  51.7 8.5 %collective-permute-start.22 = (bf16[3,2,64,128]{3,2,1,0:T(8,128)(2,1)S(1)}, bf16[3,2,64,128]{3,2,1,0:T(8,128)(2,1)S(1)}, u32[]{:S(2)}, u32[]{:S(2)}) collective-permute-start(bf16[3,2,64,128]{3,2,1,0:T(8,128)(2,1)S(1)} %get-tuple-element.41), channel_id=1, source_target_pairs={{0,34},{32,2},{1,35},{33,3},{2,32},{34,0},{3,33},{35,1},{4,38},{36... | collective-permute-start | bytes 294920 | tf_op jit(solution)/shard_map/ppermute | solution.py:249
  55.7 10.9 %collective-permute-start.15 = (bf16[4,2,2,64,128]{4,3,2,1,0:T(8,128)(2,1)S(1)}, bf16[4,2,2,64,128]{4,3,2,1,0:T(8,128)(2,1)S(1)}, u32[]{:S(2)}, u32[]{:S(2)}) collective-permute-start(bf16[4,2,2,64,128]{4,3,2,1,0:T(8,128)(2,1)S(1)} %pad_maximum_fusion.3.refs_0_), channel_id=1, source_target_pairs={{0,32},{32,0},{1,33},{33,1},{2,34},{34,2},{3,35},{35,3},{4,36},{36... | collective-permute-start | bytes 786440 | tf_op jit(solution)/shard_map/ppermute | solution.py:257
  58.4 22.2 %collective-permute-start.27 = (bf16[4,3,4,64,128]{4,3,2,1,0:T(8,128)(2,1)S(1)}, bf16[4,3,4,64,128]{4,3,2,1,0:T(8,128)(2,1)S(1)}, u32[]{:S(2)}, u32[]{:S(2)}) collective-permute-start(bf16[4,3,4,64,128]{4,3,2,1,0:T(8,128)(2,1)S(1)} %pad_maximum_fusion.refs_1_), channel_id=1, source_target_pairs={{0,24},{8,0},{16,8},{24,16},{1,25},{9,1},{17,9},{25,17},{2,26},{10... | collective-permute-start | bytes 2359304 | tf_op jit(solution)/shard_map/ppermute | solution.py:225
  60.1 21.0 %collective-permute-start.26 = (bf16[4,3,4,64,128]{4,3,2,1,0:T(8,128)(2,1)S(1)}, bf16[4,3,4,64,128]{4,3,2,1,0:T(8,128)(2,1)S(1)}, u32[]{:S(2)}, u32[]{:S(2)}) collective-permute-start(bf16[4,3,4,64,128]{4,3,2,1,0:T(8,128)(2,1)S(1)} %pad_maximum_fusion.refs_1_), channel_id=1, source_target_pairs={{0,8},{8,16},{16,24},{24,0},{1,9},{9,17},{17,25},{25,1},{2,10},{10... | collective-permute-start | bytes 2359304 | tf_op jit(solution)/shard_map/ppermute | solution.py:224
  60.5 10.1 %collective-permute-start.35 = (bf16[4,3,2,64,128]{4,3,2,1,0:T(8,128)(2,1)S(1)}, bf16[4,3,2,64,128]{4,3,2,1,0:T(8,128)(2,1)S(1)}, u32[]{:S(2)}, u32[]{:S(2)}) collective-permute-start(bf16[4,3,2,64,128]{4,3,2,1,0:T(8,128)(2,1)S(1)} %pad_maximum_fusion.2.refs_0_), channel_id=1, source_target_pairs={{0,32},{32,0},{1,33},{33,1},{2,34},{34,2},{3,35},{35,3},{4,36},{36... | collective-permute-start | bytes 1179656 | tf_op jit(solution)/shard_map/ppermute | solution.py:257
  63.2 13.9 %collective-permute-start.9 = (bf16[2,2,4,64,128]{4,3,2,1,0:T(8,128)(2,1)S(1)}, bf16[2,2,4,64,128]{4,3,2,1,0:T(8,128)(2,1)S(1)}, u32[]{:S(2)}, u32[]{:S(2)}) collective-permute-start(bf16[2,2,4,64,128]{4,3,2,1,0:T(8,128)(2,1)S(1)} %slice.17), channel_id=1, source_target_pairs={{0,24},{8,0},{16,8},{24,16},{1,25},{9,1},{17,9},{25,17},{2,26},{10... | collective-permute-start | bytes 786440 | tf_op jit(solution)/shard_map/ppermute | solution.py:233
  66.6 14.1 %collective-permute-start.8 = (bf16[2,2,4,64,128]{4,3,2,1,0:T(8,128)(2,1)S(1)}, bf16[2,2,4,64,128]{4,3,2,1,0:T(8,128)(2,1)S(1)}, u32[]{:S(2)}, u32[]{:S(2)}) collective-permute-start(bf16[2,2,4,64,128]{4,3,2,1,0:T(8,128)(2,1)S(1)} %slice.16), channel_id=1, source_target_pairs={{0,8},{8,16},{16,24},{24,0},{1,9},{9,17},{17,25},{25,1},{2,10},{10... | collective-permute-start | bytes 786440 | tf_op jit(solution)/shard_map/ppermute | solution.py:232
  70.6 10.7 %collective-permute-start.10 = (bf16[4,2,4,64,128]{4,3,2,1,0:T(8,128)(2,1)S(1)}, bf16[4,2,4,64,128]{4,3,2,1,0:T(8,128)(2,1)S(1)}, u32[]{:S(2)}, u32[]{:S(2)}) collective-permute-start(bf16[4,2,4,64,128]{4,3,2,1,0:T(8,128)(2,1)S(1)} %pad_maximum_fusion.1.refs_1_), channel_id=1, source_target_pairs={{0,4},{4,0},{1,5},{5,1},{2,6},{6,2},{3,7},{7,3},{8,12},{12,8},{9,1... | collective-permute-start | bytes 1572872 | tf_op jit(solution)/shard_map/ppermute | solution.py:238
  77.1 4.7 %collective-permute-start.12 = (bf16[4,2,4,64,128]{4,3,2,1,0:T(8,128)(2,1)S(1)}, bf16[4,2,4,64,128]{4,3,2,1,0:T(8,128)(2,1)S(1)}, u32[]{:S(2)}, u32[]{:S(2)}) collective-permute-start(bf16[4,2,4,64,128]{4,3,2,1,0:T(8,128)(2,1)S(1)} %collective-permute-done.7.refs_3_), channel_id=1, source_target_pairs={{0,4},{4,0},{1,5},{5,1},{2,6},{6,2},{3,7},{7,3},{8,12},{12,8},{9,1... | collective-permute-start | bytes 1572872 | tf_op jit(solution)/shard_map/ppermute | solution.py:238
  80.6 2.9 %collective-permute-start.11 = (bf16[4,2,4,64,128]{4,3,2,1,0:T(8,128)(2,1)S(1)}, bf16[4,2,4,64,128]{4,3,2,1,0:T(8,128)(2,1)S(1)}, u32[]{:S(2)}, u32[]{:S(2)}) collective-permute-start(bf16[4,2,4,64,128]{4,3,2,1,0:T(8,128)(2,1)S(1)} %collective-permute-done.6.refs_2_), channel_id=1, source_target_pairs={{0,4},{4,0},{1,5},{5,1},{2,6},{6,2},{3,7},{7,3},{8,12},{12,8},{9,1... | collective-permute-start | bytes 1572872 | tf_op jit(solution)/shard_map/ppermute | solution.py:238
  80.6 3.2 %collective-permute-start.14 = (bf16[2,2,4,64,128]{4,3,2,1,0:T(8,128)(2,1)S(1)}, bf16[2,2,4,64,128]{4,3,2,1,0:T(8,128)(2,1)S(1)}, u32[]{:S(2)}, u32[]{:S(2)}) collective-permute-start(bf16[2,2,4,64,128]{4,3,2,1,0:T(8,128)(2,1)S(1)} %collective-permute-done.9.refs_5_), channel_id=1, source_target_pairs={{0,4},{4,0},{1,5},{5,1},{2,6},{6,2},{3,7},{7,3},{8,12},{12,8},{9,1... | collective-permute-start | bytes 786440 | tf_op jit(solution)/shard_map/ppermute | solution.py:238
  81.2 2.7 %collective-permute-start.13 = (bf16[2,2,4,64,128]{4,3,2,1,0:T(8,128)(2,1)S(1)}, bf16[2,2,4,64,128]{4,3,2,1,0:T(8,128)(2,1)S(1)}, u32[]{:S(2)}, u32[]{:S(2)}) collective-permute-start(bf16[2,2,4,64,128]{4,3,2,1,0:T(8,128)(2,1)S(1)} %collective-permute-done.8.refs_4_), channel_id=1, source_target_pairs={{0,4},{4,0},{1,5},{5,1},{2,6},{6,2},{3,7},{7,3},{8,12},{12,8},{9,1... | collective-permute-start | bytes 786440 | tf_op jit(solution)/shard_map/ppermute | solution.py:238
  81.3 18.3 %collective-permute-start.30 = (bf16[4,3,4,64,128]{4,3,2,1,0:T(8,128)(2,1)S(1)}, bf16[4,3,4,64,128]{4,3,2,1,0:T(8,128)(2,1)S(1)}, u32[]{:S(2)}, u32[]{:S(2)}) collective-permute-start(bf16[4,3,4,64,128]{4,3,2,1,0:T(8,128)(2,1)S(1)} %pad_maximum_fusion.refs_1_), channel_id=1, source_target_pairs={{0,4},{4,0},{1,5},{5,1},{2,6},{6,2},{3,7},{7,3},{8,12},{12,8},{9,1... | collective-permute-start | bytes 2359304 | tf_op jit(solution)/shard_map/ppermute | solution.py:238
  81.8 11.1 %collective-permute-start.29 = (bf16[2,3,4,64,128]{4,3,2,1,0:T(8,128)(2,1)S(1)}, bf16[2,3,4,64,128]{4,3,2,1,0:T(8,128)(2,1)S(1)}, u32[]{:S(2)}, u32[]{:S(2)}) collective-permute-start(bf16[2,3,4,64,128]{4,3,2,1,0:T(8,128)(2,1)S(1)} %slice.19), channel_id=1, source_target_pairs={{0,24},{8,0},{16,8},{24,16},{1,25},{9,1},{17,9},{25,17},{2,26},{10... | collective-permute-start | bytes 1179656 | tf_op jit(solution)/shard_map/ppermute | solution.py:233
  83.6 12.0 %collective-permute-start.28 = (bf16[2,3,4,64,128]{4,3,2,1,0:T(8,128)(2,1)S(1)}, bf16[2,3,4,64,128]{4,3,2,1,0:T(8,128)(2,1)S(1)}, u32[]{:S(2)}, u32[]{:S(2)}) collective-permute-start(bf16[2,3,4,64,128]{4,3,2,1,0:T(8,128)(2,1)S(1)} %slice.18), channel_id=1, source_target_pairs={{0,8},{8,16},{16,24},{24,0},{1,9},{9,17},{17,25},{25,1},{2,10},{10... | collective-permute-start | bytes 1179656 | tf_op jit(solution)/shard_map/ppermute | solution.py:232
  83.9 18.0 %collective-permute-start.32 = (bf16[4,3,4,64,128]{4,3,2,1,0:T(8,128)(2,1)S(1)}, bf16[4,3,4,64,128]{4,3,2,1,0:T(8,128)(2,1)S(1)}, u32[]{:S(2)}, u32[]{:S(2)}) collective-permute-start(bf16[4,3,4,64,128]{4,3,2,1,0:T(8,128)(2,1)S(1)} %collective-permute-done.27.refs_3_), channel_id=1, source_target_pairs={{0,4},{4,0},{1,5},{5,1},{2,6},{6,2},{3,7},{7,3},{8,12},{12,8},{9,1... | collective-permute-start | bytes 2359304 | tf_op jit(solution)/shard_map/ppermute | solution.py:238
  83.9 18.0 %collective-permute-start.31 = (bf16[4,3,4,64,128]{4,3,2,1,0:T(8,128)(2,1)S(1)}, bf16[4,3,4,64,128]{4,3,2,1,0:T(8,128)(2,1)S(1)}, u32[]{:S(2)}, u32[]{:S(2)}) collective-permute-start(bf16[4,3,4,64,128]{4,3,2,1,0:T(8,128)(2,1)S(1)} %collective-permute-done.26.refs_2_), channel_id=1, source_target_pairs={{0,4},{4,0},{1,5},{5,1},{2,6},{6,2},{3,7},{7,3},{8,12},{12,8},{9,1... | collective-permute-start | bytes 2359304 | tf_op jit(solution)/shard_map/ppermute | solution.py:238
  92.9 9.0 %collective-permute-start.34 = (bf16[2,3,4,64,128]{4,3,2,1,0:T(8,128)(2,1)S(1)}, bf16[2,3,4,64,128]{4,3,2,1,0:T(8,128)(2,1)S(1)}, u32[]{:S(2)}, u32[]{:S(2)}) collective-permute-start(bf16[2,3,4,64,128]{4,3,2,1,0:T(8,128)(2,1)S(1)} %collective-permute-done.29.refs_5_), channel_id=1, source_target_pairs={{0,4},{4,0},{1,5},{5,1},{2,6},{6,2},{3,7},{7,3},{8,12},{12,8},{9,1... | collective-permute-start | bytes 1179656 | tf_op jit(solution)/shard_map/ppermute | solution.py:238
  95.6 6.3 %collective-permute-start.33 = (bf16[2,3,4,64,128]{4,3,2,1,0:T(8,128)(2,1)S(1)}, bf16[2,3,4,64,128]{4,3,2,1,0:T(8,128)(2,1)S(1)}, u32[]{:S(2)}, u32[]{:S(2)}) collective-permute-start(bf16[2,3,4,64,128]{4,3,2,1,0:T(8,128)(2,1)S(1)} %collective-permute-done.28.refs_4_), channel_id=1, source_target_pairs={{0,4},{4,0},{1,5},{5,1},{2,6},{6,2},{3,7},{7,3},{8,12},{12,8},{9,1... | collective-permute-start | bytes 1179656 | tf_op jit(solution)/shard_map/ppermute | solution.py:238
  99.6 9.6 %collective-permute-start.16 = (bf16[2,544,128]{2,1,0:T(8,128)(2,1)S(1)}, bf16[2,544,128]{2,1,0:T(8,128)(2,1)S(1)}, u32[]{:S(2)}, u32[]{:S(2)}) collective-permute-start(bf16[2,544,128]{2,1,0:T(8,128)(2,1)S(1)} %far_rows.2), channel_id=1, source_target_pairs={{0,32},{32,0},{1,33},{33,1},{2,34},{34,2},{3,35},{35,3},{4,36},{36... | collective-permute-start | bytes 835592 | tf_op jit(solution)/shard_map/ppermute | solution.py:261
  107.9 11.9 %collective-permute-start.36 = (bf16[3,544,128]{2,1,0:T(8,128)(2,1)S(1)}, bf16[3,544,128]{2,1,0:T(8,128)(2,1)S(1)}, u32[]{:S(2)}, u32[]{:S(2)}) collective-permute-start(bf16[3,544,128]{2,1,0:T(8,128)(2,1)S(1)} %far_rows.3), channel_id=1, source_target_pairs={{0,32},{32,0},{1,33},{33,1},{2,34},{34,2},{3,35},{35,3},{4,36},{36... | collective-permute-start | bytes 1253384 | tf_op jit(solution)/shard_map/ppermute | solution.py:261
  113.0 19.4 %collective-permute-start.17 = (bf16[2,2,64,128]{3,2,1,0:T(8,128)(2,1)S(1)}, bf16[2,2,64,128]{3,2,1,0:T(8,128)(2,1)S(1)}, u32[]{:S(2)}, u32[]{:S(2)}) collective-permute-start(bf16[2,2,64,128]{3,2,1,0:T(8,128)(2,1)S(1)} %get-tuple-element.35), channel_id=1, source_target_pairs={{0,35},{32,1},{1,32},{33,2},{2,33},{34,3},{3,34},{35,0},{4,39},{36... | collective-permute-start | bytes 196616 | tf_op jit(solution)/shard_map/ppermute | solution.py:263
  125.4 16.8 %collective-permute-start.37 = (bf16[3,2,64,128]{3,2,1,0:T(8,128)(2,1)S(1)}, bf16[3,2,64,128]{3,2,1,0:T(8,128)(2,1)S(1)}, u32[]{:S(2)}, u32[]{:S(2)}) collective-permute-start(bf16[3,2,64,128]{3,2,1,0:T(8,128)(2,1)S(1)} %get-tuple-element.47), channel_id=1, source_target_pairs={{0,35},{32,1},{1,32},{33,2},{2,33},{34,3},{3,34},{35,0},{4,39},{36... | collective-permute-start | bytes 294920 | tf_op jit(solution)/shard_map/ppermute | solution.py:263
  126.5 15.7 %collective-permute-start.38 = (bf16[3,2,64,128]{3,2,1,0:T(8,128)(2,1)S(1)}, bf16[3,2,64,128]{3,2,1,0:T(8,128)(2,1)S(1)}, u32[]{:S(2)}, u32[]{:S(2)}) collective-permute-start(bf16[3,2,64,128]{3,2,1,0:T(8,128)(2,1)S(1)} %get-tuple-element.48), channel_id=1, source_target_pairs={{0,3},{32,33},{1,0},{33,34},{2,1},{34,35},{3,2},{35,32},{4,7},{36,... | collective-permute-start | bytes 294920 | tf_op jit(solution)/shard_map/ppermute | solution.py:263
  129.8 12.5 %collective-permute-start.39 = (bf16[3,2,64,128]{3,2,1,0:T(8,128)(2,1)S(1)}, bf16[3,2,64,128]{3,2,1,0:T(8,128)(2,1)S(1)}, u32[]{:S(2)}, u32[]{:S(2)}) collective-permute-start(bf16[3,2,64,128]{3,2,1,0:T(8,128)(2,1)S(1)} %get-tuple-element.49), channel_id=1, source_target_pairs={{0,34},{32,2},{1,35},{33,3},{2,32},{34,0},{3,33},{35,1},{4,38},{36... | collective-permute-start | bytes 294920 | tf_op jit(solution)/shard_map/ppermute | solution.py:263
  131.1 9.7 %collective-permute-start.18 = (bf16[2,2,64,128]{3,2,1,0:T(8,128)(2,1)S(1)}, bf16[2,2,64,128]{3,2,1,0:T(8,128)(2,1)S(1)}, u32[]{:S(2)}, u32[]{:S(2)}) collective-permute-start(bf16[2,2,64,128]{3,2,1,0:T(8,128)(2,1)S(1)} %get-tuple-element.36), channel_id=1, source_target_pairs={{0,3},{32,33},{1,0},{33,34},{2,1},{34,35},{3,2},{35,32},{4,7},{36,... | collective-permute-start | bytes 196616 | tf_op jit(solution)/shard_map/ppermute | solution.py:263
  132.4 9.8 %collective-permute-start.19 = (bf16[2,2,64,128]{3,2,1,0:T(8,128)(2,1)S(1)}, bf16[2,2,64,128]{3,2,1,0:T(8,128)(2,1)S(1)}, u32[]{:S(2)}, u32[]{:S(2)}) collective-permute-start(bf16[2,2,64,128]{3,2,1,0:T(8,128)(2,1)S(1)} %get-tuple-element.37), channel_id=1, source_target_pairs={{0,34},{32,2},{1,35},{33,3},{2,32},{34,0},{3,33},{35,1},{4,38},{36... | collective-permute-start | bytes 196616 | tf_op jit(solution)/shard_map/ppermute | solution.py:263

commit v2 on v1

v2 whole, which is shorter than its diff:
```python
import functools

import jax
import jax.numpy as jnp
from jax import lax
from jax.experimental import pallas as pl
from jax.experimental.pallas import tpu as pltpu
from jax.sharding import Mesh
from jax.sharding import PartitionSpec as P

HEAD_DIM = 128
HEADS_HERE = 5
GROUPS = 4
ROWS = 64
KV_BLOCKS, Q_BLOCKS = 4 * HEADS_HERE, 2 * HEADS_HERE
AXES = ("clip", "zlo", "x", "core", "zhi")
Z = ("zlo", "zhi")
SCALE = HEAD_DIM**-0.5
LOG2E = 1.4426950408889634
CHUNKS = ((0, 2), (2, 5))
VMEM = 40 * 1024 * 1024
ORDER = (("far", 0), ("far", 1), ("near", 0), ("near", 1))


def z_index(z):
    return (z % 2) * 4 + z // 2


def z_perm(even, odd):
    return [(z_index(z), z_index((z + (odd if z % 2 else even)) % 8)) for z in range(8)]


TO = (z_perm(-1, 1), z_perm(2, -2), z_perm(-3, 3))
BACK = (z_perm(-1, 1), z_perm(-2, 2), z_perm(-3, 3))
PAIR = z_perm(1, -1)
SWAP = [(0, 1), (1, 0)]
AROUND_X = [[(i, (i + k) % 4) for i in range(4)] for k in (1, 3, 2)]


def spec(shape, index_map=None):
    return pl.BlockSpec(shape, index_map) if index_map else pl.BlockSpec(memory_space=pltpu.VMEM)


def pack_body(offs, *refs):
    sources, outs, held, sems = refs[:6], refs[6:-7], refs[-7:-1], refs[-1]
    copies = [pltpu.make_async_copy(a, b, sems.at[i]) for i, (a, b) in enumerate(zip(sources, held))]
    for copy in copies:
        copy.start()
    for a in range(6):
        copies[a].wait()
        for slot in range(4):
            for h in range(HEADS_HERE):
                col = pl.multiple_of(offs[slot] + h * HEAD_DIM, HEAD_DIM)
                block = held[a][:, pl.ds(col, HEAD_DIM)]
                if a < 4:
                    outs[slot][h * 4 + a] = block
                elif slot == 1:
                    outs[slot][KV_BLOCKS + h * 2 + a - 4] = block
                else:
                    outs[4 + slot // 2 + slot // 3][h * 2 + a - 4] = block


def pack(offs, arrays):
    block = lambda count: jax.ShapeDtypeStruct((count, ROWS, HEAD_DIM), jnp.bfloat16)
    return pl.pallas_call(
        pack_body,
        out_shape=[block(KV_BLOCKS), block(KV_BLOCKS + Q_BLOCKS)]
        + [block(KV_BLOCKS)] * 2
        + [block(Q_BLOCKS)] * 3,
        in_specs=[pl.BlockSpec(memory_space=pltpu.SMEM)] + [pl.BlockSpec(memory_space=pl.ANY)] * 6,
        out_specs=[spec(None)] * 7,
        scratch_shapes=[pltpu.VMEM(arrays[0].shape, jnp.bfloat16)] * 6
        + [pltpu.SemaphoreType.DMA((6,))],
        compiler_params=pltpu.CompilerParams(vmem_limit_bytes=60 * 1024 * 1024),
        name="pack",
    )(offs, *arrays)


def unpack_body(chunk, offs, *refs):
    low, high = CHUNKS[chunk]
    pieces, before, (out, out_tan) = refs[:4], refs[4:-2], refs[-2:]
    if before:
        out[...] = before[0][...]
        out_tan[...] = before[1][...]
    for slot, ref in enumerate(pieces):
        for h in range(low, high):
            col = pl.multiple_of(offs[slot] + h * HEAD_DIM, HEAD_DIM)
            out[:, pl.ds(col, HEAD_DIM)] = ref[h - low, 0]
            out_tan[:, pl.ds(col, HEAD_DIM)] = ref[h - low, 1]


def unpack(chunk, offs, pieces, before):
    shape = jax.ShapeDtypeStruct((ROWS, GROUPS * HEADS_HERE * HEAD_DIM), jnp.bfloat16)
    return pl.pallas_call(
        functools.partial(unpack_body, chunk),
        out_shape=[shape, shape],
        in_specs=[pl.BlockSpec(memory_space=pltpu.SMEM)] + [spec(None)] * (4 + len(before)),
        out_specs=[spec(None)] * 2,
        compiler_params=pltpu.CompilerParams(vmem_limit_bytes=VMEM),
        name="unpack",
    )(offs, *pieces, *before)


def fold(block):
    return block.reshape(block.shape[0] * block.shape[1], block.shape[2])


def core_part(q_ref, kv_refs, kk, vv):
    row = 0
    for ref in kv_refs:
        rows = pl.ds(row, ROWS)
        row += ROWS
        kk[rows, :HEAD_DIM] = ref[0]
        kk[rows, HEAD_DIM:] = ref[2]
        vv[rows, :HEAD_DIM] = ref[1]
        vv[rows, HEAD_DIM:] = ref[3]
    q, dq = fold(q_ref[:, 0]), fold(q_ref[:, 1])
    nt = (((1,), (1,)), ((), ()))
    dot = functools.partial(lax.dot_general, preferred_element_type=jnp.float32)
    s = dot(q, kk[:, :HEAD_DIM], nt)
    st = dot(jnp.concatenate([dq, q], axis=1), kk[...], nt)
    m = jnp.max(s, axis=1, keepdims=True)
    p = jnp.exp2((s - m) * (SCALE * LOG2E))
    t = p * st
    total = jnp.sum(p, axis=1, keepdims=True)
    slope = jnp.sum(t, axis=1, keepdims=True)
    nn = (((1,), (0,)), ((), ()))
    pv = dot(p.astype(jnp.bfloat16), vv[...], nn)
    tv = dot(t.astype(jnp.bfloat16), vv[:, :HEAD_DIM], nn)
    inverse = 1.0 / total
    att = pv[:, :HEAD_DIM] * inverse
    slope = slope * (inverse * SCALE)
    tan = (pv[:, HEAD_DIM:] + tv * SCALE) * inverse - att * slope
    return att, tan, m * SCALE + jnp.log(total), slope


def three(value):
    high = value.astype(jnp.bfloat16).astype(jnp.float32)
    rest = value - high
    middle = rest.astype(jnp.bfloat16).astype(jnp.float32)
    return high, middle, rest - middle


def far_body(count, *refs):
    q_ref, kv_refs, (out, kk, vv) = refs[0], refs[1 : 1 + count], refs[1 + count :]
    att, tan, lse, slope = core_part(q_ref, kv_refs, kk, vv)
    n = att.shape[0]
    out[0, :n] = att.astype(jnp.bfloat16)
    out[0, n : 2 * n] = tan.astype(jnp.bfloat16)
    lane = lax.broadcasted_iota(jnp.int32, (n, HEAD_DIM), 1)
    stats = jnp.zeros((n, HEAD_DIM), jnp.float32)
    for i, column in enumerate(three(lse) + three(slope)):
        stats = jnp.where(lane == i, column, stats)
    flat = jnp.transpose(stats)[:16].astype(jnp.bfloat16)
    out[0, 2 * n : 2 * n + 16] = flat[:, :HEAD_DIM]
    out[0, 2 * n + 16 :] = flat[:, HEAD_DIM:]


def near_body(count, *refs):
    q_ref, kv_refs, got = refs[0], refs[1 : 1 + count], refs[1 + count]
    outs, (kk, vv) = refs[2 + count : 6 + count], refs[6 + count :]
    att, tan, lse, slope = core_part(q_ref, kv_refs, kk, vv)
    n = att.shape[0]
    att2 = got[0, :n].astype(jnp.float32)
    tan2 = got[0, n : 2 * n].astype(jnp.float32)
    flat = jnp.concatenate([got[0, 2 * n : 2 * n + 16], got[0, 2 * n + 16 :]], axis=1)
    flat = flat.astype(jnp.float32)

    def column(i):
        line = flat[i : i + 1] + flat[i + 1 : i + 2] + flat[i + 2 : i + 3]
        return jnp.transpose(jnp.broadcast_to(line, (HEAD_DIM, n)))

    lse2, slope2 = column(0), column(3)
    w1 = 1.0 / (1.0 + jnp.exp(lse2 - lse))
    w2 = 1.0 / (1.0 + jnp.exp(lse - lse2))
    tan = w1 * tan + w2 * tan2 + (w1 * w2) * (slope - slope2) * (att - att2)
    att = w1 * att + w2 * att2
    for slot in range(4):
        rows = slice(slot * ROWS, (slot + 1) * ROWS)
        outs[slot][0, 0] = att[rows].astype(jnp.bfloat16)
        outs[slot][0, 1] = tan[rows].astype(jnp.bfloat16)


def attend(q, pieces, low, high, got=None):
    heads = high - low
    keys = len(pieces) * ROWS
    rows = 4 * ROWS
    in_specs = [pl.BlockSpec((4, 2, ROWS, HEAD_DIM), lambda h: (0, h + low, 0, 0))]
    for _, i in pieces:
        in_specs.append(
            pl.BlockSpec((4, ROWS, HEAD_DIM), lambda h, i=i: (h + low + i * HEADS_HERE, 0, 0))
        )
    args = [q] + [p for p, _ in pieces]
    wide = 2 * rows + 32
    if got is None:
        body = functools.partial(far_body, len(pieces))
        out_shape = jax.ShapeDtypeStruct((heads, wide, HEAD_DIM), jnp.bfloat16)
        out_specs = pl.BlockSpec((1, wide, HEAD_DIM), lambda h: (h, 0, 0))
    else:
        body = functools.partial(near_body, len(pieces))
        args.append(got)
        in_specs.append(pl.BlockSpec((1, wide, HEAD_DIM), lambda h: (h, 0, 0)))
        out_shape = [jax.ShapeDtypeStruct((heads, 2, ROWS, HEAD_DIM), jnp.bfloat16)] * 4
        out_specs = [pl.BlockSpec((1, 2, ROWS, HEAD_DIM), lambda h: (h, 0, 0, 0))] * 4
    return pl.pallas_call(
        body,
        grid=(heads,),
        out_shape=out_shape,
        in_specs=in_specs,
        out_specs=out_specs,
        scratch_shapes=[pltpu.VMEM((keys, 2 * HEAD_DIM), jnp.bfloat16)] * 2,
        compiler_params=pltpu.CompilerParams(vmem_limit_bytes=VMEM),
        cost_estimate=pl.CostEstimate(
            flops=16 * heads * rows * keys * HEAD_DIM,
            bytes_accessed=heads * keys * 4 * HEAD_DIM * 2,
            transcendentals=heads * rows * keys,
        ),
        name="far_rows" if got is None else "near_rows",
    )(*args)


def after(value, *needed):
    return lax.optimization_barrier((value, *needed))[0]


def per_device(query_rows, key_rows, value_rows, query_tan, key_tan, value_tan):
    group, parity = lax.axis_index("zhi"), lax.axis_index("zlo")
    step = 2 * parity - 1
    slots = jnp.stack([group, group + step, group - step, group + 2]) % GROUPS
    offs = (slots * (HEADS_HERE * HEAD_DIM)).astype(jnp.int32)
    own, to_one, to_two, to_three, own_q, to_two_q, to_three_q = pack(
        offs, (key_rows, value_rows, key_tan, value_tan, query_rows, query_tan)
    )
    around = lambda array: [lax.ppermute(array, "x", perm) for perm in AROUND_X]
    swap = lambda arrays: [lax.ppermute(a, "core", SWAP) for a in arrays]
    one = lax.ppermute(to_one, Z, TO[0])
    two_q = lax.ppermute(to_two_q, Z, TO[1])
    own_x = around(own)
    one, two_q, own, own_x, to_two, to_three_q, to_three = lax.optimization_barrier(
        (one, two_q, own, own_x, to_two, to_three_q, to_three)
    )
    one, one_q = one[:KV_BLOCKS], one[KV_BLOCKS:]
    two = lax.ppermute(to_two, Z, TO[1])
    three_q = lax.ppermute(to_three_q, Z, TO[2])
    one_x = around(one)
    two, three_q, one, one_x, own, own_x, to_three = lax.optimization_barrier(
        (two, three_q, one, one_x, own, own_x, to_three)
    )
    three_ = lax.ppermute(to_three, Z, TO[2])
    two_x = around(two)
    own_s = lax.ppermute(jnp.concatenate([own, *own_x]), "core", SWAP)
    near_q = jnp.stack([own_q, one_q, two_q, three_q])
    three_, two, two_x, one, one_x, own_s, near_q = lax.optimization_barrier(
        (three_, two, two_x, one, one_x, own_s, near_q)
    )
    three_x = around(three_)
    far_q = lax.ppermute(near_q, Z, PAIR)
    both_s = lax.ppermute(jnp.concatenate([one, *one_x, two, *two_x]), "core", SWAP)
    three_, three_x, both_s, far_q = lax.optimization_barrier((three_, three_x, both_s, far_q))
    three_s = swap([three_, *three_x])
    pieces = [(p, 0) for p in (own, *own_x, one, *one_x, two, *two_x, three_, *three_x, *three_s)]
    pieces += [(own_s, i) for i in range(4)] + [(both_s, i) for i in range(8)]
    sent, got, result, last, back = {}, {}, (), (), []
    for kind, c in ORDER:
        low, high = CHUNKS[c]
        if kind == "far":
            sent[c] = attend(after(far_q, *last), pieces, low, high)
            got[c] = lax.ppermute(sent[c], Z, PAIR)
            last = (sent[c],)
        else:
            near = attend(after(near_q, *last), pieces, low, high, got[c])
            if back:
                result = unpack(c - 1, offs, [after(back[0], *near), *back[1:]], result)
            back = [near[0]]
            back += [lax.ppermute(after(o, *result), Z, perm) for o, perm in zip(near[1:], BACK)]
            last = (near[0],)
    return tuple(unpack(len(CHUNKS) - 1, offs, back, result))


def solution(mesh):
    fine = Mesh(mesh.devices.reshape(4, 2, 4, 2, 4), AXES)
    rows = P(AXES, None)
    return jax.shard_map(
        per_device,
        mesh=fine,
        in_specs=(rows,) * 6,
        out_specs=(rows, rows),
        check_vma=False,
    )
```

time: 146 us -> 140 us (0.959)
  starting transfers between devices: 61.8 us -> 45.2 us
  waiting for transfers between devices: 53.1 us -> 66.4 us
  local copies, waits for them, and re-layouts: 5.92 us -> 0.39 us
  Pallas kernels: 21.8 us -> 23.7 us
  other arithmetic: 0.34 us -> 1.85 us
    ppermute x40 -> x32, starting transfers between devices: 61.8 us -> 45.2 us  [the longest x12 18 us: per_device(): around = lambda array: [lax.ppermute(array, 'x', perm) for perm in AROUND_X]]
    ppermute x40 -> x32, waiting for transfers between devices: 53.1 us -> 66.4 us  [the longest x12 19.5 us: per_device(): around = lambda array: [lax.ppermute(array, 'x', perm) for perm in AROUND_X]]
    unnamed x12 -> x15, local copies, waits for them, and re-layouts: 5.83 us -> 0.31 us
    pallas_call x2 -> x3, Pallas kernels: 2.4 us -> 5.5 us  [the longest x1 3.42 us: pack(): pl.pallas_call(pack_body, out_shape=[block(KV_BLOCKS), block(KV_BLOCKS +...]
  transfers between devices with their start and end apart: 40 -> 32, of which waited for: 13 -> 15; matrix products, arithmetic and copies ran while one was open for 0% -> 0% of each run, Pallas kernels for 13% -> 10%
where the time goes in v2:
time: 140 us; the launch traced here: 138 us
  waiting for transfers between devices  66.4 us (47%)
  starting transfers between devices  45.2 us (32%)
  Pallas kernels  23.7 us (17%)
  other arithmetic  1.85 us (1%)
    ppermute x12, waiting for transfers between devices, per_device(): around = lambda array: [lax.ppermute(array, 'x', perm) for perm in AROUND_X]  19.5 us
    pallas_call x4, Pallas kernels, attend(): pl.pallas_call(body, grid=(heads,), out_shape=out_shape, in_specs=in_spec...  18.2 us
    ppermute x12, starting transfers between devices, per_device(): around = lambda array: [lax.ppermute(array, 'x', perm) for perm in AROUND_X]  18 us
    ppermute x1, waiting for transfers between devices, per_device(): three_ = lax.ppermute(to_three, Z, TO[2])  16.8 us
    ppermute x1, waiting for transfers between devices, per_device(): three_q = lax.ppermute(to_three_q, Z, TO[2])  14.4 us
    ppermute x6, starting transfers between devices, per_device(): lax.ppermute(after(o, *result), Z, perm)  11.5 us
    ppermute x6, waiting for transfers between devices, per_device(): lax.ppermute(after(o, *result), Z, perm)  5.96 us
    ppermute x1, waiting for transfers between devices, per_device(): two_q = lax.ppermute(to_two_q, Z, TO[1])  4.47 us
  transfers between devices with their start and end apart: 32, of which 15 were waited for; matrix products, arithmetic and copies ran while one was open for 0% of the time, Pallas kernels for 10%

profile of v2, /device:TPU:40, one launch (start us, length us, event | category | flops | bytes accessed | tf_op | source)
XLA Modules:
  0.0 138.4 jit_solution(12760797298193555220)
XLA Ops:
  0.6 0.6 fusion.offs
  1.3 3.4 %pack.1 = (bf16[20,64,128]{2,1,0:T(8,128)(2,1)}, bf16[30,64,128]{2,1,0:T(8,128)(2,1)}, bf16[20,64,128]{2,1,0:T(8,128)(2,1)}, bf16[20,64,128]{2,1,0:T(8,128)(2,1)...) custom-call(s32[4]{0:T(128)} %fusion.offs, bf16[64,2560]{1,0:T(8,128)(2,1)} %refs_0_.1, ...), custom_call_target="tpu_custom_call" | custom-call | tf_op jit(solution)/shard_map/pack/pallas_call | solution.py:65
  4.7 2.0 %collective-permute-start = (bf16[30,64,128]{2,1,0:T(8,128)(2,1)}, bf16[30,64,128]{2,1,0:T(8,128)(2,1)S(1)}, u32[]{:S(2)}, u32[]{:S(2)}) collective-permute-start(bf16[30,64,128]{2,1,0:T(8,128)(2,1)} %get-tuple-element.63), channel_id=1, source_target_pairs={{0,35},{32,1},{1,32},{33,2},{2,33},{34,3},{3,34},{35,0},{4,39},{36... | collective-permute-start | bytes 1474568 | tf_op jit(solution)/shard_map/ppermute | solution.py:236
  6.7 1.5 %collective-permute-start.2 = (bf16[20,64,128]{2,1,0:T(8,128)(2,1)}, bf16[20,64,128]{2,1,0:T(8,128)(2,1)S(1)}, u32[]{:S(2)}, u32[]{:S(2)}) collective-permute-start(bf16[20,64,128]{2,1,0:T(8,128)(2,1)} %get-tuple-element.83.refs_1_), channel_id=1, source_target_pairs={{0,8},{8,16},{16,24},{24,0},{1,9},{9,17},{17,25},{25,1},{2,10},{10... | collective-permute-start | bytes 983048 | tf_op jit(solution)/shard_map/ppermute | solution.py:234
  8.2 1.7 %collective-permute-start.3 = (bf16[20,64,128]{2,1,0:T(8,128)(2,1)}, bf16[20,64,128]{2,1,0:T(8,128)(2,1)S(1)}, u32[]{:S(2)}, u32[]{:S(2)}) collective-permute-start(bf16[20,64,128]{2,1,0:T(8,128)(2,1)} %get-tuple-element.83.refs_1_), channel_id=1, source_target_pairs={{0,24},{8,0},{16,8},{24,16},{1,25},{9,1},{17,9},{25,17},{2,26},{10... | collective-permute-start | bytes 983048 | tf_op jit(solution)/shard_map/ppermute | solution.py:234
  10.0 1.8 %collective-permute-start.4 = (bf16[20,64,128]{2,1,0:T(8,128)(2,1)}, bf16[20,64,128]{2,1,0:T(8,128)(2,1)S(1)}, u32[]{:S(2)}, u32[]{:S(2)}) collective-permute-start(bf16[20,64,128]{2,1,0:T(8,128)(2,1)} %get-tuple-element.83.refs_1_), channel_id=1, source_target_pairs={{0,16},{8,24},{16,0},{24,8},{1,17},{9,25},{17,1},{25,9},{2,18},{10... | collective-permute-start | bytes 983048 | tf_op jit(solution)/shard_map/ppermute | solution.py:234
  11.8 3.6 %collective-permute-start.1 = (bf16[10,64,128]{2,1,0:T(8,128)(2,1)}, bf16[10,64,128]{2,1,0:T(8,128)(2,1)S(1)}, u32[]{:S(2)}, u32[]{:S(2)}) collective-permute-start(bf16[10,64,128]{2,1,0:T(8,128)(2,1)} %get-tuple-element.64), channel_id=1, source_target_pairs={{0,1},{32,35},{1,2},{33,32},{2,3},{34,33},{3,0},{35,34},{4,5},{36,... | collective-permute-start | bytes 491528 | tf_op jit(solution)/shard_map/ppermute | solution.py:237
  15.3 4.5 %collective-permute-done.1 = bf16[10,64,128]{2,1,0:T(8,128)(2,1)S(1)} collective-permute-done((bf16[10,64,128]{2,1,0:T(8,128)(2,1)}, bf16[10,64,128]{2,1,0:T(8,128)(2,1)S(1)}, u32[]{:S(2)}, u32[]{:S(2)}) %collective-permute-start.1) | collective-permute-done | bytes 163872 | tf_op jit(solution)/shard_map/ppermute | solution.py:237
  19.8 3.9 %collective-permute-done.3.refs_3_ = bf16[20,64,128]{2,1,0:T(8,128)(2,1)S(1)} collective-permute-done((bf16[20,64,128]{2,1,0:T(8,128)(2,1)}, bf16[20,64,128]{2,1,0:T(8,128)(2,1)S(1)}, u32[]{:S(2)}, u32[]{:S(2)}) %collective-permute-start.3) | collective-permute-done | bytes 327712 | tf_op jit(solution)/shard_map/ppermute | solution.py:234
  23.7 1.6 %collective-permute-done.4.refs_4_ = bf16[20,64,128]{2,1,0:T(8,128)(2,1)S(1)} collective-permute-done((bf16[20,64,128]{2,1,0:T(8,128)(2,1)}, bf16[20,64,128]{2,1,0:T(8,128)(2,1)S(1)}, u32[]{:S(2)}, u32[]{:S(2)}) %collective-permute-start.4) | collective-permute-done | bytes 327712 | tf_op jit(solution)/shard_map/ppermute | solution.py:234
  25.3 1.2 collective-permute-start.7
  26.6 2.1 %collective-permute-start.8 = (bf16[20,64,128]{2,1,0:T(8,128)(2,1)S(1)}, bf16[20,64,128]{2,1,0:T(8,128)(2,1)S(1)}, u32[]{:S(2)}, u32[]{:S(2)}) collective-permute-start(bf16[20,64,128]{2,1,0:T(8,128)(2,1)S(1)} %slice.6.refs_5_), channel_id=1, source_target_pairs={{0,24},{8,0},{16,8},{24,16},{1,25},{9,1},{17,9},{25,17},{2,26},{10... | collective-permute-start | bytes 983048 | tf_op jit(solution)/shard_map/ppermute | solution.py:234
  28.9 4.4 %collective-permute-start.5 = (bf16[20,64,128]{2,1,0:T(8,128)(2,1)}, bf16[20,64,128]{2,1,0:T(8,128)(2,1)S(1)}, u32[]{:S(2)}, u32[]{:S(2)}) collective-permute-start(bf16[20,64,128]{2,1,0:T(8,128)(2,1)} %get-tuple-element.69), channel_id=1, source_target_pairs={{0,1},{32,35},{1,2},{33,32},{2,3},{34,33},{3,0},{35,34},{4,5},{36,... | collective-permute-start | bytes 983048 | tf_op jit(solution)/shard_map/ppermute | solution.py:243
  33.2 2.0 %collective-permute-start.6 = (bf16[10,64,128]{2,1,0:T(8,128)(2,1)}, bf16[10,64,128]{2,1,0:T(8,128)(2,1)S(1)}, u32[]{:S(2)}, u32[]{:S(2)}) collective-permute-start(bf16[10,64,128]{2,1,0:T(8,128)(2,1)} %get-tuple-element.70), channel_id=1, source_target_pairs={{0,34},{32,2},{1,35},{33,3},{2,32},{34,0},{3,33},{35,1},{4,38},{36... | collective-permute-start | bytes 491528 | tf_op jit(solution)/shard_map/ppermute | solution.py:244
  35.3 14.4 %collective-permute-done.6 = bf16[10,64,128]{2,1,0:T(8,128)(2,1)S(1)} collective-permute-done((bf16[10,64,128]{2,1,0:T(8,128)(2,1)}, bf16[10,64,128]{2,1,0:T(8,128)(2,1)S(1)}, u32[]{:S(2)}, u32[]{:S(2)}) %collective-permute-start.6) | collective-permute-done | bytes 163872 | tf_op jit(solution)/shard_map/ppermute | solution.py:244
  49.6 1.1 pad_maximum_fusion
  50.9 0.9 collective-permute-start.11
  51.8 2.4 %collective-permute-start.12 = (bf16[20,64,128]{2,1,0:T(8,128)(2,1)S(1)}, bf16[20,64,128]{2,1,0:T(8,128)(2,1)S(1)}, u32[]{:S(2)}, u32[]{:S(2)}) collective-permute-start(bf16[20,64,128]{2,1,0:T(8,128)(2,1)S(1)} %collective-permute-done.5.refs_9_), channel_id=1, source_target_pairs={{0,24},{8,0},{16,8},{24,16},{1,25},{9,1},{17,9},{25,17},{2,26},{10... | collective-permute-start | bytes 983048 | tf_op jit(solution)/shard_map/ppermute | solution.py:234
  54.2 2.0 %collective-permute-start.13 = (bf16[20,64,128]{2,1,0:T(8,128)(2,1)S(1)}, bf16[20,64,128]{2,1,0:T(8,128)(2,1)S(1)}, u32[]{:S(2)}, u32[]{:S(2)}) collective-permute-start(bf16[20,64,128]{2,1,0:T(8,128)(2,1)S(1)} %collective-permute-done.5.refs_9_), channel_id=1, source_target_pairs={{0,16},{8,24},{16,0},{24,8},{1,17},{9,25},{17,1},{25,9},{2,18},{10... | collective-permute-start | bytes 983048 | tf_op jit(solution)/shard_map/ppermute | solution.py:234
  56.4 16.8 %collective-permute-done.10.refs_13_ = bf16[20,64,128]{2,1,0:T(8,128)(2,1)S(1)} collective-permute-done((bf16[20,64,128]{2,1,0:T(8,128)(2,1)S(1)}, bf16[20,64,128]{2,1,0:T(8,128)(2,1)S(1)}, u32[]{:S(2)}, u32[]{:S(2)}) %collective-permute-start.10) | collective-permute-done | bytes 327712 | tf_op jit(solution)/shard_map/ppermute | solution.py:249
  74.1 3.2 %collective-permute-start.16 = (bf16[20,64,128]{2,1,0:T(8,128)(2,1)S(1)}, bf16[20,64,128]{2,1,0:T(8,128)(2,1)S(1)}, u32[]{:S(2)}, u32[]{:S(2)}) collective-permute-start(bf16[20,64,128]{2,1,0:T(8,128)(2,1)S(1)} %collective-permute-done.10.refs_13_), channel_id=1, source_target_pairs={{0,24},{8,0},{16,8},{24,16},{1,25},{9,1},{17,9},{25,17},{2,26},{10... | collective-permute-start | bytes 983048 | tf_op jit(solution)/shard_map/ppermute | solution.py:234
  77.3 0.8 collective-permute-start.17
  78.1 14.0 %collective-permute-done.15.refs_14_ = bf16[20,64,128]{2,1,0:T(8,128)(2,1)S(1)} collective-permute-done((bf16[20,64,128]{2,1,0:T(8,128)(2,1)S(1)}, bf16[20,64,128]{2,1,0:T(8,128)(2,1)S(1)}, u32[]{:S(2)}, u32[]{:S(2)}) %collective-permute-start.15) | collective-permute-done | bytes 327712 | tf_op jit(solution)/shard_map/ppermute | solution.py:234
  92.2 0.5 collective-permute-start.21
  92.8 0.4 collective-permute-start.23
  93.2 0.6 collective-permute-done.20.refs_17_
  93.8 0.5 collective-permute-done.21.refs_18_
  94.3 0.5 collective-permute-done.22.refs_19_
  94.8 0.5 collective-permute-done.23.refs_20_
  95.2 3.7 %far_rows.2 = bf16[2,544,128]{2,1,0:T(8,128)(2,1)S(1)} custom-call(bf16[4,10,64,128]{3,2,1,0:T(8,128)(2,1)S(1)} %collective-permute-done.19.refs_0_, bf16[20,64,128]{2,1,0:T(8,128)(2,1)S(1)} %copy-done, bf16[20,64,128]{2,1,0:T(8,128)(2,1)S(1)} %collective-permute-done.2.refs_2_, bf16[20,64,128]{2,1,0:T(8,128)(2,1)S(1)} %collective-permute-done.3.refs_3_, ...), custom_call_target="tpu_custom_call" | custom-call | flops 2147483648 | bytes 4194304 | tf_op jit(solution)/shard_map/far_rows/pallas_call | solution.py:205
  99.0 1.8 %collective-permute-start.24 = (bf16[2,544,128]{2,1,0:T(8,128)(2,1)S(1)}, bf16[2,544,128]{2,1,0:T(8,128)(2,1)S(1)}, u32[]{:S(2)}, u32[]{:S(2)}) collective-permute-start(bf16[2,544,128]{2,1,0:T(8,128)(2,1)S(1)} %far_rows.2), channel_id=1, source_target_pairs={{0,32},{32,0},{1,33},{33,1},{2,34},{34,2},{3,35},{35,3},{4,36},{36... | collective-permute-start | bytes 835592 | tf_op jit(solution)/shard_map/ppermute | solution.py:268
  100.8 5.6 %far_rows.3 = bf16[3,544,128]{2,1,0:T(8,128)(2,1)S(1)} custom-call(bf16[4,10,64,128]{3,2,1,0:T(8,128)(2,1)S(1)} %collective-permute-done.19.refs_0_, bf16[20,64,128]{2,1,0:T(8,128)(2,1)S(1)} %copy-done, bf16[20,64,128]{2,1,0:T(8,128)(2,1)S(1)} %collective-permute-done.2.refs_2_, bf16[20,64,128]{2,1,0:T(8,128)(2,1)S(1)} %collective-permute-done.3.refs_3_, ...), custom_call_target="tpu_custom_call" | custom-call | flops 3221225472 | bytes 6291456 | tf_op jit(solution)/shard_map/far_rows/pallas_call | solution.py:205
  106.4 0.4 collective-permute-start.25
  106.7 1.0 collective-permute-done.24.refs_33_
  107.8 3.6 %near_rows.2 = (bf16[2,2,64,128]{3,2,1,0:T(8,128)(2,1)S(1)}, bf16[2,2,64,128]{3,2,1,0:T(8,128)(2,1)S(1)}, bf16[2,2,64,128]{3,2,1,0:T(8,128)(2,1)S(1)}, bf16[2,2,64,128]{3,2,1,0:T(8,128)(2,1)S(1)}) custom-call(bf16[4,10,64,128]{3,2,1,0:T(8,128)(2,1)S(1)} %pad_maximum_fusion.1.refs_0_, bf16[20,64,128]{2,1,0:T(8,128)(2,1)S(1)} %copy-done, ...), custom_call_target="tpu_custom_call" | custom-call | flops 2147483648 | bytes 4194304 | tf_op jit(solution)/shard_map/near_rows/pallas_call | solution.py:205
  111.3 1.1 collective-permute-start.26
  112.5 3.9 %collective-permute-start.27 = (bf16[2,2,64,128]{3,2,1,0:T(8,128)(2,1)S(1)}, bf16[2,2,64,128]{3,2,1,0:T(8,128)(2,1)S(1)}, u32[]{:S(2)}, u32[]{:S(2)}) collective-permute-start(bf16[2,2,64,128]{3,2,1,0:T(8,128)(2,1)S(1)} %get-tuple-element.117), channel_id=1, source_target_pairs={{0,3},{32,33},{1,0},{33,34},{2,1},{34,35},{3,2},{35,32},{4,7},{36,... | collective-permute-start | bytes 196616 | tf_op jit(solution)/shard_map/ppermute | solution.py:275
  116.3 0.7 collective-permute-start.28
  117.0 2.3 %collective-permute-done.25.refs_33_ = bf16[3,544,128]{2,1,0:T(8,128)(2,1)S(1)} collective-permute-done((bf16[3,544,128]{2,1,0:T(8,128)(2,1)S(1)}, bf16[3,544,128]{2,1,0:T(8,128)(2,1)S(1)}, u32[]{:S(2)}, u32[]{:S(2)}) %collective-permute-start.25) | collective-permute-done | bytes 417824 | tf_op jit(solution)/shard_map/ppermute | solution.py:268
  119.3 5.3 %near_rows.3 = (bf16[3,2,64,128]{3,2,1,0:T(8,128)(2,1)S(1)}, bf16[3,2,64,128]{3,2,1,0:T(8,128)(2,1)S(1)}, bf16[3,2,64,128]{3,2,1,0:T(8,128)(2,1)S(1)}, bf16[3,2,64,128]{3,2,1,0:T(8,128)(2,1)S(1)}) custom-call(bf16[4,10,64,128]{3,2,1,0:T(8,128)(2,1)S(1)} %pad_maximum_fusion.1.refs_0_, bf16[20,64,128]{2,1,0:T(8,128)(2,1)S(1)} %copy-done, ...), custom_call_target="tpu_custom_call" | custom-call | flops 3221225472 | bytes 6291456 | tf_op jit(solution)/shard_map/near_rows/pallas_call | solution.py:205
  124.6 0.6 unpack.2
  125.2 3.8 %collective-permute-start.31 = (bf16[3,2,64,128]{3,2,1,0:T(8,128)(2,1)S(1)}, bf16[3,2,64,128]{3,2,1,0:T(8,128)(2,1)S(1)}, u32[]{:S(2)}, u32[]{:S(2)}) collective-permute-start(bf16[3,2,64,128]{3,2,1,0:T(8,128)(2,1)S(1)} %get-tuple-element.123), channel_id=1, source_target_pairs={{0,34},{32,2},{1,35},{33,3},{2,32},{34,0},{3,33},{35,1},{4,38},{36... | collective-permute-start | bytes 294920 | tf_op jit(solution)/shard_map/ppermute | solution.py:275
  129.1 0.9 collective-permute-start.30
  130.0 1.0 collective-permute-start.29
  131.0 3.6 %collective-permute-done.31.refs_3_ = bf16[3,2,64,128]{3,2,1,0:T(8,128)(2,1)S(1)} collective-permute-done((bf16[3,2,64,128]{3,2,1,0:T(8,128)(2,1)S(1)}, bf16[3,2,64,128]{3,2,1,0:T(8,128)(2,1)S(1)}, u32[]{:S(2)}, u32[]{:S(2)}) %collective-permute-start.31) | collective-permute-done | bytes 98336 | tf_op jit(solution)/shard_map/ppermute | solution.py:275
  134.6 2.1 %collective-permute-done.30.refs_2_ = bf16[3,2,64,128]{3,2,1,0:T(8,128)(2,1)S(1)} collective-permute-done((bf16[3,2,64,128]{3,2,1,0:T(8,128)(2,1)S(1)}, bf16[3,2,64,128]{3,2,1,0:T(8,128)(2,1)S(1)}, u32[]{:S(2)}, u32[]{:S(2)}) %collective-permute-start.30) | collective-permute-done | bytes 98336 | tf_op jit(solution)/shard_map/ppermute | solution.py:275
  136.6 0.3 collective-permute-done.29.refs_1_
  137.0 1.5 %unpack.3 = (bf16[64,2560]{1,0:T(8,128)(2,1)}, bf16[64,2560]{1,0:T(8,128)(2,1)}) custom-call(s32[4]{0:T(128)S(1)} %copy-done.1, bf16[3,2,64,128]{3,2,1,0:T(8,128)(2,1)S(1)} %get-tuple-element.111.refs_0_, bf16[3,2,64,128]{3,2,1,0:T(8,128)(2,1)S(1)} %collective-permute-done.29.refs_1_, bf16[3,2,64,128]{3,2,1,0:T(8,128)(2,1)S(1)} %collective-permute-done.30.refs_2_, ...), custom_call_target="tpu_custom_call" | custom-call | tf_op jit(solution)/shard_map/unpack/pallas_call | solution.py:94
  (44 shorter events, 1.5 us)
Async XLA Ops:
  4.7 51.6 %copy-start.3 = (bf16[20,64,128]{2,1,0:T(8,128)(2,1)S(1)}, bf16[20,64,128]{2,1,0:T(8,128)(2,1)}, u32[]{:S(2)}) copy-start(bf16[20,64,128]{2,1,0:T(8,128)(2,1)} %get-tuple-element.77) | copy-start | bytes 983044
  4.7 51.6 %copy-start.2 = (bf16[10,64,128]{2,1,0:T(8,128)(2,1)S(1)}, bf16[10,64,128]{2,1,0:T(8,128)(2,1)}, u32[]{:S(2)}) copy-start(bf16[10,64,128]{2,1,0:T(8,128)(2,1)} %get-tuple-element.87) | copy-start | bytes 491524
  4.7 20.6 %collective-permute-start = (bf16[30,64,128]{2,1,0:T(8,128)(2,1)}, bf16[30,64,128]{2,1,0:T(8,128)(2,1)S(1)}, u32[]{:S(2)}, u32[]{:S(2)}) collective-permute-start(bf16[30,64,128]{2,1,0:T(8,128)(2,1)} %get-tuple-element.63), channel_id=1, source_target_pairs={{0,35},{32,1},{1,32},{33,2},{2,33},{34,3},{3,34},{35,0},{4,39},{36... | collective-permute-start | bytes 1474568 | tf_op jit(solution)/shard_map/ppermute | solution.py:236
  6.7 13.1 %collective-permute-start.2 = (bf16[20,64,128]{2,1,0:T(8,128)(2,1)}, bf16[20,64,128]{2,1,0:T(8,128)(2,1)S(1)}, u32[]{:S(2)}, u32[]{:S(2)}) collective-permute-start(bf16[20,64,128]{2,1,0:T(8,128)(2,1)} %get-tuple-element.83.refs_1_), channel_id=1, source_target_pairs={{0,8},{8,16},{16,24},{24,0},{1,9},{9,17},{17,25},{25,1},{2,10},{10... | collective-permute-start | bytes 983048 | tf_op jit(solution)/shard_map/ppermute | solution.py:234
  8.2 15.5 %collective-permute-start.3 = (bf16[20,64,128]{2,1,0:T(8,128)(2,1)}, bf16[20,64,128]{2,1,0:T(8,128)(2,1)S(1)}, u32[]{:S(2)}, u32[]{:S(2)}) collective-permute-start(bf16[20,64,128]{2,1,0:T(8,128)(2,1)} %get-tuple-element.83.refs_1_), channel_id=1, source_target_pairs={{0,24},{8,0},{16,8},{24,16},{1,25},{9,1},{17,9},{25,17},{2,26},{10... | collective-permute-start | bytes 983048 | tf_op jit(solution)/shard_map/ppermute | solution.py:234
  10.0 15.4 %collective-permute-start.4 = (bf16[20,64,128]{2,1,0:T(8,128)(2,1)}, bf16[20,64,128]{2,1,0:T(8,128)(2,1)S(1)}, u32[]{:S(2)}, u32[]{:S(2)}) collective-permute-start(bf16[20,64,128]{2,1,0:T(8,128)(2,1)} %get-tuple-element.83.refs_1_), channel_id=1, source_target_pairs={{0,16},{8,24},{16,0},{24,8},{1,17},{9,25},{17,1},{25,9},{2,18},{10... | collective-permute-start | bytes 983048 | tf_op jit(solution)/shard_map/ppermute | solution.py:234
  11.8 8.0 %collective-permute-start.1 = (bf16[10,64,128]{2,1,0:T(8,128)(2,1)}, bf16[10,64,128]{2,1,0:T(8,128)(2,1)S(1)}, u32[]{:S(2)}, u32[]{:S(2)}) collective-permute-start(bf16[10,64,128]{2,1,0:T(8,128)(2,1)} %get-tuple-element.64), channel_id=1, source_target_pairs={{0,1},{32,35},{1,2},{33,32},{2,3},{34,33},{3,0},{35,34},{4,5},{36,... | collective-permute-start | bytes 491528 | tf_op jit(solution)/shard_map/ppermute | solution.py:237
  25.3 24.3 %collective-permute-start.7 = (bf16[20,64,128]{2,1,0:T(8,128)(2,1)S(1)}, bf16[20,64,128]{2,1,0:T(8,128)(2,1)S(1)}, u32[]{:S(2)}, u32[]{:S(2)}) collective-permute-start(bf16[20,64,128]{2,1,0:T(8,128)(2,1)S(1)} %slice.6.refs_5_), channel_id=1, source_target_pairs={{0,8},{8,16},{16,24},{24,0},{1,9},{9,17},{17,25},{25,1},{2,10},{10... | collective-permute-start | bytes 983048 | tf_op jit(solution)/shard_map/ppermute | solution.py:234
  26.6 23.1 %collective-permute-start.8 = (bf16[20,64,128]{2,1,0:T(8,128)(2,1)S(1)}, bf16[20,64,128]{2,1,0:T(8,128)(2,1)S(1)}, u32[]{:S(2)}, u32[]{:S(2)}) collective-permute-start(bf16[20,64,128]{2,1,0:T(8,128)(2,1)S(1)} %slice.6.refs_5_), channel_id=1, source_target_pairs={{0,24},{8,0},{16,8},{24,16},{1,25},{9,1},{17,9},{25,17},{2,26},{10... | collective-permute-start | bytes 983048 | tf_op jit(solution)/shard_map/ppermute | solution.py:234
  28.7 21.0 %collective-permute-start.9 = (bf16[20,64,128]{2,1,0:T(8,128)(2,1)S(1)}, bf16[20,64,128]{2,1,0:T(8,128)(2,1)S(1)}, u32[]{:S(2)}, u32[]{:S(2)}) collective-permute-start(bf16[20,64,128]{2,1,0:T(8,128)(2,1)S(1)} %slice.6.refs_5_), channel_id=1, source_target_pairs={{0,16},{8,24},{16,0},{24,8},{1,17},{9,25},{17,1},{25,9},{2,18},{10... | collective-permute-start | bytes 983048 | tf_op jit(solution)/shard_map/ppermute | solution.py:234
  28.9 20.8 %collective-permute-start.5 = (bf16[20,64,128]{2,1,0:T(8,128)(2,1)}, bf16[20,64,128]{2,1,0:T(8,128)(2,1)S(1)}, u32[]{:S(2)}, u32[]{:S(2)}) collective-permute-start(bf16[20,64,128]{2,1,0:T(8,128)(2,1)} %get-tuple-element.69), channel_id=1, source_target_pairs={{0,1},{32,35},{1,2},{33,32},{2,3},{34,33},{3,0},{35,34},{4,5},{36,... | collective-permute-start | bytes 983048 | tf_op jit(solution)/shard_map/ppermute | solution.py:243
  33.2 16.4 %collective-permute-start.6 = (bf16[10,64,128]{2,1,0:T(8,128)(2,1)}, bf16[10,64,128]{2,1,0:T(8,128)(2,1)S(1)}, u32[]{:S(2)}, u32[]{:S(2)}) collective-permute-start(bf16[10,64,128]{2,1,0:T(8,128)(2,1)} %get-tuple-element.70), channel_id=1, source_target_pairs={{0,34},{32,2},{1,35},{33,3},{2,32},{34,0},{3,33},{35,1},{4,38},{36... | collective-permute-start | bytes 491528 | tf_op jit(solution)/shard_map/ppermute | solution.py:244
  50.8 22.4 %collective-permute-start.14 = (bf16[80,64,128]{2,1,0:T(8,128)(2,1)S(1)}, bf16[80,64,128]{2,1,0:T(8,128)(2,1)S(1)}, u32[]{:S(2)}, u32[]{:S(2)}) collective-permute-start(bf16[80,64,128]{2,1,0:T(8,128)(2,1)S(1)} %pad_maximum_fusion), channel_id=1, source_target_pairs={{0,4},{4,0},{1,5},{5,1},{2,6},{6,2},{3,7},{7,3},{8,12},{12,8},{9,1... | collective-permute-start | bytes 3932168 | tf_op jit(solution)/shard_map/ppermute | solution.py:251
  50.9 22.3 %collective-permute-start.11 = (bf16[20,64,128]{2,1,0:T(8,128)(2,1)S(1)}, bf16[20,64,128]{2,1,0:T(8,128)(2,1)S(1)}, u32[]{:S(2)}, u32[]{:S(2)}) collective-permute-start(bf16[20,64,128]{2,1,0:T(8,128)(2,1)S(1)} %collective-permute-done.5.refs_9_), channel_id=1, source_target_pairs={{0,8},{8,16},{16,24},{24,0},{1,9},{9,17},{17,25},{25,1},{2,10},{10... | collective-permute-start | bytes 983048 | tf_op jit(solution)/shard_map/ppermute | solution.py:234
  51.8 21.4 %collective-permute-start.12 = (bf16[20,64,128]{2,1,0:T(8,128)(2,1)S(1)}, bf16[20,64,128]{2,1,0:T(8,128)(2,1)S(1)}, u32[]{:S(2)}, u32[]{:S(2)}) collective-permute-start(bf16[20,64,128]{2,1,0:T(8,128)(2,1)S(1)} %collective-permute-done.5.refs_9_), channel_id=1, source_target_pairs={{0,24},{8,0},{16,8},{24,16},{1,25},{9,1},{17,9},{25,17},{2,26},{10... | collective-permute-start | bytes 983048 | tf_op jit(solution)/shard_map/ppermute | solution.py:234
  54.2 19.0 %collective-permute-start.13 = (bf16[20,64,128]{2,1,0:T(8,128)(2,1)S(1)}, bf16[20,64,128]{2,1,0:T(8,128)(2,1)S(1)}, u32[]{:S(2)}, u32[]{:S(2)}) collective-permute-start(bf16[20,64,128]{2,1,0:T(8,128)(2,1)S(1)} %collective-permute-done.5.refs_9_), channel_id=1, source_target_pairs={{0,16},{8,24},{16,0},{24,8},{1,17},{9,25},{17,1},{25,9},{2,18},{10... | collective-permute-start | bytes 983048 | tf_op jit(solution)/shard_map/ppermute | solution.py:234
  56.2 17.0 %collective-permute-start.10 = (bf16[20,64,128]{2,1,0:T(8,128)(2,1)S(1)}, bf16[20,64,128]{2,1,0:T(8,128)(2,1)S(1)}, u32[]{:S(2)}, u32[]{:S(2)}) collective-permute-start(bf16[20,64,128]{2,1,0:T(8,128)(2,1)S(1)} %copy-done.3), channel_id=1, source_target_pairs={{0,34},{32,2},{1,35},{33,3},{2,32},{34,0},{3,33},{35,1},{4,38},{36... | collective-permute-start | bytes 983048 | tf_op jit(solution)/shard_map/ppermute | solution.py:249
  56.4 38.9 %copy-start = (bf16[20,64,128]{2,1,0:T(8,128)(2,1)S(1)}, bf16[20,64,128]{2,1,0:T(8,128)(2,1)}, u32[]{:S(2)}) copy-start(bf16[20,64,128]{2,1,0:T(8,128)(2,1)} %get-tuple-element.83.refs_1_) | copy-start | bytes 983044
  73.6 18.5 %collective-permute-start.18 = (bf16[160,64,128]{2,1,0:T(8,128)(2,1)S(1)}, bf16[160,64,128]{2,1,0:T(8,128)(2,1)S(1)}, u32[]{:S(2)}, u32[]{:S(2)}) collective-permute-start(bf16[160,64,128]{2,1,0:T(8,128)(2,1)S(1)} %constant_dynamic-update-slice_fusion), channel_id=1, source_target_pairs={{0,4},{4,0},{1,5},{5,1},{2,6},{6,2},{3,7},{7,3},{8,12},{12,8},{9,1... | collective-permute-start | bytes 7864328 | tf_op jit(solution)/shard_map/ppermute | solution.py:258
  73.7 18.4 %collective-permute-start.19 = (bf16[4,10,64,128]{3,2,1,0:T(8,128)(2,1)S(1)}, bf16[4,10,64,128]{3,2,1,0:T(8,128)(2,1)S(1)}, u32[]{:S(2)}, u32[]{:S(2)}) collective-permute-start(bf16[4,10,64,128]{3,2,1,0:T(8,128)(2,1)S(1)} %pad_maximum_fusion.1.refs_0_), channel_id=1, source_target_pairs={{0,32},{32,0},{1,33},{33,1},{2,34},{34,2},{3,35},{35,3},{4,36},{36... | collective-permute-start | bytes 1966088 | tf_op jit(solution)/shard_map/ppermute | solution.py:257
  74.0 18.1 %collective-permute-start.15 = (bf16[20,64,128]{2,1,0:T(8,128)(2,1)S(1)}, bf16[20,64,128]{2,1,0:T(8,128)(2,1)S(1)}, u32[]{:S(2)}, u32[]{:S(2)}) collective-permute-start(bf16[20,64,128]{2,1,0:T(8,128)(2,1)S(1)} %collective-permute-done.10.refs_13_), channel_id=1, source_target_pairs={{0,8},{8,16},{16,24},{24,0},{1,9},{9,17},{17,25},{25,1},{2,10},{10... | collective-permute-start | bytes 983048 | tf_op jit(solution)/shard_map/ppermute | solution.py:234
  74.1 18.0 %collective-permute-start.16 = (bf16[20,64,128]{2,1,0:T(8,128)(2,1)S(1)}, bf16[20,64,128]{2,1,0:T(8,128)(2,1)S(1)}, u32[]{:S(2)}, u32[]{:S(2)}) collective-permute-start(bf16[20,64,128]{2,1,0:T(8,128)(2,1)S(1)} %collective-permute-done.10.refs_13_), channel_id=1, source_target_pairs={{0,24},{8,0},{16,8},{24,16},{1,25},{9,1},{17,9},{25,17},{2,26},{10... | collective-permute-start | bytes 983048 | tf_op jit(solution)/shard_map/ppermute | solution.py:234
  77.3 14.8 %collective-permute-start.17 = (bf16[20,64,128]{2,1,0:T(8,128)(2,1)S(1)}, bf16[20,64,128]{2,1,0:T(8,128)(2,1)S(1)}, u32[]{:S(2)}, u32[]{:S(2)}) collective-permute-start(bf16[20,64,128]{2,1,0:T(8,128)(2,1)S(1)} %collective-permute-done.10.refs_13_), channel_id=1, source_target_pairs={{0,16},{8,24},{16,0},{24,8},{1,17},{9,25},{17,1},{25,9},{2,18},{10... | collective-permute-start | bytes 983048 | tf_op jit(solution)/shard_map/ppermute | solution.py:234
  92.1 1.7 %collective-permute-start.20 = (bf16[20,64,128]{2,1,0:T(8,128)(2,1)S(1)}, bf16[20,64,128]{2,1,0:T(8,128)(2,1)S(1)}, u32[]{:S(2)}, u32[]{:S(2)}) collective-permute-start(bf16[20,64,128]{2,1,0:T(8,128)(2,1)S(1)} %collective-permute-done.10.refs_13_), channel_id=1, source_target_pairs={{0,4},{4,0},{1,5},{5,1},{2,6},{6,2},{3,7},{7,3},{8,12},{12,8},{9,1... | collective-permute-start | bytes 983048 | tf_op jit(solution)/shard_map/ppermute | solution.py:235
  92.2 2.1 %collective-permute-start.21 = (bf16[20,64,128]{2,1,0:T(8,128)(2,1)S(1)}, bf16[20,64,128]{2,1,0:T(8,128)(2,1)S(1)}, u32[]{:S(2)}, u32[]{:S(2)}) collective-permute-start(bf16[20,64,128]{2,1,0:T(8,128)(2,1)S(1)} %collective-permute-done.15.refs_14_), channel_id=1, source_target_pairs={{0,4},{4,0},{1,5},{5,1},{2,6},{6,2},{3,7},{7,3},{8,12},{12,8},{9,1... | collective-permute-start | bytes 983048 | tf_op jit(solution)/shard_map/ppermute | solution.py:235
  92.7 2.1 %collective-permute-start.22 = (bf16[20,64,128]{2,1,0:T(8,128)(2,1)S(1)}, bf16[20,64,128]{2,1,0:T(8,128)(2,1)S(1)}, u32[]{:S(2)}, u32[]{:S(2)}) collective-permute-start(bf16[20,64,128]{2,1,0:T(8,128)(2,1)S(1)} %collective-permute-done.16.refs_15_), channel_id=1, source_target_pairs={{0,4},{4,0},{1,5},{5,1},{2,6},{6,2},{3,7},{7,3},{8,12},{12,8},{9,1... | collective-permute-start | bytes 983048 | tf_op jit(solution)/shard_map/ppermute | solution.py:235
  92.8 2.4 %collective-permute-start.23 = (bf16[20,64,128]{2,1,0:T(8,128)(2,1)S(1)}, bf16[20,64,128]{2,1,0:T(8,128)(2,1)S(1)}, u32[]{:S(2)}, u32[]{:S(2)}) collective-permute-start(bf16[20,64,128]{2,1,0:T(8,128)(2,1)S(1)} %collective-permute-done.17.refs_16_), channel_id=1, source_target_pairs={{0,4},{4,0},{1,5},{5,1},{2,6},{6,2},{3,7},{7,3},{8,12},{12,8},{9,1... | collective-permute-start | bytes 983048 | tf_op jit(solution)/shard_map/ppermute | solution.py:235
  99.0 8.8 %collective-permute-start.24 = (bf16[2,544,128]{2,1,0:T(8,128)(2,1)S(1)}, bf16[2,544,128]{2,1,0:T(8,128)(2,1)S(1)}, u32[]{:S(2)}, u32[]{:S(2)}) collective-permute-start(bf16[2,544,128]{2,1,0:T(8,128)(2,1)S(1)} %far_rows.2), channel_id=1, source_target_pairs={{0,32},{32,0},{1,33},{33,1},{2,34},{34,2},{3,35},{35,3},{4,36},{36... | collective-permute-start | bytes 835592 | tf_op jit(solution)/shard_map/ppermute | solution.py:268
  106.4 12.9 %collective-permute-start.25 = (bf16[3,544,128]{2,1,0:T(8,128)(2,1)S(1)}, bf16[3,544,128]{2,1,0:T(8,128)(2,1)S(1)}, u32[]{:S(2)}, u32[]{:S(2)}) collective-permute-start(bf16[3,544,128]{2,1,0:T(8,128)(2,1)S(1)} %far_rows.3), channel_id=1, source_target_pairs={{0,32},{32,0},{1,33},{33,1},{2,34},{34,2},{3,35},{35,3},{4,36},{36... | collective-permute-start | bytes 1253384 | tf_op jit(solution)/shard_map/ppermute | solution.py:268
  111.3 13.3 %collective-permute-start.26 = (bf16[2,2,64,128]{3,2,1,0:T(8,128)(2,1)S(1)}, bf16[2,2,64,128]{3,2,1,0:T(8,128)(2,1)S(1)}, u32[]{:S(2)}, u32[]{:S(2)}) collective-permute-start(bf16[2,2,64,128]{3,2,1,0:T(8,128)(2,1)S(1)} %get-tuple-element.116), channel_id=1, source_target_pairs={{0,35},{32,1},{1,32},{33,2},{2,33},{34,3},{3,34},{35,0},{4,39},{36... | collective-permute-start | bytes 196616 | tf_op jit(solution)/shard_map/ppermute | solution.py:275
  112.5 12.1 %collective-permute-start.27 = (bf16[2,2,64,128]{3,2,1,0:T(8,128)(2,1)S(1)}, bf16[2,2,64,128]{3,2,1,0:T(8,128)(2,1)S(1)}, u32[]{:S(2)}, u32[]{:S(2)}) collective-permute-start(bf16[2,2,64,128]{3,2,1,0:T(8,128)(2,1)S(1)} %get-tuple-element.117), channel_id=1, source_target_pairs={{0,3},{32,33},{1,0},{33,34},{2,1},{34,35},{3,2},{35,32},{4,7},{36,... | collective-permute-start | bytes 196616 | tf_op jit(solution)/shard_map/ppermute | solution.py:275
  116.3 8.3 %copy-start.1 = (s32[4]{0:T(128)S(1)}, s32[4]{0:T(128)}, u32[]{:S(2)}) copy-start(s32[4]{0:T(128)} %fusion.offs) | copy-start | bytes 52
  116.3 8.3 %collective-permute-start.28 = (bf16[2,2,64,128]{3,2,1,0:T(8,128)(2,1)S(1)}, bf16[2,2,64,128]{3,2,1,0:T(8,128)(2,1)S(1)}, u32[]{:S(2)}, u32[]{:S(2)}) collective-permute-start(bf16[2,2,64,128]{3,2,1,0:T(8,128)(2,1)S(1)} %get-tuple-element.118), channel_id=1, source_target_pairs={{0,34},{32,2},{1,35},{33,3},{2,32},{34,0},{3,33},{35,1},{4,38},{36... | collective-permute-start | bytes 196616 | tf_op jit(solution)/shard_map/ppermute | solution.py:275
  125.2 9.3 %collective-permute-start.31 = (bf16[3,2,64,128]{3,2,1,0:T(8,128)(2,1)S(1)}, bf16[3,2,64,128]{3,2,1,0:T(8,128)(2,1)S(1)}, u32[]{:S(2)}, u32[]{:S(2)}) collective-permute-start(bf16[3,2,64,128]{3,2,1,0:T(8,128)(2,1)S(1)} %get-tuple-element.123), channel_id=1, source_target_pairs={{0,34},{32,2},{1,35},{33,3},{2,32},{34,0},{3,33},{35,1},{4,38},{36... | collective-permute-start | bytes 294920 | tf_op jit(solution)/shard_map/ppermute | solution.py:275
  129.1 7.6 %collective-permute-start.30 = (bf16[3,2,64,128]{3,2,1,0:T(8,128)(2,1)S(1)}, bf16[3,2,64,128]{3,2,1,0:T(8,128)(2,1)S(1)}, u32[]{:S(2)}, u32[]{:S(2)}) collective-permute-start(bf16[3,2,64,128]{3,2,1,0:T(8,128)(2,1)S(1)} %get-tuple-element.122), channel_id=1, source_target_pairs={{0,3},{32,33},{1,0},{33,34},{2,1},{34,35},{3,2},{35,32},{4,7},{36,... | collective-permute-start | bytes 294920 | tf_op jit(solution)/shard_map/ppermute | solution.py:275
  130.0 7.0 %collective-permute-start.29 = (bf16[3,2,64,128]{3,2,1,0:T(8,128)(2,1)S(1)}, bf16[3,2,64,128]{3,2,1,0:T(8,128)(2,1)S(1)}, u32[]{:S(2)}, u32[]{:S(2)}) collective-permute-start(bf16[3,2,64,128]{3,2,1,0:T(8,128)(2,1)S(1)} %get-tuple-element.121), channel_id=1, source_target_pairs={{0,35},{32,1},{1,32},{33,2},{2,33},{34,3},{3,34},{35,0},{4,39},{36... | collective-permute-start | bytes 294920 | tf_op jit(solution)/shard_map/ppermute | solution.py:275

commit v3 on v2

--- a/solution.py
+++ b/solution.py
@@ -105,7 +105,7 @@
     return block.reshape(block.shape[0] * block.shape[1], block.shape[2])
 
 
-def core_part(q_ref, kv_refs, kk, vv):
+def load_keys(kv_refs, kk, vv):
     row = 0
     for ref in kv_refs:
         rows = pl.ds(row, ROWS)
@@ -114,6 +114,9 @@
         kk[rows, HEAD_DIM:] = ref[2]
         vv[rows, :HEAD_DIM] = ref[1]
         vv[rows, HEAD_DIM:] = ref[3]
+
+
+def core_part(q_ref, kk, vv):
     q, dq = fold(q_ref[:, 0]), fold(q_ref[:, 1])
     nt = (((1,), (1,)), ((), ()))
     dot = functools.partial(lax.dot_general, preferred_element_type=jnp.float32)
@@ -141,29 +144,26 @@
     return high, middle, rest - middle
 
 
-def far_body(count, *refs):
-    q_ref, kv_refs, (out, kk, vv) = refs[0], refs[1 : 1 + count], refs[1 + count :]
-    att, tan, lse, slope = core_part(q_ref, kv_refs, kk, vv)
+def write_part(out, part):
+    att, tan, lse, slope = part
     n = att.shape[0]
-    out[0, :n] = att.astype(jnp.bfloat16)
-    out[0, n : 2 * n] = tan.astype(jnp.bfloat16)
+    out[:n] = att.astype(jnp.bfloat16)
+    out[n : 2 * n] = tan.astype(jnp.bfloat16)
     lane = lax.broadcasted_iota(jnp.int32, (n, HEAD_DIM), 1)
     stats = jnp.zeros((n, HEAD_DIM), jnp.float32)
     for i, column in enumerate(three(lse) + three(slope)):
         stats = jnp.where(lane == i, column, stats)
     flat = jnp.transpose(stats)[:16].astype(jnp.bfloat16)
-    out[0, 2 * n : 2 * n + 16] = flat[:, :HEAD_DIM]
-    out[0, 2 * n + 16 :] = flat[:, HEAD_DIM:]
-
-
-def near_body(count, *refs):
-    q_ref, kv_refs, got = refs[0], refs[1 : 1 + count], refs[1 + count]
-    outs, (kk, vv) = refs[2 + count : 6 + count], refs[6 + count :]
-    att, tan, lse, slope = core_part(q_ref, kv_refs, kk, vv)
+    out[2 * n : 2 * n + 16] = flat[:, :HEAD_DIM]
+    out[2 * n + 16 :] = flat[:, HEAD_DIM:]
+
+
+def merge(part, got):
+    att, tan, lse, slope = part
     n = att.shape[0]
-    att2 = got[0, :n].astype(jnp.float32)
-    tan2 = got[0, n : 2 * n].astype(jnp.float32)
-    flat = jnp.concatenate([got[0, 2 * n : 2 * n + 16], got[0, 2 * n + 16 :]], axis=1)
+    att2 = got[:n].astype(jnp.float32)
+    tan2 = got[n : 2 * n].astype(jnp.float32)
+    flat = jnp.concatenate([got[2 * n : 2 * n + 16], got[2 * n + 16 :]], axis=1)
     flat = flat.astype(jnp.float32)
 
     def column(i):
@@ -173,37 +173,59 @@
     lse2, slope2 = column(0), column(3)
     w1 = 1.0 / (1.0 + jnp.exp(lse2 - lse))
     w2 = 1.0 / (1.0 + jnp.exp(lse - lse2))
-    tan = w1 * tan + w2 * tan2 + (w1 * w2) * (slope - slope2) * (att - att2)
-    att = w1 * att + w2 * att2
-    for slot in range(4):
-        rows = slice(slot * ROWS, (slot + 1) * ROWS)
-        outs[slot][0, 0] = att[rows].astype(jnp.bfloat16)
-        outs[slot][0, 1] = tan[rows].astype(jnp.bfloat16)
-
-
-def attend(q, pieces, low, high, got=None):
+    top = jnp.maximum(lse, lse2)
+    return (
+        w1 * att + w2 * att2,
+        w1 * tan + w2 * tan2 + (w1 * w2) * (slope - slope2) * (att - att2),
+        top + jnp.log(jnp.exp(lse - top) + jnp.exp(lse2 - top)),
+        w1 * slope + w2 * slope2,
+    )
+
+
+def attend_body(q_count, got_count, piece_count, *refs):
+    refs = list(refs)
+    take = lambda n: [refs.pop(0) for _ in range(n)]
+    q_refs, got_refs, kv_refs = take(q_count), take(got_count), take(piece_count)
+    kk, vv = refs.pop(-2), refs.pop(-1)
+    load_keys(kv_refs, kk, vv)
+    for i, q_ref in enumerate(q_refs):
+        part = core_part(q_ref, kk, vv)
+        for got in got_refs:
+            part = merge(part, got.at[0, 0])
+        if len(refs) == 1:
+            write_part(refs[0].at[0, i], part)
+        else:
+            for slot in range(4):
+                rows = slice(slot * ROWS, (slot + 1) * ROWS)
+                refs[slot][0, 0] = part[0][rows].astype(jnp.bfloat16)
+                refs[slot][0, 1] = part[1][rows].astype(jnp.bfloat16)
+
+
+def attend(name, qs, pieces, chunk, gots=(), last=False):
+    low, high = chunk
     heads = high - low
     keys = len(pieces) * ROWS
     rows = 4 * ROWS
-    in_specs = [pl.BlockSpec((4, 2, ROWS, HEAD_DIM), lambda h: (0, h + low, 0, 0))]
+    wide = 2 * rows + 32
+    in_specs = [pl.BlockSpec((4, 2, ROWS, HEAD_DIM), lambda h: (0, h + low, 0, 0))] * len(qs)
+    for _, start, which in gots:
+        in_specs.append(
+            pl.BlockSpec(
+                (1, 1, wide, HEAD_DIM), lambda h, n=low - start, i=which: (h + n, i, 0, 0)
+            )
+        )
     for _, i in pieces:
         in_specs.append(
             pl.BlockSpec((4, ROWS, HEAD_DIM), lambda h, i=i: (h + low + i * HEADS_HERE, 0, 0))
         )
-    args = [q] + [p for p, _ in pieces]
-    wide = 2 * rows + 32
-    if got is None:
-        body = functools.partial(far_body, len(pieces))
-        out_shape = jax.ShapeDtypeStruct((heads, wide, HEAD_DIM), jnp.bfloat16)
-        out_specs = pl.BlockSpec((1, wide, HEAD_DIM), lambda h: (h, 0, 0))
-    else:
-        body = functools.partial(near_body, len(pieces))
-        args.append(got)
-        in_specs.append(pl.BlockSpec((1, wide, HEAD_DIM), lambda h: (h, 0, 0)))
+    if last:
         out_shape = [jax.ShapeDtypeStruct((heads, 2, ROWS, HEAD_DIM), jnp.bfloat16)] * 4
         out_specs = [pl.BlockSpec((1, 2, ROWS, HEAD_DIM), lambda h: (h, 0, 0, 0))] * 4
+    else:
+        out_shape = jax.ShapeDtypeStruct((heads, len(qs), wide, HEAD_DIM), jnp.bfloat16)
+        out_specs = pl.BlockSpec((1, len(qs), wide, HEAD_DIM), lambda h: (h, 0, 0, 0))
     return pl.pallas_call(
-        body,
+        functools.partial(attend_body, len(qs), len(gots), len(pieces)),
         grid=(heads,),
         out_shape=out_shape,
         in_specs=in_specs,
@@ -211,12 +233,12 @@
         scratch_shapes=[pltpu.VMEM((keys, 2 * HEAD_DIM), jnp.bfloat16)] * 2,
         compiler_params=pltpu.CompilerParams(vmem_limit_bytes=VMEM),
         cost_estimate=pl.CostEstimate(
-            flops=16 * heads * rows * keys * HEAD_DIM,
+            flops=16 * len(qs) * heads * rows * keys * HEAD_DIM,
             bytes_accessed=heads * keys * 4 * HEAD_DIM * 2,
-            transcendentals=heads * rows * keys,
+            transcendentals=len(qs) * heads * rows * keys,
         ),
-        name="far_rows" if got is None else "near_rows",
-    )(*args)
+        name=name,
+    )(*qs, *[array for array, _, _ in gots], *[p for p, _ in pieces])
 
 
 def after(value, *needed):
@@ -256,19 +278,26 @@
     three_x = around(three_)
     far_q = lax.ppermute(near_q, Z, PAIR)
     both_s = lax.ppermute(jnp.concatenate([one, *one_x, two, *two_x]), "core", SWAP)
-    three_, three_x, both_s, far_q = lax.optimization_barrier((three_, three_x, both_s, far_q))
+    pieces = [(p, 0) for p in (own, *own_x, one, *one_x, two, *two_x)]
+    pieces += [(own_s, i) for i in range(4)] + [(both_s, i) for i in range(8)]
+    early = attend("early", [near_q], pieces, (0, HEADS_HERE))
+    three_, three_x, far_q, early = lax.optimization_barrier((three_, three_x, far_q, early))
     three_s = swap([three_, *three_x])
-    pieces = [(p, 0) for p in (own, *own_x, one, *one_x, two, *two_x, three_, *three_x, *three_s)]
-    pieces += [(own_s, i) for i in range(4)] + [(both_s, i) for i in range(8)]
-    sent, got, result, last, back = {}, {}, (), (), []
+    late = [(p, 0) for p in (three_, *three_x, *three_s)]
+    early_far = attend("early_far", [far_q], pieces, CHUNKS[0])
+    paired, result, last, back = {}, (), (), []
     for kind, c in ORDER:
-        low, high = CHUNKS[c]
+        chunk = CHUNKS[c]
         if kind == "far":
-            sent[c] = attend(after(far_q, *last), pieces, low, high)
-            got[c] = lax.ppermute(sent[c], Z, PAIR)
-            last = (sent[c],)
+            if c == 0:
+                part = attend(kind, [far_q], late, chunk, [(early_far, chunk[0], 0)])
+            else:
+                part = attend(kind, [after(far_q, *last)], pieces + late, chunk)
+            paired[c] = lax.ppermute(after(part, *paired.values()), Z, PAIR)
+            last = (part,)
         else:
-            near = attend(after(near_q, *last), pieces, low, high, got[c])
+            gots = [(early, 0, 0), (paired[c], chunk[0], 0)]
+            near = attend(kind, [after(near_q, *last)], late, chunk, gots, last=True)
             if back:
                 result = unpack(c - 1, offs, [after(back[0], *near), *back[1:]], result)
             back = [near[0]]

time: 140 us -> 140 us (level)
  waiting for transfers between devices: 66.4 us -> 60.4 us
  Pallas kernels: 23.7 us -> 27.6 us
  starting transfers between devices: 45.2 us -> 48.5 us
    ppermute x12, waiting for transfers between devices: 19.5 us -> 11.8 us  [per_device(): around = lambda array: [lax.ppermute(array, 'x', perm) for perm in AROUND_X]]
    pallas_call x4 -> x6, Pallas kernels: 18.2 us -> 22.1 us  [attend(): pl.pallas_call(functools.partial(attend_body, len(qs), len(gots), len(pie...]
    ppermute x6, waiting for transfers between devices: 5.96 us -> 8.68 us  [per_device(): lax.ppermute(after(o, *result), Z, perm)]
    ppermute x6, starting transfers between devices: 11.5 us -> 13.6 us  [per_device(): lax.ppermute(after(o, *result), Z, perm)]
    ppermute x4, waiting for transfers between devices: 2.01 us -> 0.01 us  [per_device(): swap = lambda arrays: [lax.ppermute(a, 'core', SWAP) for a in arrays]]
  transfers between devices with their start and end apart: 32 -> 32, of which waited for: 15 -> 11; matrix products, arithmetic and copies ran while one was open for 0% -> 0% of each run, Pallas kernels for 10% -> 15%
where the time goes in v3:
time: 140 us
  waiting for transfers between devices  60.4 us (43%)
  starting transfers between devices  48.5 us (35%)
  Pallas kernels  27.6 us (20%)
  other arithmetic  1.85 us (1%)
    pallas_call x6, Pallas kernels, attend(): pl.pallas_call(functools.partial(attend_body, len(qs), len(gots), len(pie...  22.1 us
    ppermute x12, starting transfers between devices, per_device(): around = lambda array: [lax.ppermute(array, 'x', perm) for perm in AROUND_X]  17.9 us
    ppermute x1, waiting for transfers between devices, per_device(): three_ = lax.ppermute(to_three, Z, TO[2])  16.8 us
    ppermute x1, waiting for transfers between devices, per_device(): three_q = lax.ppermute(to_three_q, Z, TO[2])  15.7 us
    ppermute x6, starting transfers between devices, per_device(): lax.ppermute(after(o, *result), Z, perm)  13.6 us
    ppermute x12, waiting for transfers between devices, per_device(): around = lambda array: [lax.ppermute(array, 'x', perm) for perm in AROUND_X]  11.8 us
    ppermute x6, waiting for transfers between devices, per_device(): lax.ppermute(after(o, *result), Z, perm)  8.68 us
    ppermute x1, waiting for transfers between devices, per_device(): two_q = lax.ppermute(to_two_q, Z, TO[1])  4.46 us
  transfers between devices with their start and end apart: 32, of which 11 were waited for; matrix products, arithmetic and copies ran while one was open for 0% of the time, Pallas kernels for 15%

profile of v3, /device:TPU:40, one launch (start us, length us, event | category | flops | bytes accessed | tf_op | source)
XLA Modules:
  0.0 139.7 jit_solution(14250308695017778445)
XLA Ops:
  0.6 0.6 fusion.offs
  1.3 3.4 %pack.1 = (bf16[20,64,128]{2,1,0:T(8,128)(2,1)}, bf16[30,64,128]{2,1,0:T(8,128)(2,1)}, bf16[20,64,128]{2,1,0:T(8,128)(2,1)}, bf16[20,64,128]{2,1,0:T(8,128)(2,1)...) custom-call(s32[4]{0:T(128)} %fusion.offs, bf16[64,2560]{1,0:T(8,128)(2,1)} %refs_0_.1, ...), custom_call_target="tpu_custom_call" | custom-call | tf_op jit(solution)/shard_map/pack/pallas_call | solution.py:65
  4.7 2.0 %collective-permute-start = (bf16[30,64,128]{2,1,0:T(8,128)(2,1)}, bf16[30,64,128]{2,1,0:T(8,128)(2,1)S(1)}, u32[]{:S(2)}, u32[]{:S(2)}) collective-permute-start(bf16[30,64,128]{2,1,0:T(8,128)(2,1)} %get-tuple-element.64), channel_id=1, source_target_pairs={{0,35},{32,1},{1,32},{33,2},{2,33},{34,3},{3,34},{35,0},{4,39},{36... | collective-permute-start | bytes 1474568 | tf_op jit(solution)/shard_map/ppermute | solution.py:258
  6.7 3.0 %collective-permute-start.4 = (bf16[20,64,128]{2,1,0:T(8,128)(2,1)}, bf16[20,64,128]{2,1,0:T(8,128)(2,1)S(1)}, u32[]{:S(2)}, u32[]{:S(2)}) collective-permute-start(bf16[20,64,128]{2,1,0:T(8,128)(2,1)} %get-tuple-element.84.refs_1_), channel_id=1, source_target_pairs={{0,16},{8,24},{16,0},{24,8},{1,17},{9,25},{17,1},{25,9},{2,18},{10... | collective-permute-start | bytes 983048 | tf_op jit(solution)/shard_map/ppermute | solution.py:256
  9.7 1.1 collective-permute-start.3
  10.9 0.9 collective-permute-start.2
  11.8 3.6 %collective-permute-start.1 = (bf16[10,64,128]{2,1,0:T(8,128)(2,1)}, bf16[10,64,128]{2,1,0:T(8,128)(2,1)S(1)}, u32[]{:S(2)}, u32[]{:S(2)}) collective-permute-start(bf16[10,64,128]{2,1,0:T(8,128)(2,1)} %get-tuple-element.65), channel_id=1, source_target_pairs={{0,1},{32,35},{1,2},{33,32},{2,3},{34,33},{3,0},{35,34},{4,5},{36,... | collective-permute-start | bytes 491528 | tf_op jit(solution)/shard_map/ppermute | solution.py:259
  15.3 4.5 %collective-permute-done.1 = bf16[10,64,128]{2,1,0:T(8,128)(2,1)S(1)} collective-permute-done((bf16[10,64,128]{2,1,0:T(8,128)(2,1)}, bf16[10,64,128]{2,1,0:T(8,128)(2,1)S(1)}, u32[]{:S(2)}, u32[]{:S(2)}) %collective-permute-start.1) | collective-permute-done | bytes 163872 | tf_op jit(solution)/shard_map/ppermute | solution.py:259
  19.8 4.9 %collective-permute-done.3.refs_3_ = bf16[20,64,128]{2,1,0:T(8,128)(2,1)S(1)} collective-permute-done((bf16[20,64,128]{2,1,0:T(8,128)(2,1)}, bf16[20,64,128]{2,1,0:T(8,128)(2,1)S(1)}, u32[]{:S(2)}, u32[]{:S(2)}) %collective-permute-start.3) | collective-permute-done | bytes 327712 | tf_op jit(solution)/shard_map/ppermute | solution.py:256
  24.8 3.0 %collective-permute-start.9 = (bf16[20,64,128]{2,1,0:T(8,128)(2,1)S(1)}, bf16[20,64,128]{2,1,0:T(8,128)(2,1)S(1)}, u32[]{:S(2)}, u32[]{:S(2)}) collective-permute-start(bf16[20,64,128]{2,1,0:T(8,128)(2,1)S(1)} %slice.6.refs_5_), channel_id=1, source_target_pairs={{0,16},{8,24},{16,0},{24,8},{1,17},{9,25},{17,1},{25,9},{2,18},{10... | collective-permute-start | bytes 983048 | tf_op jit(solution)/shard_map/ppermute | solution.py:256
  27.8 1.2 collective-permute-start.8
  29.0 0.8 collective-permute-start.7
  29.8 3.9 %collective-permute-start.5 = (bf16[20,64,128]{2,1,0:T(8,128)(2,1)}, bf16[20,64,128]{2,1,0:T(8,128)(2,1)S(1)}, u32[]{:S(2)}, u32[]{:S(2)}) collective-permute-start(bf16[20,64,128]{2,1,0:T(8,128)(2,1)} %get-tuple-element.70), channel_id=1, source_target_pairs={{0,1},{32,35},{1,2},{33,32},{2,3},{34,33},{3,0},{35,34},{4,5},{36,... | collective-permute-start | bytes 983048 | tf_op jit(solution)/shard_map/ppermute | solution.py:265
  33.7 2.5 %collective-permute-start.6 = (bf16[10,64,128]{2,1,0:T(8,128)(2,1)}, bf16[10,64,128]{2,1,0:T(8,128)(2,1)S(1)}, u32[]{:S(2)}, u32[]{:S(2)}) collective-permute-start(bf16[10,64,128]{2,1,0:T(8,128)(2,1)} %get-tuple-element.71), channel_id=1, source_target_pairs={{0,34},{32,2},{1,35},{33,3},{2,32},{34,0},{3,33},{35,1},{4,38},{36... | collective-permute-start | bytes 491528 | tf_op jit(solution)/shard_map/ppermute | solution.py:266
  36.2 15.7 %collective-permute-done.6 = bf16[10,64,128]{2,1,0:T(8,128)(2,1)S(1)} collective-permute-done((bf16[10,64,128]{2,1,0:T(8,128)(2,1)}, bf16[10,64,128]{2,1,0:T(8,128)(2,1)S(1)}, u32[]{:S(2)}, u32[]{:S(2)}) %collective-permute-start.6) | collective-permute-done | bytes 163872 | tf_op jit(solution)/shard_map/ppermute | solution.py:266
  51.9 1.1 pad_maximum_fusion
  53.0 0.1 collective-permute-start.14
  53.1 1.0 collective-permute-start.13
  54.1 2.3 %collective-permute-start.12 = (bf16[20,64,128]{2,1,0:T(8,128)(2,1)S(1)}, bf16[20,64,128]{2,1,0:T(8,128)(2,1)S(1)}, u32[]{:S(2)}, u32[]{:S(2)}) collective-permute-start(bf16[20,64,128]{2,1,0:T(8,128)(2,1)S(1)} %collective-permute-done.5.refs_9_), channel_id=1, source_target_pairs={{0,24},{8,0},{16,8},{24,16},{1,25},{9,1},{17,9},{25,17},{2,26},{10... | collective-permute-start | bytes 983048 | tf_op jit(solution)/shard_map/ppermute | solution.py:256
  56.6 16.8 %collective-permute-done.10.refs_2_.refs_25_.refs_3_ = bf16[20,64,128]{2,1,0:T(8,128)(2,1)S(1)} collective-permute-done((bf16[20,64,128]{2,1,0:T(8,128)(2,1)S(1)}, bf16[20,64,128]{2,1,0:T(8,128)(2,1)S(1)}, u32[]{:S(2)}, u32[]{:S(2)}) %collective-permute-start.10) | collective-permute-done | bytes 327712 | tf_op jit(solution)/shard_map/ppermute | solution.py:271
  73.8 0.1 collective-permute-start.19
  73.9 0.3 collective-permute-start.18
  74.2 2.1 %collective-permute-start.17 = (bf16[20,64,128]{2,1,0:T(8,128)(2,1)S(1)}, bf16[20,64,128]{2,1,0:T(8,128)(2,1)S(1)}, u32[]{:S(2)}, u32[]{:S(2)}) collective-permute-start(bf16[20,64,128]{2,1,0:T(8,128)(2,1)S(1)} %collective-permute-done.10.refs_2_.refs_25_.refs_3_), channel_id=1, source_target_pairs={{0,16},{8,24},{16,0},{24,8},{1,17},{9,25},{17,1},{25,9},{2,18},{10... | collective-permute-start | bytes 983048 | tf_op jit(solution)/shard_map/ppermute | solution.py:256
  76.3 2.3 %collective-permute-start.16 = (bf16[20,64,128]{2,1,0:T(8,128)(2,1)S(1)}, bf16[20,64,128]{2,1,0:T(8,128)(2,1)S(1)}, u32[]{:S(2)}, u32[]{:S(2)}) collective-permute-start(bf16[20,64,128]{2,1,0:T(8,128)(2,1)S(1)} %collective-permute-done.10.refs_2_.refs_25_.refs_3_), channel_id=1, source_target_pairs={{0,24},{8,0},{16,8},{24,16},{1,25},{9,1},{17,9},{25,17},{2,26},{10... | collective-permute-start | bytes 983048 | tf_op jit(solution)/shard_map/ppermute | solution.py:256
  78.7 0.2 collective-permute-done.19.refs_17_.refs_18_.refs_19_.refs_20_.refs_21_.refs_22_.refs_23_.refs_24_
  78.8 7.2 %early.1.refs_1_ = bf16[5,1,544,128]{3,2,1,0:T(8,128)(2,1)S(1)} custom-call(bf16[4,10,64,128]{3,2,1,0:T(8,128)(2,1)S(1)} %pad_maximum_fusion.1.refs_0_, bf16[20,64,128]{2,1,0:T(8,128)(2,1)S(1)} %copy-done, bf16[20,64,128]{2,1,0:T(8,128)(2,1)S(1)} %collective-permute-done.2.refs_2_, bf16[20,64,128]{2,1,0:T(8,128)(2,1)S(1)} %collective-permute-done.3.refs_3_, ...), custom_call_target="tpu_custom_call" | custom-call | flops 4026531840 | bytes 7864320 | tf_op jit(solution)/shard_map/early/pallas_call | solution.py:227
  86.0 0.4 collective-permute-done.17.refs_5_.refs_28_.refs_6_
  86.4 6.5 %collective-permute-done.16.refs_4_.refs_27_.refs_5_ = bf16[20,64,128]{2,1,0:T(8,128)(2,1)S(1)} collective-permute-done((bf16[20,64,128]{2,1,0:T(8,128)(2,1)S(1)}, bf16[20,64,128]{2,1,0:T(8,128)(2,1)S(1)}, u32[]{:S(2)}, u32[]{:S(2)}) %collective-permute-start.16) | collective-permute-done | bytes 327712 | tf_op jit(solution)/shard_map/ppermute | solution.py:256
  92.9 0.5 collective-permute-start.21
  93.5 0.4 collective-permute-start.23
  93.9 2.9 %early_far.1.refs_1_ = bf16[2,1,544,128]{3,2,1,0:T(8,128)(2,1)S(1)} custom-call(bf16[4,10,64,128]{3,2,1,0:T(8,128)(2,1)S(1)} %collective-permute-done.18.refs_0_, bf16[20,64,128]{2,1,0:T(8,128)(2,1)S(1)} %copy-done, bf16[20,64,128]{2,1,0:T(8,128)(2,1)S(1)} %collective-permute-done.2.refs_2_, bf16[20,64,128]{2,1,0:T(8,128)(2,1)S(1)} %collective-permute-done.3.refs_3_, ...), custom_call_target="tpu_custom_call" | custom-call | flops 1610612736 | bytes 3145728 | tf_op jit(solution)/shard_map/early_far/pallas_call | solution.py:227
  96.9 1.8 %far.2 = bf16[2,1,544,128]{3,2,1,0:T(8,128)(2,1)S(1)} custom-call(bf16[4,10,64,128]{3,2,1,0:T(8,128)(2,1)S(1)} %collective-permute-done.18.refs_0_, bf16[2,1,544,128]{3,2,1,0:T(8,128)(2,1)S(1)} %early_far.1.refs_1_, bf16[20,64,128]{2,1,0:T(8,128)(2,1)S(1)} %collective-permute-done.10.refs_2_.refs_25_.refs_3_, ...), custom_call_target="tpu_custom_call" | custom-call | flops 536870912 | bytes 1048576 | tf_op jit(solution)/shard_map/far/pallas_call | solution.py:227
  98.6 1.8 %collective-permute-start.24 = (bf16[2,1,544,128]{3,2,1,0:T(8,128)(2,1)S(1)}, bf16[2,1,544,128]{3,2,1,0:T(8,128)(2,1)S(1)}, u32[]{:S(2)}, u32[]{:S(2)}) collective-permute-start(bf16[2,1,544,128]{3,2,1,0:T(8,128)(2,1)S(1)} %far.2), channel_id=1, source_target_pairs={{0,32},{32,0},{1,33},{33,1},{2,34},{34,2},{3,35},{35,3},{4,36},{36... | collective-permute-start | bytes 835592 | tf_op jit(solution)/shard_map/ppermute | solution.py:296
  100.4 5.7 %far.3 = bf16[3,1,544,128]{3,2,1,0:T(8,128)(2,1)S(1)} custom-call(bf16[4,10,64,128]{3,2,1,0:T(8,128)(2,1)S(1)} %collective-permute-done.18.refs_0_, bf16[20,64,128]{2,1,0:T(8,128)(2,1)S(1)} %copy-done, bf16[20,64,128]{2,1,0:T(8,128)(2,1)S(1)} %collective-permute-done.2.refs_2_, bf16[20,64,128]{2,1,0:T(8,128)(2,1)S(1)} %collective-permute-done.3.refs_3_, ...), custom_call_target="tpu_custom_call" | custom-call | flops 3221225472 | bytes 6291456 | tf_op jit(solution)/shard_map/far/pallas_call | solution.py:227
  106.1 1.2 collective-permute-done.24.refs_2_
  107.4 1.7 %collective-permute-start.25 = (bf16[3,1,544,128]{3,2,1,0:T(8,128)(2,1)S(1)}, bf16[3,1,544,128]{3,2,1,0:T(8,128)(2,1)S(1)}, u32[]{:S(2)}, u32[]{:S(2)}) collective-permute-start(bf16[3,1,544,128]{3,2,1,0:T(8,128)(2,1)S(1)} %far.3), channel_id=1, source_target_pairs={{0,32},{32,0},{1,33},{33,1},{2,34},{34,2},{3,35},{35,3},{4,36},{36... | collective-permute-start | bytes 1253384 | tf_op jit(solution)/shard_map/ppermute | solution.py:296
  109.1 1.9 %near.2 = (bf16[2,2,64,128]{3,2,1,0:T(8,128)(2,1)S(1)}, bf16[2,2,64,128]{3,2,1,0:T(8,128)(2,1)S(1)}, bf16[2,2,64,128]{3,2,1,0:T(8,128)(2,1)S(1)}, bf16[2,2,64,128]{3,2,1,0:T(8,128)(2,1)S(1)}) custom-call(bf16[4,10,64,128]{3,2,1,0:T(8,128)(2,1)S(1)} %pad_maximum_fusion.1.refs_0_, bf16[5,1,544,128]{3,2,1,0:T(8,128)(2,1)S(1)} %early.1.refs_1_, ...), custom_call_target="tpu_custom_call" | custom-call | flops 536870912 | bytes 1048576 | tf_op jit(solution)/shard_map/near/pallas_call | solution.py:227
  111.0 1.0 collective-permute-start.27
  112.0 1.0 collective-permute-start.26
  113.0 5.7 %collective-permute-start.28 = (bf16[2,2,64,128]{3,2,1,0:T(8,128)(2,1)S(1)}, bf16[2,2,64,128]{3,2,1,0:T(8,128)(2,1)S(1)}, u32[]{:S(2)}, u32[]{:S(2)}) collective-permute-start(bf16[2,2,64,128]{3,2,1,0:T(8,128)(2,1)S(1)} %get-tuple-element.120), channel_id=1, source_target_pairs={{0,34},{32,2},{1,35},{33,3},{2,32},{34,0},{3,33},{35,1},{4,38},{36... | collective-permute-start | bytes 196616 | tf_op jit(solution)/shard_map/ppermute | solution.py:304
  118.7 1.5 %collective-permute-done.25.refs_2_ = bf16[3,1,544,128]{3,2,1,0:T(8,128)(2,1)S(1)} collective-permute-done((bf16[3,1,544,128]{3,2,1,0:T(8,128)(2,1)S(1)}, bf16[3,1,544,128]{3,2,1,0:T(8,128)(2,1)S(1)}, u32[]{:S(2)}, u32[]{:S(2)}) %collective-permute-start.25) | collective-permute-done | bytes 417824 | tf_op jit(solution)/shard_map/ppermute | solution.py:296
  120.3 2.8 %near.3 = (bf16[3,2,64,128]{3,2,1,0:T(8,128)(2,1)S(1)}, bf16[3,2,64,128]{3,2,1,0:T(8,128)(2,1)S(1)}, bf16[3,2,64,128]{3,2,1,0:T(8,128)(2,1)S(1)}, bf16[3,2,64,128]{3,2,1,0:T(8,128)(2,1)S(1)}) custom-call(bf16[4,10,64,128]{3,2,1,0:T(8,128)(2,1)S(1)} %pad_maximum_fusion.1.refs_0_, bf16[5,1,544,128]{3,2,1,0:T(8,128)(2,1)S(1)} %early.1.refs_1_, ...), custom_call_target="tpu_custom_call" | custom-call | flops 805306368 | bytes 1572864 | tf_op jit(solution)/shard_map/near/pallas_call | solution.py:227
  123.1 0.6 unpack.2
  123.7 1.1 collective-permute-start.29
  124.8 4.7 %collective-permute-start.30 = (bf16[3,2,64,128]{3,2,1,0:T(8,128)(2,1)S(1)}, bf16[3,2,64,128]{3,2,1,0:T(8,128)(2,1)S(1)}, u32[]{:S(2)}, u32[]{:S(2)}) collective-permute-start(bf16[3,2,64,128]{3,2,1,0:T(8,128)(2,1)S(1)} %get-tuple-element.124), channel_id=1, source_target_pairs={{0,3},{32,33},{1,0},{33,34},{2,1},{34,35},{3,2},{35,32},{4,7},{36,... | collective-permute-start | bytes 294920 | tf_op jit(solution)/shard_map/ppermute | solution.py:304
  129.6 3.5 %collective-permute-done.30.refs_2_ = bf16[3,2,64,128]{3,2,1,0:T(8,128)(2,1)S(1)} collective-permute-done((bf16[3,2,64,128]{3,2,1,0:T(8,128)(2,1)S(1)}, bf16[3,2,64,128]{3,2,1,0:T(8,128)(2,1)S(1)}, u32[]{:S(2)}, u32[]{:S(2)}) %collective-permute-start.30) | collective-permute-done | bytes 98336 | tf_op jit(solution)/shard_map/ppermute | solution.py:304
  133.1 5.2 %collective-permute-done.31.refs_3_ = bf16[3,2,64,128]{3,2,1,0:T(8,128)(2,1)S(1)} collective-permute-done((bf16[3,2,64,128]{3,2,1,0:T(8,128)(2,1)S(1)}, bf16[3,2,64,128]{3,2,1,0:T(8,128)(2,1)S(1)}, u32[]{:S(2)}, u32[]{:S(2)}) %collective-permute-start.31) | collective-permute-done | bytes 98336 | tf_op jit(solution)/shard_map/ppermute | solution.py:304
  138.2 1.5 %unpack.3 = (bf16[64,2560]{1,0:T(8,128)(2,1)}, bf16[64,2560]{1,0:T(8,128)(2,1)}) custom-call(s32[4]{0:T(128)S(1)} %copy-done.1, bf16[3,2,64,128]{3,2,1,0:T(8,128)(2,1)S(1)} %get-tuple-element.113.refs_0_, bf16[3,2,64,128]{3,2,1,0:T(8,128)(2,1)S(1)} %collective-permute-done.29.refs_1_, bf16[3,2,64,128]{3,2,1,0:T(8,128)(2,1)S(1)} %collective-permute-done.30.refs_2_, ...), custom_call_target="tpu_custom_call" | custom-call | tf_op jit(solution)/shard_map/unpack/pallas_call | solution.py:94
  (46 shorter events, 0.6 us)
Async XLA Ops:
  4.7 51.8 %copy-start.3 = (bf16[20,64,128]{2,1,0:T(8,128)(2,1)S(1)}, bf16[20,64,128]{2,1,0:T(8,128)(2,1)}, u32[]{:S(2)}) copy-start(bf16[20,64,128]{2,1,0:T(8,128)(2,1)} %get-tuple-element.78) | copy-start | bytes 983044
  4.7 51.8 %copy-start.2 = (bf16[10,64,128]{2,1,0:T(8,128)(2,1)S(1)}, bf16[10,64,128]{2,1,0:T(8,128)(2,1)}, u32[]{:S(2)}) copy-start(bf16[10,64,128]{2,1,0:T(8,128)(2,1)} %get-tuple-element.88) | copy-start | bytes 491524
  4.7 20.0 %collective-permute-start = (bf16[30,64,128]{2,1,0:T(8,128)(2,1)}, bf16[30,64,128]{2,1,0:T(8,128)(2,1)S(1)}, u32[]{:S(2)}, u32[]{:S(2)}) collective-permute-start(bf16[30,64,128]{2,1,0:T(8,128)(2,1)} %get-tuple-element.64), channel_id=1, source_target_pairs={{0,35},{32,1},{1,32},{33,2},{2,33},{34,3},{3,34},{35,0},{4,39},{36... | collective-permute-start | bytes 1474568 | tf_op jit(solution)/shard_map/ppermute | solution.py:258
  6.7 13.1 %collective-permute-start.4 = (bf16[20,64,128]{2,1,0:T(8,128)(2,1)}, bf16[20,64,128]{2,1,0:T(8,128)(2,1)S(1)}, u32[]{:S(2)}, u32[]{:S(2)}) collective-permute-start(bf16[20,64,128]{2,1,0:T(8,128)(2,1)} %get-tuple-element.84.refs_1_), channel_id=1, source_target_pairs={{0,16},{8,24},{16,0},{24,8},{1,17},{9,25},{17,1},{25,9},{2,18},{10... | collective-permute-start | bytes 983048 | tf_op jit(solution)/shard_map/ppermute | solution.py:256
  9.7 15.0 %collective-permute-start.3 = (bf16[20,64,128]{2,1,0:T(8,128)(2,1)}, bf16[20,64,128]{2,1,0:T(8,128)(2,1)S(1)}, u32[]{:S(2)}, u32[]{:S(2)}) collective-permute-start(bf16[20,64,128]{2,1,0:T(8,128)(2,1)} %get-tuple-element.84.refs_1_), channel_id=1, source_target_pairs={{0,24},{8,0},{16,8},{24,16},{1,25},{9,1},{17,9},{25,17},{2,26},{10... | collective-permute-start | bytes 983048 | tf_op jit(solution)/shard_map/ppermute | solution.py:256
  10.9 13.9 %collective-permute-start.2 = (bf16[20,64,128]{2,1,0:T(8,128)(2,1)}, bf16[20,64,128]{2,1,0:T(8,128)(2,1)S(1)}, u32[]{:S(2)}, u32[]{:S(2)}) collective-permute-start(bf16[20,64,128]{2,1,0:T(8,128)(2,1)} %get-tuple-element.84.refs_1_), channel_id=1, source_target_pairs={{0,8},{8,16},{16,24},{24,0},{1,9},{9,17},{17,25},{25,1},{2,10},{10... | collective-permute-start | bytes 983048 | tf_op jit(solution)/shard_map/ppermute | solution.py:256
  11.8 8.0 %collective-permute-start.1 = (bf16[10,64,128]{2,1,0:T(8,128)(2,1)}, bf16[10,64,128]{2,1,0:T(8,128)(2,1)S(1)}, u32[]{:S(2)}, u32[]{:S(2)}) collective-permute-start(bf16[10,64,128]{2,1,0:T(8,128)(2,1)} %get-tuple-element.65), channel_id=1, source_target_pairs={{0,1},{32,35},{1,2},{33,32},{2,3},{34,33},{3,0},{35,34},{4,5},{36,... | collective-permute-start | bytes 491528 | tf_op jit(solution)/shard_map/ppermute | solution.py:259
  24.8 27.1 %collective-permute-start.9 = (bf16[20,64,128]{2,1,0:T(8,128)(2,1)S(1)}, bf16[20,64,128]{2,1,0:T(8,128)(2,1)S(1)}, u32[]{:S(2)}, u32[]{:S(2)}) collective-permute-start(bf16[20,64,128]{2,1,0:T(8,128)(2,1)S(1)} %slice.6.refs_5_), channel_id=1, source_target_pairs={{0,16},{8,24},{16,0},{24,8},{1,17},{9,25},{17,1},{25,9},{2,18},{10... | collective-permute-start | bytes 983048 | tf_op jit(solution)/shard_map/ppermute | solution.py:256
  27.8 24.1 %collective-permute-start.8 = (bf16[20,64,128]{2,1,0:T(8,128)(2,1)S(1)}, bf16[20,64,128]{2,1,0:T(8,128)(2,1)S(1)}, u32[]{:S(2)}, u32[]{:S(2)}) collective-permute-start(bf16[20,64,128]{2,1,0:T(8,128)(2,1)S(1)} %slice.6.refs_5_), channel_id=1, source_target_pairs={{0,24},{8,0},{16,8},{24,16},{1,25},{9,1},{17,9},{25,17},{2,26},{10... | collective-permute-start | bytes 983048 | tf_op jit(solution)/shard_map/ppermute | solution.py:256
  29.0 22.9 %collective-permute-start.7 = (bf16[20,64,128]{2,1,0:T(8,128)(2,1)S(1)}, bf16[20,64,128]{2,1,0:T(8,128)(2,1)S(1)}, u32[]{:S(2)}, u32[]{:S(2)}) collective-permute-start(bf16[20,64,128]{2,1,0:T(8,128)(2,1)S(1)} %slice.6.refs_5_), channel_id=1, source_target_pairs={{0,8},{8,16},{16,24},{24,0},{1,9},{9,17},{17,25},{25,1},{2,10},{10... | collective-permute-start | bytes 983048 | tf_op jit(solution)/shard_map/ppermute | solution.py:256
  29.8 22.1 %collective-permute-start.5 = (bf16[20,64,128]{2,1,0:T(8,128)(2,1)}, bf16[20,64,128]{2,1,0:T(8,128)(2,1)S(1)}, u32[]{:S(2)}, u32[]{:S(2)}) collective-permute-start(bf16[20,64,128]{2,1,0:T(8,128)(2,1)} %get-tuple-element.70), channel_id=1, source_target_pairs={{0,1},{32,35},{1,2},{33,32},{2,3},{34,33},{3,0},{35,34},{4,5},{36,... | collective-permute-start | bytes 983048 | tf_op jit(solution)/shard_map/ppermute | solution.py:265
  33.7 18.2 %collective-permute-start.6 = (bf16[10,64,128]{2,1,0:T(8,128)(2,1)}, bf16[10,64,128]{2,1,0:T(8,128)(2,1)S(1)}, u32[]{:S(2)}, u32[]{:S(2)}) collective-permute-start(bf16[10,64,128]{2,1,0:T(8,128)(2,1)} %get-tuple-element.71), channel_id=1, source_target_pairs={{0,34},{32,2},{1,35},{33,3},{2,32},{34,0},{3,33},{35,1},{4,38},{36... | collective-permute-start | bytes 491528 | tf_op jit(solution)/shard_map/ppermute | solution.py:266
  53.0 20.4 %collective-permute-start.14 = (bf16[80,64,128]{2,1,0:T(8,128)(2,1)S(1)}, bf16[80,64,128]{2,1,0:T(8,128)(2,1)S(1)}, u32[]{:S(2)}, u32[]{:S(2)}) collective-permute-start(bf16[80,64,128]{2,1,0:T(8,128)(2,1)S(1)} %pad_maximum_fusion), channel_id=1, source_target_pairs={{0,4},{4,0},{1,5},{5,1},{2,6},{6,2},{3,7},{7,3},{8,12},{12,8},{9,1... | collective-permute-start | bytes 3932168 | tf_op jit(solution)/shard_map/ppermute | solution.py:273
  53.1 20.3 %collective-permute-start.13 = (bf16[20,64,128]{2,1,0:T(8,128)(2,1)S(1)}, bf16[20,64,128]{2,1,0:T(8,128)(2,1)S(1)}, u32[]{:S(2)}, u32[]{:S(2)}) collective-permute-start(bf16[20,64,128]{2,1,0:T(8,128)(2,1)S(1)} %collective-permute-done.5.refs_9_), channel_id=1, source_target_pairs={{0,16},{8,24},{16,0},{24,8},{1,17},{9,25},{17,1},{25,9},{2,18},{10... | collective-permute-start | bytes 983048 | tf_op jit(solution)/shard_map/ppermute | solution.py:256
  54.1 19.3 %collective-permute-start.12 = (bf16[20,64,128]{2,1,0:T(8,128)(2,1)S(1)}, bf16[20,64,128]{2,1,0:T(8,128)(2,1)S(1)}, u32[]{:S(2)}, u32[]{:S(2)}) collective-permute-start(bf16[20,64,128]{2,1,0:T(8,128)(2,1)S(1)} %collective-permute-done.5.refs_9_), channel_id=1, source_target_pairs={{0,24},{8,0},{16,8},{24,16},{1,25},{9,1},{17,9},{25,17},{2,26},{10... | collective-permute-start | bytes 983048 | tf_op jit(solution)/shard_map/ppermute | solution.py:256
  56.5 17.0 %collective-permute-start.11 = (bf16[20,64,128]{2,1,0:T(8,128)(2,1)S(1)}, bf16[20,64,128]{2,1,0:T(8,128)(2,1)S(1)}, u32[]{:S(2)}, u32[]{:S(2)}) collective-permute-start(bf16[20,64,128]{2,1,0:T(8,128)(2,1)S(1)} %collective-permute-done.5.refs_9_), channel_id=1, source_target_pairs={{0,8},{8,16},{16,24},{24,0},{1,9},{9,17},{17,25},{25,1},{2,10},{10... | collective-permute-start | bytes 983048 | tf_op jit(solution)/shard_map/ppermute | solution.py:256
  56.5 16.9 %collective-permute-start.10 = (bf16[20,64,128]{2,1,0:T(8,128)(2,1)S(1)}, bf16[20,64,128]{2,1,0:T(8,128)(2,1)S(1)}, u32[]{:S(2)}, u32[]{:S(2)}) collective-permute-start(bf16[20,64,128]{2,1,0:T(8,128)(2,1)S(1)} %copy-done.3), channel_id=1, source_target_pairs={{0,34},{32,2},{1,35},{33,3},{2,32},{34,0},{3,33},{35,1},{4,38},{36... | collective-permute-start | bytes 983048 | tf_op jit(solution)/shard_map/ppermute | solution.py:271
  56.6 22.2 %copy-start = (bf16[20,64,128]{2,1,0:T(8,128)(2,1)S(1)}, bf16[20,64,128]{2,1,0:T(8,128)(2,1)}, u32[]{:S(2)}) copy-start(bf16[20,64,128]{2,1,0:T(8,128)(2,1)} %get-tuple-element.84.refs_1_) | copy-start | bytes 983044
  73.8 5.0 %collective-permute-start.19 = (bf16[160,64,128]{2,1,0:T(8,128)(2,1)S(1)}, bf16[160,64,128]{2,1,0:T(8,128)(2,1)S(1)}, u32[]{:S(2)}, u32[]{:S(2)}) collective-permute-start(bf16[160,64,128]{2,1,0:T(8,128)(2,1)S(1)} %constant_dynamic-update-slice_fusion), channel_id=1, source_target_pairs={{0,4},{4,0},{1,5},{5,1},{2,6},{6,2},{3,7},{7,3},{8,12},{12,8},{9,1... | collective-permute-start | bytes 7864328 | tf_op jit(solution)/shard_map/ppermute | solution.py:280
  73.9 19.0 %collective-permute-start.18 = (bf16[4,10,64,128]{3,2,1,0:T(8,128)(2,1)S(1)}, bf16[4,10,64,128]{3,2,1,0:T(8,128)(2,1)S(1)}, u32[]{:S(2)}, u32[]{:S(2)}) collective-permute-start(bf16[4,10,64,128]{3,2,1,0:T(8,128)(2,1)S(1)} %pad_maximum_fusion.1.refs_0_), channel_id=1, source_target_pairs={{0,32},{32,0},{1,33},{33,1},{2,34},{34,2},{3,35},{35,3},{4,36},{36... | collective-permute-start | bytes 1966088 | tf_op jit(solution)/shard_map/ppermute | solution.py:279
  74.2 12.2 %collective-permute-start.17 = (bf16[20,64,128]{2,1,0:T(8,128)(2,1)S(1)}, bf16[20,64,128]{2,1,0:T(8,128)(2,1)S(1)}, u32[]{:S(2)}, u32[]{:S(2)}) collective-permute-start(bf16[20,64,128]{2,1,0:T(8,128)(2,1)S(1)} %collective-permute-done.10.refs_2_.refs_25_.refs_3_), channel_id=1, source_target_pairs={{0,16},{8,24},{16,0},{24,8},{1,17},{9,25},{17,1},{25,9},{2,18},{10... | collective-permute-start | bytes 983048 | tf_op jit(solution)/shard_map/ppermute | solution.py:256
  76.3 16.6 %collective-permute-start.16 = (bf16[20,64,128]{2,1,0:T(8,128)(2,1)S(1)}, bf16[20,64,128]{2,1,0:T(8,128)(2,1)S(1)}, u32[]{:S(2)}, u32[]{:S(2)}) collective-permute-start(bf16[20,64,128]{2,1,0:T(8,128)(2,1)S(1)} %collective-permute-done.10.refs_2_.refs_25_.refs_3_), channel_id=1, source_target_pairs={{0,24},{8,0},{16,8},{24,16},{1,25},{9,1},{17,9},{25,17},{2,26},{10... | collective-permute-start | bytes 983048 | tf_op jit(solution)/shard_map/ppermute | solution.py:256
  78.7 14.2 %collective-permute-start.15 = (bf16[20,64,128]{2,1,0:T(8,128)(2,1)S(1)}, bf16[20,64,128]{2,1,0:T(8,128)(2,1)S(1)}, u32[]{:S(2)}, u32[]{:S(2)}) collective-permute-start(bf16[20,64,128]{2,1,0:T(8,128)(2,1)S(1)} %collective-permute-done.10.refs_2_.refs_25_.refs_3_), channel_id=1, source_target_pairs={{0,8},{8,16},{16,24},{24,0},{1,9},{9,17},{17,25},{25,1},{2,10},{10... | collective-permute-start | bytes 983048 | tf_op jit(solution)/shard_map/ppermute | solution.py:256
  92.9 3.9 %collective-permute-start.20 = (bf16[20,64,128]{2,1,0:T(8,128)(2,1)S(1)}, bf16[20,64,128]{2,1,0:T(8,128)(2,1)S(1)}, u32[]{:S(2)}, u32[]{:S(2)}) collective-permute-start(bf16[20,64,128]{2,1,0:T(8,128)(2,1)S(1)} %collective-permute-done.10.refs_2_.refs_25_.refs_3_), channel_id=1, source_target_pairs={{0,4},{4,0},{1,5},{5,1},{2,6},{6,2},{3,7},{7,3},{8,12},{12,8},{9,1... | collective-permute-start | bytes 983048 | tf_op jit(solution)/shard_map/ppermute | solution.py:257
  92.9 3.9 %collective-permute-start.21 = (bf16[20,64,128]{2,1,0:T(8,128)(2,1)S(1)}, bf16[20,64,128]{2,1,0:T(8,128)(2,1)S(1)}, u32[]{:S(2)}, u32[]{:S(2)}) collective-permute-start(bf16[20,64,128]{2,1,0:T(8,128)(2,1)S(1)} %collective-permute-done.15.refs_3_.refs_26_.refs_4_), channel_id=1, source_target_pairs={{0,4},{4,0},{1,5},{5,1},{2,6},{6,2},{3,7},{7,3},{8,12},{12,8},{9,1... | collective-permute-start | bytes 983048 | tf_op jit(solution)/shard_map/ppermute | solution.py:257
  93.4 3.4 %collective-permute-start.22 = (bf16[20,64,128]{2,1,0:T(8,128)(2,1)S(1)}, bf16[20,64,128]{2,1,0:T(8,128)(2,1)S(1)}, u32[]{:S(2)}, u32[]{:S(2)}) collective-permute-start(bf16[20,64,128]{2,1,0:T(8,128)(2,1)S(1)} %collective-permute-done.16.refs_4_.refs_27_.refs_5_), channel_id=1, source_target_pairs={{0,4},{4,0},{1,5},{5,1},{2,6},{6,2},{3,7},{7,3},{8,12},{12,8},{9,1... | collective-permute-start | bytes 983048 | tf_op jit(solution)/shard_map/ppermute | solution.py:257
  93.5 3.4 %collective-permute-start.23 = (bf16[20,64,128]{2,1,0:T(8,128)(2,1)S(1)}, bf16[20,64,128]{2,1,0:T(8,128)(2,1)S(1)}, u32[]{:S(2)}, u32[]{:S(2)}) collective-permute-start(bf16[20,64,128]{2,1,0:T(8,128)(2,1)S(1)} %collective-permute-done.17.refs_5_.refs_28_.refs_6_), channel_id=1, source_target_pairs={{0,4},{4,0},{1,5},{5,1},{2,6},{6,2},{3,7},{7,3},{8,12},{12,8},{9,1... | collective-permute-start | bytes 983048 | tf_op jit(solution)/shard_map/ppermute | solution.py:257
  98.6 8.7 %collective-permute-start.24 = (bf16[2,1,544,128]{3,2,1,0:T(8,128)(2,1)S(1)}, bf16[2,1,544,128]{3,2,1,0:T(8,128)(2,1)S(1)}, u32[]{:S(2)}, u32[]{:S(2)}) collective-permute-start(bf16[2,1,544,128]{3,2,1,0:T(8,128)(2,1)S(1)} %far.2), channel_id=1, source_target_pairs={{0,32},{32,0},{1,33},{33,1},{2,34},{34,2},{3,35},{35,3},{4,36},{36... | collective-permute-start | bytes 835592 | tf_op jit(solution)/shard_map/ppermute | solution.py:296
  107.4 12.9 %collective-permute-start.25 = (bf16[3,1,544,128]{3,2,1,0:T(8,128)(2,1)S(1)}, bf16[3,1,544,128]{3,2,1,0:T(8,128)(2,1)S(1)}, u32[]{:S(2)}, u32[]{:S(2)}) collective-permute-start(bf16[3,1,544,128]{3,2,1,0:T(8,128)(2,1)S(1)} %far.3), channel_id=1, source_target_pairs={{0,32},{32,0},{1,33},{33,1},{2,34},{34,2},{3,35},{35,3},{4,36},{36... | collective-permute-start | bytes 1253384 | tf_op jit(solution)/shard_map/ppermute | solution.py:296
  111.0 12.1 %copy-start.1 = (s32[4]{0:T(128)S(1)}, s32[4]{0:T(128)}, u32[]{:S(2)}) copy-start(s32[4]{0:T(128)} %fusion.offs) | copy-start | bytes 52
  111.0 12.1 %collective-permute-start.27 = (bf16[2,2,64,128]{3,2,1,0:T(8,128)(2,1)S(1)}, bf16[2,2,64,128]{3,2,1,0:T(8,128)(2,1)S(1)}, u32[]{:S(2)}, u32[]{:S(2)}) collective-permute-start(bf16[2,2,64,128]{3,2,1,0:T(8,128)(2,1)S(1)} %get-tuple-element.119), channel_id=1, source_target_pairs={{0,3},{32,33},{1,0},{33,34},{2,1},{34,35},{3,2},{35,32},{4,7},{36,... | collective-permute-start | bytes 196616 | tf_op jit(solution)/shard_map/ppermute | solution.py:304
  112.0 11.1 %collective-permute-start.26 = (bf16[2,2,64,128]{3,2,1,0:T(8,128)(2,1)S(1)}, bf16[2,2,64,128]{3,2,1,0:T(8,128)(2,1)S(1)}, u32[]{:S(2)}, u32[]{:S(2)}) collective-permute-start(bf16[2,2,64,128]{3,2,1,0:T(8,128)(2,1)S(1)} %get-tuple-element.118), channel_id=1, source_target_pairs={{0,35},{32,1},{1,32},{33,2},{2,33},{34,3},{3,34},{35,0},{4,39},{36... | collective-permute-start | bytes 196616 | tf_op jit(solution)/shard_map/ppermute | solution.py:304
  113.0 10.1 %collective-permute-start.28 = (bf16[2,2,64,128]{3,2,1,0:T(8,128)(2,1)S(1)}, bf16[2,2,64,128]{3,2,1,0:T(8,128)(2,1)S(1)}, u32[]{:S(2)}, u32[]{:S(2)}) collective-permute-start(bf16[2,2,64,128]{3,2,1,0:T(8,128)(2,1)S(1)} %get-tuple-element.120), channel_id=1, source_target_pairs={{0,34},{32,2},{1,35},{33,3},{2,32},{34,0},{3,33},{35,1},{4,38},{36... | collective-permute-start | bytes 196616 | tf_op jit(solution)/shard_map/ppermute | solution.py:304
  123.7 5.8 %collective-permute-start.29 = (bf16[3,2,64,128]{3,2,1,0:T(8,128)(2,1)S(1)}, bf16[3,2,64,128]{3,2,1,0:T(8,128)(2,1)S(1)}, u32[]{:S(2)}, u32[]{:S(2)}) collective-permute-start(bf16[3,2,64,128]{3,2,1,0:T(8,128)(2,1)S(1)} %get-tuple-element.123), channel_id=1, source_target_pairs={{0,35},{32,1},{1,32},{33,2},{2,33},{34,3},{3,34},{35,0},{4,39},{36... | collective-permute-start | bytes 294920 | tf_op jit(solution)/shard_map/ppermute | solution.py:304
  124.8 8.2 %collective-permute-start.30 = (bf16[3,2,64,128]{3,2,1,0:T(8,128)(2,1)S(1)}, bf16[3,2,64,128]{3,2,1,0:T(8,128)(2,1)S(1)}, u32[]{:S(2)}, u32[]{:S(2)}) collective-permute-start(bf16[3,2,64,128]{3,2,1,0:T(8,128)(2,1)S(1)} %get-tuple-element.124), channel_id=1, source_target_pairs={{0,3},{32,33},{1,0},{33,34},{2,1},{34,35},{3,2},{35,32},{4,7},{36,... | collective-permute-start | bytes 294920 | tf_op jit(solution)/shard_map/ppermute | solution.py:304
  129.5 8.7 %collective-permute-start.31 = (bf16[3,2,64,128]{3,2,1,0:T(8,128)(2,1)S(1)}, bf16[3,2,64,128]{3,2,1,0:T(8,128)(2,1)S(1)}, u32[]{:S(2)}, u32[]{:S(2)}) collective-permute-start(bf16[3,2,64,128]{3,2,1,0:T(8,128)(2,1)S(1)} %get-tuple-element.125), channel_id=1, source_target_pairs={{0,34},{32,2},{1,35},{33,3},{2,32},{34,0},{3,33},{35,1},{4,38},{36... | collective-permute-start | bytes 294920 | tf_op jit(solution)/shard_map/ppermute | solution.py:304

commit v4 on v3

--- a/solution.py
+++ b/solution.py
@@ -41,7 +41,15 @@
     return pl.BlockSpec(shape, index_map) if index_map else pl.BlockSpec(memory_space=pltpu.VMEM)
 
 
-def pack_body(offs, *refs):
+def offsets():
+    group, parity = lax.axis_index("zhi"), lax.axis_index("zlo")
+    step = 2 * parity - 1
+    slots = (group, group + step + GROUPS, group - step + GROUPS, group + 2)
+    return [lax.rem(slot, GROUPS) * (HEADS_HERE * HEAD_DIM) for slot in slots]
+
+
+def pack_body(*refs):
+    offs = offsets()
     sources, outs, held, sems = refs[:6], refs[6:-7], refs[-7:-1], refs[-1]
     copies = [pltpu.make_async_copy(a, b, sems.at[i]) for i, (a, b) in enumerate(zip(sources, held))]
     for copy in copies:
@@ -60,20 +68,20 @@
                     outs[4 + slot // 2 + slot // 3][h * 2 + a - 4] = block
 
 
-def pack(offs, arrays):
+def pack(arrays):
     block = lambda count: jax.ShapeDtypeStruct((count, ROWS, HEAD_DIM), jnp.bfloat16)
     return pl.pallas_call(
         pack_body,
         out_shape=[block(KV_BLOCKS), block(KV_BLOCKS + Q_BLOCKS)]
         + [block(KV_BLOCKS)] * 2
         + [block(Q_BLOCKS)] * 3,
-        in_specs=[pl.BlockSpec(memory_space=pltpu.SMEM)] + [pl.BlockSpec(memory_space=pl.ANY)] * 6,
+        in_specs=[pl.BlockSpec(memory_space=pl.ANY)] * 6,
         out_specs=[spec(None)] * 7,
         scratch_shapes=[pltpu.VMEM(arrays[0].shape, jnp.bfloat16)] * 6
         + [pltpu.SemaphoreType.DMA((6,))],
         compiler_params=pltpu.CompilerParams(vmem_limit_bytes=60 * 1024 * 1024),
         name="pack",
-    )(offs, *arrays)
+    )(*arrays)
 
 
 def unpack_body(chunk, offs, *refs):
@@ -246,12 +254,9 @@
 
 
 def per_device(query_rows, key_rows, value_rows, query_tan, key_tan, value_tan):
-    group, parity = lax.axis_index("zhi"), lax.axis_index("zlo")
-    step = 2 * parity - 1
-    slots = jnp.stack([group, group + step, group - step, group + 2]) % GROUPS
-    offs = (slots * (HEADS_HERE * HEAD_DIM)).astype(jnp.int32)
+    offs = jnp.stack(offsets()).astype(jnp.int32)
     own, to_one, to_two, to_three, own_q, to_two_q, to_three_q = pack(
-        offs, (key_rows, value_rows, key_tan, value_tan, query_rows, query_tan)
+        (key_rows, value_rows, key_tan, value_tan, query_rows, query_tan)
     )
     around = lambda array: [lax.ppermute(array, "x", perm) for perm in AROUND_X]
     swap = lambda arrays: [lax.ppermute(a, "core", SWAP) for a in arrays]
@@ -277,13 +282,13 @@
     )
     three_x = around(three_)
     far_q = lax.ppermute(near_q, Z, PAIR)
-    both_s = lax.ppermute(jnp.concatenate([one, *one_x, two, *two_x]), "core", SWAP)
+    both_s = lax.ppermute(jnp.concatenate([one, *one_x, two, *two_x, three_]), "core", SWAP)
     pieces = [(p, 0) for p in (own, *own_x, one, *one_x, two, *two_x)]
     pieces += [(own_s, i) for i in range(4)] + [(both_s, i) for i in range(8)]
     early = attend("early", [near_q], pieces, (0, HEADS_HERE))
     three_, three_x, far_q, early = lax.optimization_barrier((three_, three_x, far_q, early))
-    three_s = swap([three_, *three_x])
-    late = [(p, 0) for p in (three_, *three_x, *three_s)]
+    three_s = swap(three_x)
+    late = [(p, 0) for p in (three_, *three_x, *three_s)] + [(both_s, 8)]
     early_far = attend("early_far", [far_q], pieces, CHUNKS[0])
     paired, result, last, back = {}, (), (), []
     for kind, c in ORDER:

time: 140 us -> 143 us (1.021); the launches traced: 140 us -> 141 us
  local copies, waits for them, and re-layouts: 0.39 us -> 8.48 us
  starting transfers between devices: 48.5 us -> 45.1 us
  waiting for transfers between devices: 60.4 us -> 57 us
    unnamed x15 -> x46, local copies, waits for them, and re-layouts: 0.31 us -> 8.41 us
    ppermute x6, starting transfers between devices: 13.6 us -> 10.5 us  [per_device(): lax.ppermute(after(o, *result), Z, perm)]
    ppermute x2, waiting for transfers between devices: 2.78 us -> 0.93 us  [per_device(): paired[c] = lax.ppermute(after(part, *paired.values()), Z, PAIR)]
  transfers between devices with their start and end apart: 32 -> 31, of which waited for: 11 -> 11; matrix products, arithmetic and copies ran while one was open for 0% -> 0% of each run, Pallas kernels for 15% -> 15%
where the time goes in v4:
time: 143 us; the launch traced here: 141 us
  waiting for transfers between devices  57 us (40%)
  starting transfers between devices  45.1 us (32%)
  Pallas kernels  28.3 us (20%)
  local copies, waits for them, and re-layouts  8.48 us (6%)
    pallas_call x6, Pallas kernels, attend(): pl.pallas_call(functools.partial(attend_body, len(qs), len(gots), len(pie...  23.4 us
    ppermute x12, starting transfers between devices, per_device(): around = lambda array: [lax.ppermute(array, 'x', perm) for perm in AROUND_X]  18 us
    ppermute x1, waiting for transfers between devices, per_device(): three_ = lax.ppermute(to_three, Z, TO[2])  16.8 us
    ppermute x1, waiting for transfers between devices, per_device(): three_q = lax.ppermute(to_three_q, Z, TO[2])  14.4 us
    ppermute x12, waiting for transfers between devices, per_device(): around = lambda array: [lax.ppermute(array, 'x', perm) for perm in AROUND_X]  11.5 us
    ppermute x6, starting transfers between devices, per_device(): lax.ppermute(after(o, *result), Z, perm)  10.5 us
    unnamed x46, local copies, waits for them, and re-layouts  8.41 us
    ppermute x6, waiting for transfers between devices, per_device(): lax.ppermute(after(o, *result), Z, perm)  7.9 us
  transfers between devices with their start and end apart: 31, of which 11 were waited for; matrix products, arithmetic and copies ran while one was open for 0% of the time, Pallas kernels for 15%

profile of v4, /device:TPU:40, one launch (start us, length us, event | category | flops | bytes accessed | tf_op | source)
XLA Modules:
  0.0 141.2 jit_solution(13121971832645903148)
XLA Ops:
  0.6 2.8 %pack.1 = (bf16[20,64,128]{2,1,0:T(8,128)(2,1)}, bf16[30,64,128]{2,1,0:T(8,128)(2,1)}, bf16[20,64,128]{2,1,0:T(8,128)(2,1)}, bf16[20,64,128]{2,1,0:T(8,128)(2,1)...) custom-call(bf16[64,2560]{1,0:T(8,128)(2,1)} %refs_0_.1, ...), custom_call_target="tpu_custom_call" | custom-call | tf_op jit(solution)/shard_map/pack/pallas_call | solution.py:73
  3.5 2.0 %collective-permute-start = (bf16[30,64,128]{2,1,0:T(8,128)(2,1)}, bf16[30,64,128]{2,1,0:T(8,128)(2,1)S(1)}, u32[]{:S(2)}, u32[]{:S(2)}) collective-permute-start(bf16[30,64,128]{2,1,0:T(8,128)(2,1)} %get-tuple-element.64), channel_id=1, source_target_pairs={{0,35},{32,1},{1,32},{33,2},{2,33},{34,3},{3,34},{35,0},{4,39},{36... | collective-permute-start | bytes 1474568 | tf_op jit(solution)/shard_map/ppermute | solution.py:263
  5.5 1.5 %collective-permute-start.2 = (bf16[20,64,128]{2,1,0:T(8,128)(2,1)}, bf16[20,64,128]{2,1,0:T(8,128)(2,1)S(1)}, u32[]{:S(2)}, u32[]{:S(2)}) collective-permute-start(bf16[20,64,128]{2,1,0:T(8,128)(2,1)} %get-tuple-element.84.refs_1_), channel_id=1, source_target_pairs={{0,8},{8,16},{16,24},{24,0},{1,9},{9,17},{17,25},{25,1},{2,10},{10... | collective-permute-start | bytes 983048 | tf_op jit(solution)/shard_map/ppermute | solution.py:261
  7.0 1.7 %collective-permute-start.3 = (bf16[20,64,128]{2,1,0:T(8,128)(2,1)}, bf16[20,64,128]{2,1,0:T(8,128)(2,1)S(1)}, u32[]{:S(2)}, u32[]{:S(2)}) collective-permute-start(bf16[20,64,128]{2,1,0:T(8,128)(2,1)} %get-tuple-element.84.refs_1_), channel_id=1, source_target_pairs={{0,24},{8,0},{16,8},{24,16},{1,25},{9,1},{17,9},{25,17},{2,26},{10... | collective-permute-start | bytes 983048 | tf_op jit(solution)/shard_map/ppermute | solution.py:261
  8.7 1.8 %collective-permute-start.4 = (bf16[20,64,128]{2,1,0:T(8,128)(2,1)}, bf16[20,64,128]{2,1,0:T(8,128)(2,1)S(1)}, u32[]{:S(2)}, u32[]{:S(2)}) collective-permute-start(bf16[20,64,128]{2,1,0:T(8,128)(2,1)} %get-tuple-element.84.refs_1_), channel_id=1, source_target_pairs={{0,16},{8,24},{16,0},{24,8},{1,17},{9,25},{17,1},{25,9},{2,18},{10... | collective-permute-start | bytes 983048 | tf_op jit(solution)/shard_map/ppermute | solution.py:261
  10.6 3.6 %collective-permute-start.1 = (bf16[10,64,128]{2,1,0:T(8,128)(2,1)}, bf16[10,64,128]{2,1,0:T(8,128)(2,1)S(1)}, u32[]{:S(2)}, u32[]{:S(2)}) collective-permute-start(bf16[10,64,128]{2,1,0:T(8,128)(2,1)} %get-tuple-element.65), channel_id=1, source_target_pairs={{0,1},{32,35},{1,2},{33,32},{2,3},{34,33},{3,0},{35,34},{4,5},{36,... | collective-permute-start | bytes 491528 | tf_op jit(solution)/shard_map/ppermute | solution.py:264
  14.1 4.5 %collective-permute-done.1 = bf16[10,64,128]{2,1,0:T(8,128)(2,1)S(1)} collective-permute-done((bf16[10,64,128]{2,1,0:T(8,128)(2,1)}, bf16[10,64,128]{2,1,0:T(8,128)(2,1)S(1)}, u32[]{:S(2)}, u32[]{:S(2)}) %collective-permute-start.1) | collective-permute-done | bytes 163872 | tf_op jit(solution)/shard_map/ppermute | solution.py:264
  18.6 3.9 %collective-permute-done.3.refs_3_ = bf16[20,64,128]{2,1,0:T(8,128)(2,1)S(1)} collective-permute-done((bf16[20,64,128]{2,1,0:T(8,128)(2,1)}, bf16[20,64,128]{2,1,0:T(8,128)(2,1)S(1)}, u32[]{:S(2)}, u32[]{:S(2)}) %collective-permute-start.3) | collective-permute-done | bytes 327712 | tf_op jit(solution)/shard_map/ppermute | solution.py:261
  22.5 1.6 %collective-permute-done.4.refs_4_ = bf16[20,64,128]{2,1,0:T(8,128)(2,1)S(1)} collective-permute-done((bf16[20,64,128]{2,1,0:T(8,128)(2,1)}, bf16[20,64,128]{2,1,0:T(8,128)(2,1)S(1)}, u32[]{:S(2)}, u32[]{:S(2)}) %collective-permute-start.4) | collective-permute-done | bytes 327712 | tf_op jit(solution)/shard_map/ppermute | solution.py:261
  24.1 1.2 collective-permute-start.7
  25.4 2.1 %collective-permute-start.8 = (bf16[20,64,128]{2,1,0:T(8,128)(2,1)S(1)}, bf16[20,64,128]{2,1,0:T(8,128)(2,1)S(1)}, u32[]{:S(2)}, u32[]{:S(2)}) collective-permute-start(bf16[20,64,128]{2,1,0:T(8,128)(2,1)S(1)} %slice.6.refs_5_), channel_id=1, source_target_pairs={{0,24},{8,0},{16,8},{24,16},{1,25},{9,1},{17,9},{25,17},{2,26},{10... | collective-permute-start | bytes 983048 | tf_op jit(solution)/shard_map/ppermute | solution.py:261
  27.7 4.4 %collective-permute-start.5 = (bf16[20,64,128]{2,1,0:T(8,128)(2,1)}, bf16[20,64,128]{2,1,0:T(8,128)(2,1)S(1)}, u32[]{:S(2)}, u32[]{:S(2)}) collective-permute-start(bf16[20,64,128]{2,1,0:T(8,128)(2,1)} %get-tuple-element.70), channel_id=1, source_target_pairs={{0,1},{32,35},{1,2},{33,32},{2,3},{34,33},{3,0},{35,34},{4,5},{36,... | collective-permute-start | bytes 983048 | tf_op jit(solution)/shard_map/ppermute | solution.py:270
  32.0 2.0 %collective-permute-start.6 = (bf16[10,64,128]{2,1,0:T(8,128)(2,1)}, bf16[10,64,128]{2,1,0:T(8,128)(2,1)S(1)}, u32[]{:S(2)}, u32[]{:S(2)}) collective-permute-start(bf16[10,64,128]{2,1,0:T(8,128)(2,1)} %get-tuple-element.71), channel_id=1, source_target_pairs={{0,34},{32,2},{1,35},{33,3},{2,32},{34,0},{3,33},{35,1},{4,38},{36... | collective-permute-start | bytes 491528 | tf_op jit(solution)/shard_map/ppermute | solution.py:271
  34.1 14.4 %collective-permute-done.6 = bf16[10,64,128]{2,1,0:T(8,128)(2,1)S(1)} collective-permute-done((bf16[10,64,128]{2,1,0:T(8,128)(2,1)}, bf16[10,64,128]{2,1,0:T(8,128)(2,1)S(1)}, u32[]{:S(2)}, u32[]{:S(2)}) %collective-permute-start.6) | collective-permute-done | bytes 163872 | tf_op jit(solution)/shard_map/ppermute | solution.py:271
  48.4 1.1 pad_maximum_fusion
  49.7 0.9 collective-permute-start.11
  50.6 2.4 %collective-permute-start.12 = (bf16[20,64,128]{2,1,0:T(8,128)(2,1)S(1)}, bf16[20,64,128]{2,1,0:T(8,128)(2,1)S(1)}, u32[]{:S(2)}, u32[]{:S(2)}) collective-permute-start(bf16[20,64,128]{2,1,0:T(8,128)(2,1)S(1)} %collective-permute-done.5.refs_9_), channel_id=1, source_target_pairs={{0,24},{8,0},{16,8},{24,16},{1,25},{9,1},{17,9},{25,17},{2,26},{10... | collective-permute-start | bytes 983048 | tf_op jit(solution)/shard_map/ppermute | solution.py:261
  53.0 2.0 %collective-permute-start.13 = (bf16[20,64,128]{2,1,0:T(8,128)(2,1)S(1)}, bf16[20,64,128]{2,1,0:T(8,128)(2,1)S(1)}, u32[]{:S(2)}, u32[]{:S(2)}) collective-permute-start(bf16[20,64,128]{2,1,0:T(8,128)(2,1)S(1)} %collective-permute-done.5.refs_9_), channel_id=1, source_target_pairs={{0,16},{8,24},{16,0},{24,8},{1,17},{9,25},{17,1},{25,9},{2,18},{10... | collective-permute-start | bytes 983048 | tf_op jit(solution)/shard_map/ppermute | solution.py:261
  55.2 16.8 %collective-permute-done.10.refs_2_.refs_25_.refs_3_ = bf16[20,64,128]{2,1,0:T(8,128)(2,1)S(1)} collective-permute-done((bf16[20,64,128]{2,1,0:T(8,128)(2,1)S(1)}, bf16[20,64,128]{2,1,0:T(8,128)(2,1)S(1)}, u32[]{:S(2)}, u32[]{:S(2)}) %collective-permute-start.10) | collective-permute-done | bytes 327712 | tf_op jit(solution)/shard_map/ppermute | solution.py:276
  72.9 3.2 %collective-permute-start.16 = (bf16[20,64,128]{2,1,0:T(8,128)(2,1)S(1)}, bf16[20,64,128]{2,1,0:T(8,128)(2,1)S(1)}, u32[]{:S(2)}, u32[]{:S(2)}) collective-permute-start(bf16[20,64,128]{2,1,0:T(8,128)(2,1)S(1)} %collective-permute-done.10.refs_2_.refs_25_.refs_3_), channel_id=1, source_target_pairs={{0,24},{8,0},{16,8},{24,16},{1,25},{9,1},{17,9},{25,17},{2,26},{10... | collective-permute-start | bytes 983048 | tf_op jit(solution)/shard_map/ppermute | solution.py:261
  76.9 1.0 collective-permute-done.19.refs_17_.refs_18_.refs_19_.refs_20_.refs_21_.refs_22_.refs_23_.refs_24_.refs_9_.refs_32_.refs_10_
  77.9 7.0 %early.1.refs_1_ = bf16[5,1,544,128]{3,2,1,0:T(8,128)(2,1)S(1)} custom-call(bf16[4,10,64,128]{3,2,1,0:T(8,128)(2,1)S(1)} %pad_maximum_fusion.1.refs_0_, bf16[20,64,128]{2,1,0:T(8,128)(2,1)S(1)} %copy-done.4, bf16[20,64,128]{2,1,0:T(8,128)(2,1)S(1)} %collective-permute-done.2.refs_2_, bf16[20,64,128]{2,1,0:T(8,128)(2,1)S(1)} %collective-permute-done.3.refs_3_, ...), custom_call_target="tpu_custom_call" | custom-call | flops 4026531840 | bytes 7864320 | tf_op jit(solution)/shard_map/early/pallas_call | solution.py:235
  85.0 5.9 %collective-permute-done.15.refs_3_.refs_26_.refs_4_ = bf16[20,64,128]{2,1,0:T(8,128)(2,1)S(1)} collective-permute-done((bf16[20,64,128]{2,1,0:T(8,128)(2,1)S(1)}, bf16[20,64,128]{2,1,0:T(8,128)(2,1)S(1)}, u32[]{:S(2)}, u32[]{:S(2)}) %collective-permute-start.15) | collective-permute-done | bytes 327712 | tf_op jit(solution)/shard_map/ppermute | solution.py:261
  91.6 2.8 %early_far.1.refs_1_ = bf16[2,1,544,128]{3,2,1,0:T(8,128)(2,1)S(1)} custom-call(bf16[4,10,64,128]{3,2,1,0:T(8,128)(2,1)S(1)} %collective-permute-done.18.refs_0_, bf16[20,64,128]{2,1,0:T(8,128)(2,1)S(1)} %copy-done.4, bf16[20,64,128]{2,1,0:T(8,128)(2,1)S(1)} %collective-permute-done.2.refs_2_, bf16[20,64,128]{2,1,0:T(8,128)(2,1)S(1)} %collective-permute-done.3.refs_3_, ...), custom_call_target="tpu_custom_call" | custom-call | flops 1610612736 | bytes 3145728 | tf_op jit(solution)/shard_map/early_far/pallas_call | solution.py:235
  94.5 1.7 %far.2 = bf16[2,1,544,128]{3,2,1,0:T(8,128)(2,1)S(1)} custom-call(bf16[4,10,64,128]{3,2,1,0:T(8,128)(2,1)S(1)} %collective-permute-done.18.refs_0_, bf16[2,1,544,128]{3,2,1,0:T(8,128)(2,1)S(1)} %early_far.1.refs_1_, bf16[20,64,128]{2,1,0:T(8,128)(2,1)S(1)} %collective-permute-done.10.refs_2_.refs_25_.refs_3_, ...), custom_call_target="tpu_custom_call" | custom-call | flops 536870912 | bytes 1048576 | tf_op jit(solution)/shard_map/far/pallas_call | solution.py:235
  96.3 1.8 %collective-permute-start.23 = (bf16[2,1,544,128]{3,2,1,0:T(8,128)(2,1)S(1)}, bf16[2,1,544,128]{3,2,1,0:T(8,128)(2,1)S(1)}, u32[]{:S(2)}, u32[]{:S(2)}) collective-permute-start(bf16[2,1,544,128]{3,2,1,0:T(8,128)(2,1)S(1)} %far.2), channel_id=1, source_target_pairs={{0,32},{32,0},{1,33},{33,1},{2,34},{34,2},{3,35},{35,3},{4,36},{36... | collective-permute-start | bytes 835592 | tf_op jit(solution)/shard_map/ppermute | solution.py:301
  98.1 6.3 %far.3 = bf16[3,1,544,128]{3,2,1,0:T(8,128)(2,1)} custom-call(bf16[4,10,64,128]{3,2,1,0:T(8,128)(2,1)S(1)} %collective-permute-done.18.refs_0_, bf16[20,64,128]{2,1,0:T(8,128)(2,1)S(1)} %copy-done.4, bf16[20,64,128]{2,1,0:T(8,128)(2,1)S(1)} %collective-permute-done.2.refs_2_, bf16[20,64,128]{2,1,0:T(8,128)(2,1)S(1)} %collective-permute-done.3.refs_3_, ...), custom_call_target="tpu_custom_call" | custom-call | flops 3221225472 | bytes 6291456 | tf_op jit(solution)/shard_map/far/pallas_call | solution.py:235
  105.4 1.7 %collective-permute-start.24 = (bf16[3,1,544,128]{3,2,1,0:T(8,128)(2,1)}, bf16[3,1,544,128]{3,2,1,0:T(8,128)(2,1)}, u32[]{:S(2)}, u32[]{:S(2)}) collective-permute-start(bf16[3,1,544,128]{3,2,1,0:T(8,128)(2,1)} %far.3), channel_id=1, source_target_pairs={{0,32},{32,0},{1,33},{33,1},{2,34},{34,2},{3,35},{35,3},{4,36},{36... | collective-permute-start | bytes 1253384 | tf_op jit(solution)/shard_map/ppermute | solution.py:301
  107.2 1.1 copy-done.1
  108.3 1.1 copy-done.3
  109.4 1.0 copy-done.6
  110.3 1.0 copy-done.8
  111.3 1.0 copy-done.10
  112.3 1.0 copy-done.12
  113.3 1.0 copy-done.14
  114.2 1.0 copy-done.16
  115.2 1.9 %near.2 = (bf16[2,2,64,128]{3,2,1,0:T(8,128)(2,1)S(1)}, bf16[2,2,64,128]{3,2,1,0:T(8,128)(2,1)S(1)}, bf16[2,2,64,128]{3,2,1,0:T(8,128)(2,1)S(1)}, bf16[2,2,64,128]{3,2,1,0:T(8,128)(2,1)S(1)}) custom-call(bf16[4,10,64,128]{3,2,1,0:T(8,128)(2,1)S(1)} %copy-done.1, bf16[5,1,544,128]{3,2,1,0:T(8,128)(2,1)S(1)} %copy-done.3, ...), custom_call_target="tpu_custom_call" | custom-call | flops 536870912 | bytes 1048576 | tf_op jit(solution)/shard_map/near/pallas_call | solution.py:235
  117.1 1.1 collective-permute-start.25
  118.2 2.3 %collective-permute-start.26 = (bf16[2,2,64,128]{3,2,1,0:T(8,128)(2,1)S(1)}, bf16[2,2,64,128]{3,2,1,0:T(8,128)(2,1)S(1)}, u32[]{:S(2)}, u32[]{:S(2)}) collective-permute-start(bf16[2,2,64,128]{3,2,1,0:T(8,128)(2,1)S(1)} %get-tuple-element.119), channel_id=1, source_target_pairs={{0,3},{32,33},{1,0},{33,34},{2,1},{34,35},{3,2},{35,32},{4,7},{36,... | collective-permute-start | bytes 196616 | tf_op jit(solution)/shard_map/ppermute | solution.py:309
  120.5 2.3 %collective-permute-start.27 = (bf16[2,2,64,128]{3,2,1,0:T(8,128)(2,1)S(1)}, bf16[2,2,64,128]{3,2,1,0:T(8,128)(2,1)S(1)}, u32[]{:S(2)}, u32[]{:S(2)}) collective-permute-start(bf16[2,2,64,128]{3,2,1,0:T(8,128)(2,1)S(1)} %get-tuple-element.120), channel_id=1, source_target_pairs={{0,34},{32,2},{1,35},{33,3},{2,32},{34,0},{3,33},{35,1},{4,38},{36... | collective-permute-start | bytes 196616 | tf_op jit(solution)/shard_map/ppermute | solution.py:309
  122.8 3.7 %near.3 = (bf16[3,2,64,128]{3,2,1,0:T(8,128)(2,1)S(1)}, bf16[3,2,64,128]{3,2,1,0:T(8,128)(2,1)S(1)}, bf16[3,2,64,128]{3,2,1,0:T(8,128)(2,1)S(1)}, bf16[3,2,64,128]{3,2,1,0:T(8,128)(2,1)S(1)}) custom-call(bf16[4,10,64,128]{3,2,1,0:T(8,128)(2,1)S(1)} %copy-done.1, bf16[5,1,544,128]{3,2,1,0:T(8,128)(2,1)S(1)} %copy-done.3, ...), custom_call_target="tpu_custom_call" | custom-call | flops 805306368 | bytes 1572864 | tf_op jit(solution)/shard_map/near/pallas_call | solution.py:235
  126.5 1.3 collective-permute-done.27.refs_3_
  128.4 2.8 %collective-permute-start.30 = (bf16[3,2,64,128]{3,2,1,0:T(8,128)(2,1)S(1)}, bf16[3,2,64,128]{3,2,1,0:T(8,128)(2,1)S(1)}, u32[]{:S(2)}, u32[]{:S(2)}) collective-permute-start(bf16[3,2,64,128]{3,2,1,0:T(8,128)(2,1)S(1)} %get-tuple-element.125), channel_id=1, source_target_pairs={{0,34},{32,2},{1,35},{33,3},{2,32},{34,0},{3,33},{35,1},{4,38},{36... | collective-permute-start | bytes 294920 | tf_op jit(solution)/shard_map/ppermute | solution.py:309
  131.2 1.0 collective-permute-start.29
  132.1 1.0 collective-permute-start.28
  133.1 4.4 %collective-permute-done.30.refs_3_ = bf16[3,2,64,128]{3,2,1,0:T(8,128)(2,1)S(1)} collective-permute-done((bf16[3,2,64,128]{3,2,1,0:T(8,128)(2,1)S(1)}, bf16[3,2,64,128]{3,2,1,0:T(8,128)(2,1)S(1)}, u32[]{:S(2)}, u32[]{:S(2)}) %collective-permute-start.30) | collective-permute-done | bytes 98336 | tf_op jit(solution)/shard_map/ppermute | solution.py:309
  137.5 2.2 %collective-permute-done.29.refs_2_ = bf16[3,2,64,128]{3,2,1,0:T(8,128)(2,1)S(1)} collective-permute-done((bf16[3,2,64,128]{3,2,1,0:T(8,128)(2,1)S(1)}, bf16[3,2,64,128]{3,2,1,0:T(8,128)(2,1)S(1)}, u32[]{:S(2)}, u32[]{:S(2)}) %collective-permute-start.29) | collective-permute-done | bytes 98336 | tf_op jit(solution)/shard_map/ppermute | solution.py:309
  139.7 1.5 %unpack.3 = (bf16[64,2560]{1,0:T(8,128)(2,1)}, bf16[64,2560]{1,0:T(8,128)(2,1)}) custom-call(s32[4]{0:T(128)S(1)} %pad_add_fusion.offs, bf16[3,2,64,128]{3,2,1,0:T(8,128)(2,1)S(1)} %get-tuple-element.113.refs_0_, bf16[3,2,64,128]{3,2,1,0:T(8,128)(2,1)S(1)} %collective-permute-done.28.refs_1_, bf16[3,2,64,128]{3,2,1,0:T(8,128)(2,1)S(1)} %collective-permute-done.29.refs_2_, ...), custom_call_target="tpu_custom_call" | custom-call | tf_op jit(solution)/shard_map/unpack/pallas_call | solution.py:102
  (75 shorter events, 4.4 us)
Async XLA Ops:
  3.5 51.6 %copy-start.18 = (bf16[20,64,128]{2,1,0:T(8,128)(2,1)S(1)}, bf16[20,64,128]{2,1,0:T(8,128)(2,1)}, u32[]{:S(2)}) copy-start(bf16[20,64,128]{2,1,0:T(8,128)(2,1)} %get-tuple-element.78) | copy-start | bytes 983044
  3.5 51.6 %copy-start.17 = (bf16[10,64,128]{2,1,0:T(8,128)(2,1)S(1)}, bf16[10,64,128]{2,1,0:T(8,128)(2,1)}, u32[]{:S(2)}) copy-start(bf16[10,64,128]{2,1,0:T(8,128)(2,1)} %get-tuple-element.88) | copy-start | bytes 491524
  3.5 20.6 %collective-permute-start = (bf16[30,64,128]{2,1,0:T(8,128)(2,1)}, bf16[30,64,128]{2,1,0:T(8,128)(2,1)S(1)}, u32[]{:S(2)}, u32[]{:S(2)}) collective-permute-start(bf16[30,64,128]{2,1,0:T(8,128)(2,1)} %get-tuple-element.64), channel_id=1, source_target_pairs={{0,35},{32,1},{1,32},{33,2},{2,33},{34,3},{3,34},{35,0},{4,39},{36... | collective-permute-start | bytes 1474568 | tf_op jit(solution)/shard_map/ppermute | solution.py:263
  5.5 13.1 %collective-permute-start.2 = (bf16[20,64,128]{2,1,0:T(8,128)(2,1)}, bf16[20,64,128]{2,1,0:T(8,128)(2,1)S(1)}, u32[]{:S(2)}, u32[]{:S(2)}) collective-permute-start(bf16[20,64,128]{2,1,0:T(8,128)(2,1)} %get-tuple-element.84.refs_1_), channel_id=1, source_target_pairs={{0,8},{8,16},{16,24},{24,0},{1,9},{9,17},{17,25},{25,1},{2,10},{10... | collective-permute-start | bytes 983048 | tf_op jit(solution)/shard_map/ppermute | solution.py:261
  7.0 15.5 %collective-permute-start.3 = (bf16[20,64,128]{2,1,0:T(8,128)(2,1)}, bf16[20,64,128]{2,1,0:T(8,128)(2,1)S(1)}, u32[]{:S(2)}, u32[]{:S(2)}) collective-permute-start(bf16[20,64,128]{2,1,0:T(8,128)(2,1)} %get-tuple-element.84.refs_1_), channel_id=1, source_target_pairs={{0,24},{8,0},{16,8},{24,16},{1,25},{9,1},{17,9},{25,17},{2,26},{10... | collective-permute-start | bytes 983048 | tf_op jit(solution)/shard_map/ppermute | solution.py:261
  8.7 15.4 %collective-permute-start.4 = (bf16[20,64,128]{2,1,0:T(8,128)(2,1)}, bf16[20,64,128]{2,1,0:T(8,128)(2,1)S(1)}, u32[]{:S(2)}, u32[]{:S(2)}) collective-permute-start(bf16[20,64,128]{2,1,0:T(8,128)(2,1)} %get-tuple-element.84.refs_1_), channel_id=1, source_target_pairs={{0,16},{8,24},{16,0},{24,8},{1,17},{9,25},{17,1},{25,9},{2,18},{10... | collective-permute-start | bytes 983048 | tf_op jit(solution)/shard_map/ppermute | solution.py:261
  10.6 8.0 %collective-permute-start.1 = (bf16[10,64,128]{2,1,0:T(8,128)(2,1)}, bf16[10,64,128]{2,1,0:T(8,128)(2,1)S(1)}, u32[]{:S(2)}, u32[]{:S(2)}) collective-permute-start(bf16[10,64,128]{2,1,0:T(8,128)(2,1)} %get-tuple-element.65), channel_id=1, source_target_pairs={{0,1},{32,35},{1,2},{33,32},{2,3},{34,33},{3,0},{35,34},{4,5},{36,... | collective-permute-start | bytes 491528 | tf_op jit(solution)/shard_map/ppermute | solution.py:264
  24.1 24.3 %collective-permute-start.7 = (bf16[20,64,128]{2,1,0:T(8,128)(2,1)S(1)}, bf16[20,64,128]{2,1,0:T(8,128)(2,1)S(1)}, u32[]{:S(2)}, u32[]{:S(2)}) collective-permute-start(bf16[20,64,128]{2,1,0:T(8,128)(2,1)S(1)} %slice.6.refs_5_), channel_id=1, source_target_pairs={{0,8},{8,16},{16,24},{24,0},{1,9},{9,17},{17,25},{25,1},{2,10},{10... | collective-permute-start | bytes 983048 | tf_op jit(solution)/shard_map/ppermute | solution.py:261
  25.4 23.1 %collective-permute-start.8 = (bf16[20,64,128]{2,1,0:T(8,128)(2,1)S(1)}, bf16[20,64,128]{2,1,0:T(8,128)(2,1)S(1)}, u32[]{:S(2)}, u32[]{:S(2)}) collective-permute-start(bf16[20,64,128]{2,1,0:T(8,128)(2,1)S(1)} %slice.6.refs_5_), channel_id=1, source_target_pairs={{0,24},{8,0},{16,8},{24,16},{1,25},{9,1},{17,9},{25,17},{2,26},{10... | collective-permute-start | bytes 983048 | tf_op jit(solution)/shard_map/ppermute | solution.py:261
  27.4 21.0 %collective-permute-start.9 = (bf16[20,64,128]{2,1,0:T(8,128)(2,1)S(1)}, bf16[20,64,128]{2,1,0:T(8,128)(2,1)S(1)}, u32[]{:S(2)}, u32[]{:S(2)}) collective-permute-start(bf16[20,64,128]{2,1,0:T(8,128)(2,1)S(1)} %slice.6.refs_5_), channel_id=1, source_target_pairs={{0,16},{8,24},{16,0},{24,8},{1,17},{9,25},{17,1},{25,9},{2,18},{10... | collective-permute-start | bytes 983048 | tf_op jit(solution)/shard_map/ppermute | solution.py:261
  27.7 20.8 %collective-permute-start.5 = (bf16[20,64,128]{2,1,0:T(8,128)(2,1)}, bf16[20,64,128]{2,1,0:T(8,128)(2,1)S(1)}, u32[]{:S(2)}, u32[]{:S(2)}) collective-permute-start(bf16[20,64,128]{2,1,0:T(8,128)(2,1)} %get-tuple-element.70), channel_id=1, source_target_pairs={{0,1},{32,35},{1,2},{33,32},{2,3},{34,33},{3,0},{35,34},{4,5},{36,... | collective-permute-start | bytes 983048 | tf_op jit(solution)/shard_map/ppermute | solution.py:270
  32.0 16.4 %collective-permute-start.6 = (bf16[10,64,128]{2,1,0:T(8,128)(2,1)}, bf16[10,64,128]{2,1,0:T(8,128)(2,1)S(1)}, u32[]{:S(2)}, u32[]{:S(2)}) collective-permute-start(bf16[10,64,128]{2,1,0:T(8,128)(2,1)} %get-tuple-element.71), channel_id=1, source_target_pairs={{0,34},{32,2},{1,35},{33,3},{2,32},{34,0},{3,33},{35,1},{4,38},{36... | collective-permute-start | bytes 491528 | tf_op jit(solution)/shard_map/ppermute | solution.py:271
  49.6 22.4 %collective-permute-start.14 = (bf16[80,64,128]{2,1,0:T(8,128)(2,1)S(1)}, bf16[80,64,128]{2,1,0:T(8,128)(2,1)S(1)}, u32[]{:S(2)}, u32[]{:S(2)}) collective-permute-start(bf16[80,64,128]{2,1,0:T(8,128)(2,1)S(1)} %pad_maximum_fusion), channel_id=1, source_target_pairs={{0,4},{4,0},{1,5},{5,1},{2,6},{6,2},{3,7},{7,3},{8,12},{12,8},{9,1... | collective-permute-start | bytes 3932168 | tf_op jit(solution)/shard_map/ppermute | solution.py:278
  49.7 22.3 %collective-permute-start.11 = (bf16[20,64,128]{2,1,0:T(8,128)(2,1)S(1)}, bf16[20,64,128]{2,1,0:T(8,128)(2,1)S(1)}, u32[]{:S(2)}, u32[]{:S(2)}) collective-permute-start(bf16[20,64,128]{2,1,0:T(8,128)(2,1)S(1)} %collective-permute-done.5.refs_9_), channel_id=1, source_target_pairs={{0,8},{8,16},{16,24},{24,0},{1,9},{9,17},{17,25},{25,1},{2,10},{10... | collective-permute-start | bytes 983048 | tf_op jit(solution)/shard_map/ppermute | solution.py:261
  50.6 21.4 %collective-permute-start.12 = (bf16[20,64,128]{2,1,0:T(8,128)(2,1)S(1)}, bf16[20,64,128]{2,1,0:T(8,128)(2,1)S(1)}, u32[]{:S(2)}, u32[]{:S(2)}) collective-permute-start(bf16[20,64,128]{2,1,0:T(8,128)(2,1)S(1)} %collective-permute-done.5.refs_9_), channel_id=1, source_target_pairs={{0,24},{8,0},{16,8},{24,16},{1,25},{9,1},{17,9},{25,17},{2,26},{10... | collective-permute-start | bytes 983048 | tf_op jit(solution)/shard_map/ppermute | solution.py:261
  53.0 19.0 %collective-permute-start.13 = (bf16[20,64,128]{2,1,0:T(8,128)(2,1)S(1)}, bf16[20,64,128]{2,1,0:T(8,128)(2,1)S(1)}, u32[]{:S(2)}, u32[]{:S(2)}) collective-permute-start(bf16[20,64,128]{2,1,0:T(8,128)(2,1)S(1)} %collective-permute-done.5.refs_9_), channel_id=1, source_target_pairs={{0,16},{8,24},{16,0},{24,8},{1,17},{9,25},{17,1},{25,9},{2,18},{10... | collective-permute-start | bytes 983048 | tf_op jit(solution)/shard_map/ppermute | solution.py:261
  55.0 17.0 %collective-permute-start.10 = (bf16[20,64,128]{2,1,0:T(8,128)(2,1)S(1)}, bf16[20,64,128]{2,1,0:T(8,128)(2,1)S(1)}, u32[]{:S(2)}, u32[]{:S(2)}) collective-permute-start(bf16[20,64,128]{2,1,0:T(8,128)(2,1)S(1)} %copy-done.18), channel_id=1, source_target_pairs={{0,34},{32,2},{1,35},{33,3},{2,32},{34,0},{3,33},{35,1},{4,38},{36... | collective-permute-start | bytes 983048 | tf_op jit(solution)/shard_map/ppermute | solution.py:276
  55.2 22.8 %copy-start = (bf16[4,10,64,128]{3,2,1,0:T(8,128)(2,1)}, bf16[4,10,64,128]{3,2,1,0:T(8,128)(2,1)S(1)}, u32[]{:S(2)}) copy-start(bf16[4,10,64,128]{3,2,1,0:T(8,128)(2,1)S(1)} %pad_maximum_fusion.1.refs_0_) | copy-start | bytes 1966084
  55.2 22.8 %copy-start.4 = (bf16[20,64,128]{2,1,0:T(8,128)(2,1)S(1)}, bf16[20,64,128]{2,1,0:T(8,128)(2,1)}, u32[]{:S(2)}) copy-start(bf16[20,64,128]{2,1,0:T(8,128)(2,1)} %get-tuple-element.84.refs_1_) | copy-start | bytes 983044
  72.5 5.5 %collective-permute-start.19 = (bf16[180,64,128]{2,1,0:T(8,128)(2,1)S(1)}, bf16[180,64,128]{2,1,0:T(8,128)(2,1)S(1)}, u32[]{:S(2)}, u32[]{:S(2)}) collective-permute-start(bf16[180,64,128]{2,1,0:T(8,128)(2,1)S(1)} %constant_dynamic-update-slice_fusion), channel_id=1, source_target_pairs={{0,4},{4,0},{1,5},{5,1},{2,6},{6,2},{3,7},{7,3},{8,12},{12,8},{9,1... | collective-permute-start | bytes 8847368 | tf_op jit(solution)/shard_map/ppermute | solution.py:285
  72.6 18.4 %collective-permute-start.18 = (bf16[4,10,64,128]{3,2,1,0:T(8,128)(2,1)S(1)}, bf16[4,10,64,128]{3,2,1,0:T(8,128)(2,1)S(1)}, u32[]{:S(2)}, u32[]{:S(2)}) collective-permute-start(bf16[4,10,64,128]{3,2,1,0:T(8,128)(2,1)S(1)} %pad_maximum_fusion.1.refs_0_), channel_id=1, source_target_pairs={{0,32},{32,0},{1,33},{33,1},{2,34},{34,2},{3,35},{35,3},{4,36},{36... | collective-permute-start | bytes 1966088 | tf_op jit(solution)/shard_map/ppermute | solution.py:284
  72.8 18.1 %collective-permute-start.15 = (bf16[20,64,128]{2,1,0:T(8,128)(2,1)S(1)}, bf16[20,64,128]{2,1,0:T(8,128)(2,1)S(1)}, u32[]{:S(2)}, u32[]{:S(2)}) collective-permute-start(bf16[20,64,128]{2,1,0:T(8,128)(2,1)S(1)} %collective-permute-done.10.refs_2_.refs_25_.refs_3_), channel_id=1, source_target_pairs={{0,8},{8,16},{16,24},{24,0},{1,9},{9,17},{17,25},{25,1},{2,10},{10... | collective-permute-start | bytes 983048 | tf_op jit(solution)/shard_map/ppermute | solution.py:261
  72.9 18.0 %collective-permute-start.16 = (bf16[20,64,128]{2,1,0:T(8,128)(2,1)S(1)}, bf16[20,64,128]{2,1,0:T(8,128)(2,1)S(1)}, u32[]{:S(2)}, u32[]{:S(2)}) collective-permute-start(bf16[20,64,128]{2,1,0:T(8,128)(2,1)S(1)} %collective-permute-done.10.refs_2_.refs_25_.refs_3_), channel_id=1, source_target_pairs={{0,24},{8,0},{16,8},{24,16},{1,25},{9,1},{17,9},{25,17},{2,26},{10... | collective-permute-start | bytes 983048 | tf_op jit(solution)/shard_map/ppermute | solution.py:261
  76.2 14.8 %collective-permute-start.17 = (bf16[20,64,128]{2,1,0:T(8,128)(2,1)S(1)}, bf16[20,64,128]{2,1,0:T(8,128)(2,1)S(1)}, u32[]{:S(2)}, u32[]{:S(2)}) collective-permute-start(bf16[20,64,128]{2,1,0:T(8,128)(2,1)S(1)} %collective-permute-done.10.refs_2_.refs_25_.refs_3_), channel_id=1, source_target_pairs={{0,16},{8,24},{16,0},{24,8},{1,17},{9,25},{17,1},{25,9},{2,18},{10... | collective-permute-start | bytes 983048 | tf_op jit(solution)/shard_map/ppermute | solution.py:261
  85.0 9.5 %copy-start.2 = (bf16[5,1,544,128]{3,2,1,0:T(8,128)(2,1)}, bf16[5,1,544,128]{3,2,1,0:T(8,128)(2,1)S(1)}, u32[]{:S(2)}) copy-start(bf16[5,1,544,128]{3,2,1,0:T(8,128)(2,1)S(1)} %early.1.refs_1_) | copy-start | bytes 2088964
  90.9 7.2 %copy-start.5 = (bf16[20,64,128]{2,1,0:T(8,128)(2,1)}, bf16[20,64,128]{2,1,0:T(8,128)(2,1)S(1)}, u32[]{:S(2)}) copy-start(bf16[20,64,128]{2,1,0:T(8,128)(2,1)S(1)} %collective-permute-done.15.refs_3_.refs_26_.refs_4_) | copy-start | bytes 983044
  90.9 7.2 %copy-start.7 = (bf16[20,64,128]{2,1,0:T(8,128)(2,1)}, bf16[20,64,128]{2,1,0:T(8,128)(2,1)S(1)}, u32[]{:S(2)}) copy-start(bf16[20,64,128]{2,1,0:T(8,128)(2,1)S(1)} %collective-permute-done.16.refs_4_.refs_27_.refs_5_) | copy-start | bytes 983044
  90.9 7.2 %copy-start.9 = (bf16[20,64,128]{2,1,0:T(8,128)(2,1)}, bf16[20,64,128]{2,1,0:T(8,128)(2,1)S(1)}, u32[]{:S(2)}) copy-start(bf16[20,64,128]{2,1,0:T(8,128)(2,1)S(1)} %collective-permute-done.17.refs_5_.refs_28_.refs_6_) | copy-start | bytes 983044
  90.9 3.5 %collective-permute-start.20 = (bf16[20,64,128]{2,1,0:T(8,128)(2,1)S(1)}, bf16[20,64,128]{2,1,0:T(8,128)(2,1)S(1)}, u32[]{:S(2)}, u32[]{:S(2)}) collective-permute-start(bf16[20,64,128]{2,1,0:T(8,128)(2,1)S(1)} %collective-permute-done.15.refs_3_.refs_26_.refs_4_), channel_id=1, source_target_pairs={{0,4},{4,0},{1,5},{5,1},{2,6},{6,2},{3,7},{7,3},{8,12},{12,8},{9,1... | collective-permute-start | bytes 983048 | tf_op jit(solution)/shard_map/ppermute | solution.py:262
  91.0 3.5 %collective-permute-start.21 = (bf16[20,64,128]{2,1,0:T(8,128)(2,1)S(1)}, bf16[20,64,128]{2,1,0:T(8,128)(2,1)S(1)}, u32[]{:S(2)}, u32[]{:S(2)}) collective-permute-start(bf16[20,64,128]{2,1,0:T(8,128)(2,1)S(1)} %collective-permute-done.16.refs_4_.refs_27_.refs_5_), channel_id=1, source_target_pairs={{0,4},{4,0},{1,5},{5,1},{2,6},{6,2},{3,7},{7,3},{8,12},{12,8},{9,1... | collective-permute-start | bytes 983048 | tf_op jit(solution)/shard_map/ppermute | solution.py:262
  91.5 3.0 %collective-permute-start.22 = (bf16[20,64,128]{2,1,0:T(8,128)(2,1)S(1)}, bf16[20,64,128]{2,1,0:T(8,128)(2,1)S(1)}, u32[]{:S(2)}, u32[]{:S(2)}) collective-permute-start(bf16[20,64,128]{2,1,0:T(8,128)(2,1)S(1)} %collective-permute-done.17.refs_5_.refs_28_.refs_6_), channel_id=1, source_target_pairs={{0,4},{4,0},{1,5},{5,1},{2,6},{6,2},{3,7},{7,3},{8,12},{12,8},{9,1... | collective-permute-start | bytes 983048 | tf_op jit(solution)/shard_map/ppermute | solution.py:262
  94.5 3.6 %copy-start.11 = (bf16[20,64,128]{2,1,0:T(8,128)(2,1)}, bf16[20,64,128]{2,1,0:T(8,128)(2,1)S(1)}, u32[]{:S(2)}) copy-start(bf16[20,64,128]{2,1,0:T(8,128)(2,1)S(1)} %collective-permute-done.20.refs_6_.refs_29_.refs_7_) | copy-start | bytes 983044
  94.5 3.6 %copy-start.13 = (bf16[20,64,128]{2,1,0:T(8,128)(2,1)}, bf16[20,64,128]{2,1,0:T(8,128)(2,1)S(1)}, u32[]{:S(2)}) copy-start(bf16[20,64,128]{2,1,0:T(8,128)(2,1)S(1)} %collective-permute-done.21.refs_7_.refs_30_.refs_8_) | copy-start | bytes 983044
  94.5 3.6 %copy-start.15 = (bf16[20,64,128]{2,1,0:T(8,128)(2,1)}, bf16[20,64,128]{2,1,0:T(8,128)(2,1)S(1)}, u32[]{:S(2)}) copy-start(bf16[20,64,128]{2,1,0:T(8,128)(2,1)S(1)} %collective-permute-done.22.refs_8_.refs_31_.refs_9_) | copy-start | bytes 983044
  96.3 9.1 %collective-permute-start.23 = (bf16[2,1,544,128]{3,2,1,0:T(8,128)(2,1)S(1)}, bf16[2,1,544,128]{3,2,1,0:T(8,128)(2,1)S(1)}, u32[]{:S(2)}, u32[]{:S(2)}) collective-permute-start(bf16[2,1,544,128]{3,2,1,0:T(8,128)(2,1)S(1)} %far.2), channel_id=1, source_target_pairs={{0,32},{32,0},{1,33},{33,1},{2,34},{34,2},{3,35},{35,3},{4,36},{36... | collective-permute-start | bytes 835592 | tf_op jit(solution)/shard_map/ppermute | solution.py:301
  105.4 17.4 %collective-permute-start.24 = (bf16[3,1,544,128]{3,2,1,0:T(8,128)(2,1)}, bf16[3,1,544,128]{3,2,1,0:T(8,128)(2,1)}, u32[]{:S(2)}, u32[]{:S(2)}) collective-permute-start(bf16[3,1,544,128]{3,2,1,0:T(8,128)(2,1)} %far.3), channel_id=1, source_target_pairs={{0,32},{32,0},{1,33},{33,1},{2,34},{34,2},{3,35},{35,3},{4,36},{36... | collective-permute-start | bytes 1253384 | tf_op jit(solution)/shard_map/ppermute | solution.py:301
  107.2 1.1 copy-start.1
  108.3 1.1 copy-start.3
  110.3 1.0 copy-start.8
  111.3 1.0 copy-start.10
  112.3 1.0 copy-start.12
  113.3 1.0 copy-start.14
  117.1 9.4 %collective-permute-start.25 = (bf16[2,2,64,128]{3,2,1,0:T(8,128)(2,1)S(1)}, bf16[2,2,64,128]{3,2,1,0:T(8,128)(2,1)S(1)}, u32[]{:S(2)}, u32[]{:S(2)}) collective-permute-start(bf16[2,2,64,128]{3,2,1,0:T(8,128)(2,1)S(1)} %get-tuple-element.118), channel_id=1, source_target_pairs={{0,35},{32,1},{1,32},{33,2},{2,33},{34,3},{3,34},{35,0},{4,39},{36... | collective-permute-start | bytes 196616 | tf_op jit(solution)/shard_map/ppermute | solution.py:309
  118.2 8.3 %collective-permute-start.26 = (bf16[2,2,64,128]{3,2,1,0:T(8,128)(2,1)S(1)}, bf16[2,2,64,128]{3,2,1,0:T(8,128)(2,1)S(1)}, u32[]{:S(2)}, u32[]{:S(2)}) collective-permute-start(bf16[2,2,64,128]{3,2,1,0:T(8,128)(2,1)S(1)} %get-tuple-element.119), channel_id=1, source_target_pairs={{0,3},{32,33},{1,0},{33,34},{2,1},{34,35},{3,2},{35,32},{4,7},{36,... | collective-permute-start | bytes 196616 | tf_op jit(solution)/shard_map/ppermute | solution.py:309
  120.5 7.3 %collective-permute-start.27 = (bf16[2,2,64,128]{3,2,1,0:T(8,128)(2,1)S(1)}, bf16[2,2,64,128]{3,2,1,0:T(8,128)(2,1)S(1)}, u32[]{:S(2)}, u32[]{:S(2)}) collective-permute-start(bf16[2,2,64,128]{3,2,1,0:T(8,128)(2,1)S(1)} %get-tuple-element.120), channel_id=1, source_target_pairs={{0,34},{32,2},{1,35},{33,3},{2,32},{34,0},{3,33},{35,1},{4,38},{36... | collective-permute-start | bytes 196616 | tf_op jit(solution)/shard_map/ppermute | solution.py:309
  128.4 9.1 %collective-permute-start.30 = (bf16[3,2,64,128]{3,2,1,0:T(8,128)(2,1)S(1)}, bf16[3,2,64,128]{3,2,1,0:T(8,128)(2,1)S(1)}, u32[]{:S(2)}, u32[]{:S(2)}) collective-permute-start(bf16[3,2,64,128]{3,2,1,0:T(8,128)(2,1)S(1)} %get-tuple-element.125), channel_id=1, source_target_pairs={{0,34},{32,2},{1,35},{33,3},{2,32},{34,0},{3,33},{35,1},{4,38},{36... | collective-permute-start | bytes 294920 | tf_op jit(solution)/shard_map/ppermute | solution.py:309
  131.2 8.6 %collective-permute-start.29 = (bf16[3,2,64,128]{3,2,1,0:T(8,128)(2,1)S(1)}, bf16[3,2,64,128]{3,2,1,0:T(8,128)(2,1)S(1)}, u32[]{:S(2)}, u32[]{:S(2)}) collective-permute-start(bf16[3,2,64,128]{3,2,1,0:T(8,128)(2,1)S(1)} %get-tuple-element.124), channel_id=1, source_target_pairs={{0,3},{32,33},{1,0},{33,34},{2,1},{34,35},{3,2},{35,32},{4,7},{36,... | collective-permute-start | bytes 294920 | tf_op jit(solution)/shard_map/ppermute | solution.py:309
  132.1 7.6 %collective-permute-start.28 = (bf16[3,2,64,128]{3,2,1,0:T(8,128)(2,1)S(1)}, bf16[3,2,64,128]{3,2,1,0:T(8,128)(2,1)S(1)}, u32[]{:S(2)}, u32[]{:S(2)}) collective-permute-start(bf16[3,2,64,128]{3,2,1,0:T(8,128)(2,1)S(1)} %get-tuple-element.123), channel_id=1, source_target_pairs={{0,35},{32,1},{1,32},{33,2},{2,33},{34,3},{3,34},{35,0},{4,39},{36... | collective-permute-start | bytes 294920 | tf_op jit(solution)/shard_map/ppermute | solution.py:309
  (2 other events, 1.9 us)
